TPU v7x, 128 devices: a whole 4x4x4 slice. The times are simulated.
128 devices in a mesh: roll: 8 (over y, core), seq: 16 (over z, x).
Axes of the slice: x: 4, y: 4, z: 4, core: 2. Of those that a mesh axis runs over, the one named last changes fastest.
Arguments:
- queries: bfloat16 [8, 4, 128, 192], P('roll', None, 'seq'), may hold values from -17 to 17
- latent_cache: bfloat16 [8, 131072, 576], P('roll', 'seq'), may hold values from -6 to 6
- lengths: int32 [8], P('roll'), may hold values from 8192 to 131072, as said below
- key_weight: bfloat16 [128, 128, 512], P('seq', None, 'roll'), may hold values from -0.5 to 0.5
- value_weight: bfloat16 [128, 512, 128], P('seq', 'roll'), may hold values from -1.5 to 1.5
Outputs:
- attended: bfloat16 [8, 4, 128, 128], P('roll', None, 'seq')
Inputs may be any that keep to these rules, and one draw needn't show every extreme that they name: `lengths`: at least 8192; some rollout has all 131072 positions live.
All inputs are finite; a program needn't handle non-finite values.
Results may differ from a plain program's by a relative error of at most 0.0068.
Values may be sent and summed in bfloat16 or wider, within the bound.
No kernel may reach another device: no remote copies, remote signals or barrier semaphores. Data moves between devices by JAX's collectives and lax.ppermute only.
A program may use at most 128 MiB of HBM per device.

v0:
```python
import jax
import jax.numpy as jnp
from jax import lax
from jax.sharding import PartitionSpec as P

NOPE = 128
ROPE = 64
LATENT = 512


masked_value = -1e30


def merged_2(value, axis, combine):
    everything = jax.tree.map(lambda part: lax.all_gather(part, axis), value)
    first = jax.tree.map(lambda part: part[0], everything)

    def hop(k, so_far):
        return combine(so_far, jax.tree.map(lambda part: part[k], everything))

    return lax.fori_loop(1, lax.axis_size(axis), hop, first)


def combine_partials(earlier, later):
    out_one, top_one, total_one = earlier
    out_two, top_two, total_two = later
    summit = jnp.maximum(top_one, top_two)
    factor_one = jnp.exp(top_one - summit)
    factor_two = jnp.exp(top_two - summit)
    merged = out_one * factor_one[..., None] + out_two * factor_two[..., None]
    return (merged, summit, total_one * factor_one + total_two * factor_two)


def on_device(queries, latent_cache, lengths, key_weight, value_weight):
    rollouts_here, frames, local_heads, query_width = queries.shape
    softmax_scale = (NOPE + ROPE) ** (-0.5)
    query_nope = queries[..., :NOPE]
    absorbed = jnp.einsum(
        "bthn,hnl->bthl",
        query_nope,
        lax.all_gather(key_weight, "roll", axis=2, tiled=True),
        preferred_element_type=jnp.float32,
    ).astype(jnp.bfloat16)
    local_query = jnp.concatenate([absorbed, queries[..., NOPE:]], axis=-1)
    full_query = lax.all_gather(local_query, "seq", axis=2, tiled=True)
    all_heads = full_query.shape[2]
    span_here = latent_cache.shape[1]
    first_position = lax.axis_index("seq") * span_here
    block_size = min(2048, span_here)
    block_count = span_here // block_size
    row_count = frames * all_heads
    outs_list, tops_list, totals_list = ([], [], [])
    query_rows = full_query[0].reshape(row_count, LATENT + ROPE)
    cache_rows = latent_cache[0]
    live_length = lengths[0]

    def advance(
        block_index, running, query_rows=query_rows, cache_rows=cache_rows, live_length=live_length
    ):
        run_top, run_total, run_out = running
        key_block = lax.dynamic_slice_in_dim(cache_rows, block_index * block_size, block_size, 0)
        scores = (
            lax.dot_general(
                query_rows, key_block, (((1,), (1,)), ((), ())), preferred_element_type=jnp.float32
            )
            * softmax_scale
        )
        positions = first_position + block_index * block_size + lax.iota(jnp.int32, block_size)
        live_mask = positions[None, :] < live_length
        masked = jnp.where(live_mask, scores, masked_value)
        block_top = jnp.max(masked, axis=1)
        weights = jnp.where(live_mask, jnp.exp(masked - block_top[:, None]), 0.0)
        block_out = jnp.dot(
            weights.astype(jnp.bfloat16), key_block[:, :LATENT], preferred_element_type=jnp.float32
        )
        fresh_top = jnp.maximum(run_top, block_top)
        factor_old = jnp.exp(run_top - fresh_top)
        factor_new = jnp.exp(block_top - fresh_top)
        new_total = run_total * factor_old + jnp.sum(weights, axis=1) * factor_new
        new_out = run_out * factor_old[:, None] + block_out * factor_new[:, None]
        return (fresh_top, new_total, new_out)

    starting = (
        jnp.full((row_count,), masked_value, jnp.float32),
        jnp.zeros((row_count,), jnp.float32),
        jnp.zeros((row_count, LATENT), jnp.float32),
    )
    finished = lax.fori_loop(0, block_count, advance, starting)
    tops_list.append(finished[0].reshape(frames, all_heads))
    totals_list.append(finished[1].reshape(frames, all_heads))
    outs_list.append(finished[2].reshape(frames, all_heads, LATENT))
    part_top = jnp.stack(tops_list)
    part_total = jnp.stack(totals_list)
    part_out = jnp.stack(outs_list)
    merged_out, merged_top, merged_total = merged_2(
        (part_out, part_top, part_total), "seq", combine_partials
    )
    context_all = (merged_out / merged_total[..., None]).astype(jnp.bfloat16)
    context = lax.dynamic_slice_in_dim(
        context_all, lax.axis_index("seq") * local_heads, local_heads, 2
    )
    result = jnp.einsum(
        "bthl,hlv->bthv",
        context,
        lax.all_gather(value_weight, "roll", axis=1, tiled=True),
        preferred_element_type=jnp.float32,
    )
    return result.astype(jnp.bfloat16)


def solution(mesh):
    placed = (
        P("roll", None, "seq", None),
        P("roll", "seq", None),
        P("roll"),
        P("seq", None, "roll"),
        P("seq", "roll", None),
    )
    return jax.shard_map(
        on_device,
        mesh=mesh,
        in_specs=placed,
        out_specs=P("roll", None, "seq", None),
        check_vma=False,
    )
```

profile of v0, /device:TPU:0, one launch (start us, length us, event | category | flops | bytes accessed | tf_op | source)
XLA Modules:
  0.0 255.7 jit_solution(3978096654424512268)
XLA Ops:
  6.5 0.0 all-gather.4.cloned.1.call-start
  6.5 0.7 all-gather.4.cloned.1.call-update
  7.3 0.0 all-gather.6.cloned.1.call-start
  7.3 0.0 slice-start.1
  7.3 0.0 slice-start
  7.4 14.1 %copy.18 = bf16[1,8192,576]{2,1,0:T(8,128)(2,1)} copy(bf16[1,8192,576]{1,2,0:T(8,128)(2,1)} %param.10) | data formatting | bytes 18874368 | tf_op args[1]
  21.5 0.0 slice-done.1
  21.5 13.4 %all-gather.4.cloned.1.call-done = bf16[8,128,512]{1,2,0:T(8,128)(2,1)} async-done(((bf16[8,128,64]{1,2,0:T(8,128)(2,1)}), bf16[8,128,512]{1,2,0:T(8,128)(2,1)}) %all-gather.4.cloned.1.call-update) | async-done | bytes 1048592 | tf_op jit(solution)/shard_map/all_gather | solution.py:41
  34.9 0.0 slice-done
  34.9 1.6 fusion.34
  36.6 24.6 %all_gather.19 = bf16[1,4,128,576]{3,1,0,2:T(4,128)(2,1)S(1)} all-gather(bf16[1,4,8,576]{3,1,0,2:T(4,128)(2,1)S(1)} %maximum_bitcast_fusion), channel_id=1, replica_groups=mesh['roll'=8,'seq'=16] {'seq'}, dimensions={2}, use_global_device_ids=true | all-gather | bytes 626688 | tf_op jit(solution)/shard_map/all_gather | solution.py:45
  61.2 0.1 copy.26
  61.3 49.7 %while.38 = (s32[]{:T(128)}, f32[512]{0:T(512)S(1)}, f32[512]{0:T(512)S(1)}, f32[512,512]{1,0:T(8,128)S(1)}, s32[]{:T(128)}, /*index=5*/s32[]{:T(128)}, bf16[819...) while((s32[]{:T(128)}, f32[512]{0:T(512)S(1)}, ...), condition=%wide.region_3.4_spmd.clone, body=%wide.region_0.3_spmd.clone.sunk | while | flops 2296388608 | bytes 36802788 | solution.py:88
  61.3 0.7 add_compare_fusion.2
  61.9 3.4 %fusion.58 = (f32[512]{0:T(512)S(1)}, f32[2048,512]{1,0:T(8,128)S(1)}) fusion(pred[2048]{0:T(1024)(128)(4,1)S(1)} %add_compare_fusion.2, bf16[512,576]{1,0:T(8,128)(2,1)S(1)} %get-tuple-element.554, bf16[8192,576]{1,0:T(8,128)(2,1)} %get-tuple-element.553, s32[]{:T(128)S(6)} %select_n.80), kind=kOutput, calls=%fused_computation.12.clone.1 | convolution fusion | flops 1211104768 | bytes 7409668 | tf_op jit(solution)/shard_map/while/body/eval_jaxpr/dot_general | solution.py:63
  65.4 0.0 copy-start
  65.4 2.0 copy-done
  67.4 1.2 fusion.59
  68.6 5.1 %fusion.61 = f32[512,512]{1,0:T(8,128)S(1)} fusion(bf16[8192,576]{1,0:T(8,128)(2,1)} %get-tuple-element.553, s32[]{:T(128)S(6)} %select_n.80, f32[2048,512]{1,0:T(8,128)} %copy-done, f32[512]{0:T(512)S(1)} %get-tuple-element.518, pred[2048]{0:T(1024)(128)(4,1)S(1)} %add_compare_fusion.2, f32[512,512]{1,0:T(8,128)S(1)} %get-tuple-element.538, ...), kind=kOutput, calls=%fused_computation.25.clone.1 | convolution fusion | flops 1080033280 | bytes 8396805 | tf_op jit(solution)/shard_map/while/body/eval_jaxpr/dot_general | solution.py:73
  73.7 0.7 add_compare_fusion.2
  74.4 3.4 %fusion.58 = (f32[512]{0:T(512)S(1)}, f32[2048,512]{1,0:T(8,128)S(1)}) fusion(pred[2048]{0:T(1024)(128)(4,1)S(1)} %add_compare_fusion.2, bf16[512,576]{1,0:T(8,128)(2,1)S(1)} %get-tuple-element.554, bf16[8192,576]{1,0:T(8,128)(2,1)} %get-tuple-element.553, s32[]{:T(128)S(6)} %select_n.80), kind=kOutput, calls=%fused_computation.12.clone.1 | convolution fusion | flops 1211104768 | bytes 7409668 | tf_op jit(solution)/shard_map/while/body/eval_jaxpr/dot_general | solution.py:63
  77.8 2.0 copy-done
  79.8 1.2 fusion.59
  81.0 5.1 %fusion.61 = f32[512,512]{1,0:T(8,128)S(1)} fusion(bf16[8192,576]{1,0:T(8,128)(2,1)} %get-tuple-element.553, s32[]{:T(128)S(6)} %select_n.80, f32[2048,512]{1,0:T(8,128)} %copy-done, f32[512]{0:T(512)S(1)} %get-tuple-element.518, pred[2048]{0:T(1024)(128)(4,1)S(1)} %add_compare_fusion.2, f32[512,512]{1,0:T(8,128)S(1)} %get-tuple-element.538, ...), kind=kOutput, calls=%fused_computation.25.clone.1 | convolution fusion | flops 1080033280 | bytes 8396805 | tf_op jit(solution)/shard_map/while/body/eval_jaxpr/dot_general | solution.py:73
  86.1 0.7 add_compare_fusion.2
  86.8 3.4 %fusion.58 = (f32[512]{0:T(512)S(1)}, f32[2048,512]{1,0:T(8,128)S(1)}) fusion(pred[2048]{0:T(1024)(128)(4,1)S(1)} %add_compare_fusion.2, bf16[512,576]{1,0:T(8,128)(2,1)S(1)} %get-tuple-element.554, bf16[8192,576]{1,0:T(8,128)(2,1)} %get-tuple-element.553, s32[]{:T(128)S(6)} %select_n.80), kind=kOutput, calls=%fused_computation.12.clone.1 | convolution fusion | flops 1211104768 | bytes 7409668 | tf_op jit(solution)/shard_map/while/body/eval_jaxpr/dot_general | solution.py:63
  90.2 2.0 copy-done
  92.3 1.2 fusion.59
  93.5 5.1 %fusion.61 = f32[512,512]{1,0:T(8,128)S(1)} fusion(bf16[8192,576]{1,0:T(8,128)(2,1)} %get-tuple-element.553, s32[]{:T(128)S(6)} %select_n.80, f32[2048,512]{1,0:T(8,128)} %copy-done, f32[512]{0:T(512)S(1)} %get-tuple-element.518, pred[2048]{0:T(1024)(128)(4,1)S(1)} %add_compare_fusion.2, f32[512,512]{1,0:T(8,128)S(1)} %get-tuple-element.538, ...), kind=kOutput, calls=%fused_computation.25.clone.1 | convolution fusion | flops 1080033280 | bytes 8396805 | tf_op jit(solution)/shard_map/while/body/eval_jaxpr/dot_general | solution.py:73
  98.6 0.7 add_compare_fusion.2
  99.2 3.4 %fusion.58 = (f32[512]{0:T(512)S(1)}, f32[2048,512]{1,0:T(8,128)S(1)}) fusion(pred[2048]{0:T(1024)(128)(4,1)S(1)} %add_compare_fusion.2, bf16[512,576]{1,0:T(8,128)(2,1)S(1)} %get-tuple-element.554, bf16[8192,576]{1,0:T(8,128)(2,1)} %get-tuple-element.553, s32[]{:T(128)S(6)} %select_n.80), kind=kOutput, calls=%fused_computation.12.clone.1 | convolution fusion | flops 1211104768 | bytes 7409668 | tf_op jit(solution)/shard_map/while/body/eval_jaxpr/dot_general | solution.py:63
  102.7 2.0 copy-done
  104.7 1.2 fusion.59
  105.9 5.1 %fusion.61 = f32[512,512]{1,0:T(8,128)S(1)} fusion(bf16[8192,576]{1,0:T(8,128)(2,1)} %get-tuple-element.553, s32[]{:T(128)S(6)} %select_n.80, f32[2048,512]{1,0:T(8,128)} %copy-done, f32[512]{0:T(512)S(1)} %get-tuple-element.518, pred[2048]{0:T(1024)(128)(4,1)S(1)} %add_compare_fusion.2, f32[512,512]{1,0:T(8,128)S(1)} %get-tuple-element.538, ...), kind=kOutput, calls=%fused_computation.25.clone.1 | convolution fusion | flops 1080033280 | bytes 8396805 | tf_op jit(solution)/shard_map/while/body/eval_jaxpr/dot_general | solution.py:73
  111.0 0.0 copy-start.1
  111.0 1.0 copy-done.1
  112.0 0.0 all-gather.6.cloned.1.call-update
  112.0 0.0 all-gather.8.cloned.1.call-start
  112.1 0.7 all-gather.8.cloned.1.call-update
  112.7 22.4 %all_gather.22 = f32[16,1,4,128]{3,2,1,0:T(4,128)S(1)} all-gather(f32[1,1,4,128]{3,2,1,0:T(4,128)S(1)} %bitcast.69), channel_id=1, replica_groups=mesh['roll'=8,'seq'=16] {'seq'}, dimensions={0}, use_global_device_ids=true | all-gather | bytes 34816 | tf_op jit(solution)/shard_map/all_gather | solution.py:15
  135.1 21.4 %all_gather.21 = f32[16,1,4,128]{3,2,1,0:T(4,128)S(1)} all-gather(f32[1,1,4,128]{3,2,1,0:T(4,128)S(1)} %bitcast.68), channel_id=1, replica_groups=mesh['roll'=8,'seq'=16] {'seq'}, dimensions={0}, use_global_device_ids=true | all-gather | bytes 34816 | tf_op jit(solution)/shard_map/all_gather | solution.py:15
  156.5 64.9 %all-gather.6.cloned.1.call-done = f32[16,1,4,128,512]{4,3,2,1,0:T(8,128)} async-done(((f32[1,1,4,128,512]{4,3,2,1,0:T(8,128)}), f32[16,1,4,128,512]{4,3,2,1,0:T(8,128)}) %all-gather.6.cloned.1.call-update) | async-done | bytes 16777232 | tf_op jit(solution)/shard_map/all_gather | solution.py:15
  221.4 1.3 slice_bitcast_fusion
  222.7 24.2 %while.37 = (s32[]{:T(128)}, f32[1,4,128,512]{3,2,1,0:T(8,128)S(1)}, f32[1,4,128]{2,1,0:T(4,128)S(1)}, f32[1,4,128]{2,1,0:T(4,128)S(1)}, f32[16,1,4,128]{3,2,1,0...) while((s32[]{:T(128)}, ...), condition=%wide.region_5.6_spmd, body=%wide.region_4.5_spmd.sunk | while | flops 790533 | bytes 3176603 | solution.py:21
  222.8 1.5 fusion.54
  224.4 1.5 fusion.54
  226.0 1.5 fusion.54
  227.6 1.5 fusion.54
  229.2 1.5 fusion.54
  230.8 1.5 fusion.54
  232.5 1.5 fusion.54
  234.1 1.5 fusion.54
  235.7 1.5 fusion.54
  237.3 1.5 fusion.54
  238.9 1.5 fusion.54
  240.5 1.6 fusion.54
  242.2 1.5 fusion.54
  243.8 1.5 fusion.54
  245.4 1.5 fusion.54
  246.9 0.1 constant_dynamic-slice_fusion
  247.0 0.1 fusion.36
  247.1 0.0 all-gather.8.cloned.1.call-done
  247.1 1.5 fusion.35
  248.6 0.6 copy.25
  (59 shorter events, 0.7 us)
Async XLA Ops:
  6.5 28.4 %all-gather.4.cloned.1.call-start = ((), (), s32[]{:S(2)}) async-start(), calls=%async_computation | async-start | bytes 1179648 | tf_op jit(solution)/shard_map/all_gather | solution.py:41
  7.3 214.2 %all-gather.6.cloned.1.call-start = ((), (), s32[]{:S(2)}) async-start(), calls=%async_computation.1 | async-start | bytes 17825792 | tf_op jit(solution)/shard_map/all_gather | solution.py:15
  7.3 14.1 %slice-start.1 = ((bf16[1,4,8,192]{3,2,1,0:T(8,128)(2,1)}), bf16[1,4,8,64]{3,2,1,0:T(8,128)(2,1)S(1)}, s32[]{:S(2)}) async-start(bf16[1,4,8,192]{3,2,1,0:T(8,128)(2,1)} %param.9), calls=%async_computation.4 | async-start | bytes 16384 | tf_op jit(solution)/shard_map/slice | solution.py:44
  7.3 27.6 %slice-start = ((bf16[1,4,8,192]{3,2,1,0:T(8,128)(2,1)}), bf16[1,4,8,128]{3,2,1,0:T(8,128)(2,1)S(1)}, s32[]{:S(2)}) async-start(bf16[1,4,8,192]{3,2,1,0:T(8,128)(2,1)} %param.9), calls=%async_computation.3 | async-start | bytes 16384 | tf_op jit(solution)/shard_map/slice | solution.py:37
  65.4 2.1 copy-start
  77.8 2.1 copy-start
  90.2 2.1 copy-start
  102.7 2.1 copy-start
  111.0 1.0 copy-start.1
  112.0 135.1 %all-gather.8.cloned.1.call-start = ((), (), s32[]{:S(2)}) async-start(), calls=%async_computation.2 | async-start | bytes 1179648 | tf_op jit(solution)/shard_map/all_gather | solution.py:105
Sparse Core Ops, SparseCore 0:
  9.0 25.8 all-gather.3
  112.1 109.2 all-gather.5
  223.1 22.9 all-gather.7
where the time goes:
time: 258 us; the launch traced here: 256 us
  waiting for transfers between devices  79.8 us (31%)
  blocking collectives  68.4 us (27%)
  matrix products  37 us (14%)
  other arithmetic  31 us (12%)
  local copies, waits for them, and re-layouts  25.4 us (10%)
  between operations  13.2 us (5%)
    all_gather x1, waiting for transfers between devices, merged_2(): everything = jax.tree.map(lambda part: lax.all_gather(part, axis), value)  64.9 us
    all_gather x2, blocking collectives, merged_2(): everything = jax.tree.map(lambda part: lax.all_gather(part, axis), value)  43.8 us
    all_gather x1, blocking collectives, on_device(): full_query = lax.all_gather(local_query, 'seq', axis=2, tiled=True)  24.6 us
    add x15, other arithmetic, combine_partials(): merged = out_one * factor_one[..., None] + out_two * factor_two[..., None]  23 us
    dot_general x4, matrix products, advance(): jnp.dot(weights.astype(jnp.bfloat16), key_block[:, :LATENT], preferred_el...  20.3 us
    unnamed x5, local copies, waits for them, and re-layouts  15.2 us
    dot_general x4, matrix products, advance(): lax.dot_general(query_rows, key_block, (((1,), (1,)), ((), ())), preferre...  13.7 us
    all_gather x1, waiting for transfers between devices, on_device(): lax.all_gather(key_weight, 'roll', axis=2, tiled=True)  13.4 us
  transfers between devices with their start and end apart: 3, of which 2 were waited for; matrix products, arithmetic and copies ran while one was open for 15% of the time, Pallas kernels for 0%

commit v1 on v0

v1 whole, which is shorter than its diff:
```python
import functools

import jax
import jax.numpy as jnp
from jax import lax
from jax.experimental import pallas as pl
from jax.experimental.pallas import tpu as pltpu
from jax.sharding import PartitionSpec as P

NOPE = 128
ROPE = 64
LATENT = 512
WIDTH = LATENT + ROPE
PAYLOAD = LATENT + 128
RING = 4
CORES = 2

MASKED = -1e30
TO_LOG2 = (NOPE + ROPE) ** (-0.5) * 1.4426950408889634

VMEM = pl.BlockSpec(memory_space=pltpu.VMEM)
SMEM = pl.BlockSpec(memory_space=pltpu.SMEM)
ANY = pl.BlockSpec(memory_space=pl.ANY)
BF16 = jnp.bfloat16
F32 = jnp.float32


def y_shift(value, hops):
    pairs = [(CORES * y + c, CORES * ((y + hops) % RING) + c) for y in range(RING) for c in range(CORES)]
    return lax.ppermute(value, "roll", pairs)


def core_swap(value):
    pairs = [(CORES * y + c, CORES * y + 1 - c) for y in range(RING) for c in range(CORES)]
    return lax.ppermute(value, "roll", pairs)


def z_shift(value, hops):
    pairs = [(RING * z + x, RING * ((z + hops) % RING) + x) for z in range(RING) for x in range(RING)]
    return lax.ppermute(value, "seq", pairs)


def x_shift(value, hops):
    pairs = [(RING * z + x, RING * z + (x + hops) % RING) for z in range(RING) for x in range(RING)]
    return lax.ppermute(value, "seq", pairs)


def two_terms(value):
    high = value.astype(BF16).astype(F32)
    return high, (value - high).astype(BF16).astype(F32)


def pack_stats(top, total, rows):
    lane = lax.broadcasted_iota(jnp.int32, (rows, 128), 1)
    packed = jnp.zeros((rows, 128), F32)
    for at, term in enumerate(two_terms(top) + two_terms(total)):
        packed = jnp.where(lane == at, term, packed)
    return packed.astype(BF16)


def merge(parts):
    tops, totals = [], []
    for part in parts:
        stats = part[:, LATENT:].astype(F32)
        tops.append(stats[:, 0:1] + stats[:, 1:2])
        totals.append(stats[:, 2:3] + stats[:, 3:4])
    top = functools.reduce(jnp.maximum, tops)
    weights = [jnp.exp2(t - top) * n for t, n in zip(tops, totals)]
    total = functools.reduce(jnp.add, weights)
    inverse = jnp.where(total > 0, 1.0 / total, 0.0)
    out = functools.reduce(
        jnp.add, [part[:, :LATENT].astype(F32) * (w * inverse) for part, w in zip(parts, weights)]
    )
    return out, top, total


def absorb_kernel(place, mine, other, kw0, kw1, kw2, kw3, out_mine, out_other, weights):
    y, core = place[0], place[1]
    heads = mine.shape[1]
    weights[...] = jnp.zeros_like(weights)
    for hops, block in enumerate((kw0, kw1, kw2, kw3)):
        chunk = lax.rem(y + RING - hops, RING) * CORES + core
        weights[:, pl.ds(pl.multiple_of(chunk * 64, 64), 64), :] = block[...]
    for h in range(heads):
        rows = jnp.concatenate([mine[:, h, :], other[:, h, :]], axis=0)
        absorbed = lax.dot_general(
            rows[:, :NOPE], weights[h], (((1,), (1,)), ((), ())), preferred_element_type=F32
        ).astype(BF16)
        out_mine[h] = jnp.concatenate([absorbed[:4], rows[:4, NOPE:]], axis=1)
        out_other[h] = jnp.concatenate([absorbed[4:], jnp.zeros((4, ROPE), BF16)], axis=1)


def absorb(place, mine, other, blocks):
    frames, heads, _ = mine.shape
    shape = jax.ShapeDtypeStruct((heads, frames, WIDTH), BF16)
    return pl.pallas_call(
        absorb_kernel,
        out_shape=[shape, shape],
        in_specs=[SMEM] + [VMEM] * 6,
        out_specs=[VMEM, VMEM],
        scratch_shapes=[pltpu.VMEM((heads, LATENT, NOPE), BF16)],
    )(place, mine, other, *blocks)


def stack_kernel(a, b, c, d, out):
    rows = a.shape[0]
    for at, block in enumerate((a, b, c, d)):
        out[at * rows : (at + 1) * rows, :] = block[...]


def stack(blocks):
    rows, width = blocks[0].shape
    return pl.pallas_call(
        stack_kernel,
        out_shape=jax.ShapeDtypeStruct((4 * rows, width), BF16),
        in_specs=[VMEM] * 4,
        out_specs=VMEM,
    )(*blocks)


def fold(op, value):
    so_far = value[:, :128]
    for at in range(128, value.shape[1], 128):
        so_far = op(so_far, value[:, at : at + 128])
    return so_far


def attend_kernel(live_ref, qa, qb, qc, qd, cache, oa, ob, oc, od, query, held, scores, tops, totals, acc, sems, *, block):
    blocks = cache.shape[1] // block
    rows = query.shape[0]
    live = live_ref[0]

    def arrival(i):
        at = pl.ds(pl.multiple_of(i * block, block), block)
        return pltpu.make_async_copy(cache.at[:, at], held.at[:, at], sems.at[i])

    for i in range(blocks):
        arrival(i).start()
    group = qa.shape[0]
    for at, part in enumerate((qa, qb, qc, qd)):
        query[at * group : (at + 1) * group, :] = part[...]
    tops[...] = jnp.full(tops.shape, MASKED, F32)
    totals[...] = jnp.zeros(totals.shape, F32)
    acc[...] = jnp.zeros(acc.shape, F32)

    def score(i, masked):
        start = pl.multiple_of(i * block, block)
        at = pl.ds(start, block)
        arrival(i).wait()
        s = jnp.dot(query[...], held[:, at], preferred_element_type=F32)
        if masked:
            s = jnp.where(start + lax.broadcasted_iota(jnp.int32, s.shape, 1) < live, s, MASKED)
        scores[:, at] = s
        tops[...] = jnp.maximum(tops[...], fold(jnp.maximum, s))

    def top_of():
        high, low = two_terms(jnp.max(tops[...], axis=1, keepdims=True) * TO_LOG2)
        return high + low

    def weigh(i, top):
        at = pl.ds(pl.multiple_of(i * block, block), block)
        p = jnp.exp2(scores[:, at] * TO_LOG2 - top)
        totals[...] += fold(jnp.add, p)
        acc[...] += lax.dot_general(
            p.astype(BF16), held[:LATENT, at], (((1,), (1,)), ((), ())), preferred_element_type=F32
        )

    def loop(first, last, body):
        lax.fori_loop(first, last, lambda i, c: (body(i), c)[1], 0)

    full = live >= blocks * block

    @pl.when(full)
    def _():
        loop(0, blocks, lambda i: score(i, False))
        top = top_of()
        loop(0, blocks, lambda i: weigh(i, top))

    @pl.when(jnp.logical_not(full))
    def _():
        some = (live + block - 1) // block
        loop(0, some, lambda i: score(i, True))
        loop(some, blocks, lambda i: arrival(i).wait())
        top = top_of()
        loop(0, some, lambda i: weigh(i, top))

    total = jnp.sum(totals[...], axis=1, keepdims=True)
    normal = (acc[...] * jnp.where(total > 0, 1.0 / total, 0.0)).astype(BF16)
    stats = pack_stats(top_of(), total, rows)
    for at, out in enumerate((oa, ob, oc, od)):
        out[:, :LATENT] = normal[at * group : (at + 1) * group]
        out[:, LATENT:] = stats[at * group : (at + 1) * group]


def attend(live, parts, cache, block=2048):
    group = parts[0].shape[0]
    rows, span = group * len(parts), cache.shape[1]
    return pl.pallas_call(
        functools.partial(attend_kernel, block=block),
        out_shape=[jax.ShapeDtypeStruct((group, PAYLOAD), BF16)] * 4,
        in_specs=[SMEM] + [VMEM] * 4 + [ANY],
        out_specs=[VMEM] * 4,
        scratch_shapes=[
            pltpu.VMEM((rows, WIDTH), BF16),
            pltpu.VMEM((WIDTH, span), BF16),
            pltpu.VMEM((rows, span), F32),
            pltpu.VMEM((rows, 128), F32),
            pltpu.VMEM((rows, 128), F32),
            pltpu.VMEM((rows, LATENT), F32),
            pltpu.SemaphoreType.DMA((span // block,)),
        ],
        compiler_params=pltpu.CompilerParams(vmem_limit_bytes=56 * 2**20),
        cost_estimate=pl.CostEstimate(
            flops=2 * rows * span * (WIDTH + LATENT), bytes_accessed=span * WIDTH * 2, transcendentals=rows * span
        ),
    )(live, *parts, cache)


def merge_kernel(a, b, c, d, oa, ob, oc, od):
    out, top, total = merge([a[...], b[...], c[...], d[...]])
    stats = pack_stats(top, total, out.shape[0])
    rows = oa.shape[0]
    for at, part in enumerate((oa, ob, oc, od)):
        here = slice(at * rows, (at + 1) * rows)
        part[:, :LATENT] = out[here].astype(BF16)
        part[:, LATENT:] = stats[here]


def merge_groups(parts):
    rows, width = parts[0].shape
    return pl.pallas_call(
        merge_kernel,
        out_shape=[jax.ShapeDtypeStruct((rows // 4, width), BF16)] * 4,
        in_specs=[VMEM] * 4,
        out_specs=[VMEM] * 4,
    )(*parts)


def finish_kernel(a, b, c, d, weight, out, context):
    context[...] = merge([a[...], b[...], c[...], d[...]])[0].astype(BF16)
    frames, heads, _ = out.shape
    for h in range(heads):
        out[:, h, :] = jnp.dot(
            context[h * frames : (h + 1) * frames, :], weight[h], preferred_element_type=F32
        ).astype(BF16)


def finish(parts, weight, frames):
    heads, _, vhead = weight.shape
    return pl.pallas_call(
        finish_kernel,
        out_shape=jax.ShapeDtypeStruct((frames, heads, vhead), BF16),
        in_specs=[VMEM] * 5,
        out_specs=VMEM,
        scratch_shapes=[pltpu.VMEM(parts[0].shape[:1] + (LATENT,), BF16)],
    )(*parts, weight)


def on_device(queries, latent_cache, lengths, key_weight, value_weight):
    frames, heads, _ = queries.shape[1:]
    roll, seq = lax.axis_index("roll"), lax.axis_index("seq")
    place = jnp.stack([roll // CORES, roll % CORES]).astype(jnp.int32)
    span = latent_cache.shape[1]
    live = jnp.clip(lengths - seq * span, 0, span).astype(jnp.int32)
    cache = latent_cache[0].T
    value_all = lax.all_gather(value_weight, "roll", axis=1, tiled=True)

    mine = queries[0]
    block = jnp.swapaxes(key_weight, 1, 2)
    blocks = [block] + [y_shift(block, hops) for hops in (1, 2, 3)]
    other = core_swap(mine)
    own, others = absorb(place, mine, other, blocks)
    local = (own + core_swap(others)).reshape(heads * frames, WIDTH)

    near = stack([local] + [z_shift(local, hops) for hops in (1, 2, 3)])
    groups = [near] + [x_shift(near, hops) for hops in (1, 2, 3)]

    parts = attend(live, groups, cache)

    near = merge_groups([parts[0]] + [x_shift(parts[hops], -hops) for hops in (1, 2, 3)])
    last = [near[0]] + [z_shift(near[hops], -hops) for hops in (1, 2, 3)]
    return finish(last, value_all, frames)[None]


def solution(mesh):
    placed = (
        P("roll", None, "seq", None),
        P("roll", "seq", None),
        P("roll"),
        P("seq", None, "roll"),
        P("seq", "roll", None),
    )
    return jax.shard_map(
        on_device,
        mesh=mesh,
        in_specs=placed,
        out_specs=P("roll", None, "seq", None),
        check_vma=False,
    )
```

time: 258 us -> 95.5 us (0.37); the launches traced: 256 us -> 96 us
  blocking collectives: 68.4 us -> 0 us
  waiting for transfers between devices: 79.8 us -> 28.2 us
  matrix products: 37 us -> 0 us
  other arithmetic: 31 us -> 1.45 us
  Pallas kernels: 0 us -> 25 us
  starting transfers between devices: 0.08 us -> 23.3 us
  local copies, waits for them, and re-layouts: 25.4 us -> 3.92 us
    all_gather x3 -> x1, waiting for transfers between devices: 78.4 us -> 0.01 us  [on_device(): value_all = lax.all_gather(value_weight, 'roll', axis=1, tiled=True)]
    all_gather x3 -> x0, blocking collectives: 68.4 us -> none  [the longest x2 43.8 us: merged_2(): everything = jax.tree.map(lambda part: lax.all_gather(part, axis), value)]
    dot_general x10 -> x0, matrix products: 37 us -> none  [the longest x4 20.3 us: advance(): jnp.dot(weights.astype(jnp.bfloat16), key_block[:, :LATENT], preferred_el...]
    ppermute x0 -> x17, waiting for transfers between devices: none -> 27.5 us  [the longest x6 14 us: x_shift(): return lax.ppermute(value, 'seq', pairs)]
    pallas_call x0 -> x5, Pallas kernels: none -> 25 us  [the longest x1 16.4 us: attend(): pl.pallas_call(functools.partial(attend_kernel, block=block), out_shape=[...]
    ppermute x0 -> x17, starting transfers between devices: none -> 23.2 us  [the longest x6 10.1 us: z_shift(): return lax.ppermute(value, 'seq', pairs)]
    add x34 -> x1, other arithmetic: 23.4 us -> 0.8 us  [on_device(): local = (own + core_swap(others)).reshape(heads * frames, WIDTH)]
    unnamed x5 -> x34, local copies, waits for them, and re-layouts: 15.2 us -> 3.89 us
  transfers between devices with their start and end apart: 3 -> 18, of which waited for: 2 -> 13; matrix products, arithmetic and copies ran while one was open for 15% -> 2% of each run, Pallas kernels for 0% -> 23%
where the time goes in v1:
time: 95.5 us; the launch traced here: 96 us
  waiting for transfers between devices  28.2 us (30%)
  Pallas kernels  25 us (26%)
  starting transfers between devices  23.3 us (24%)
  between operations  14.1 us (15%)
  local copies, waits for them, and re-layouts  3.92 us (4%)
  other arithmetic  1.45 us (2%)
    pallas_call x1, Pallas kernels, attend(): pl.pallas_call(functools.partial(attend_kernel, block=block), out_shape=[...  16.4 us
    ppermute x6, waiting for transfers between devices, x_shift(): return lax.ppermute(value, 'seq', pairs)  14 us
    ppermute x6, starting transfers between devices, z_shift(): return lax.ppermute(value, 'seq', pairs)  10.1 us
    ppermute x6, waiting for transfers between devices, z_shift(): return lax.ppermute(value, 'seq', pairs)  7.82 us
    ppermute x6, starting transfers between devices, x_shift(): return lax.ppermute(value, 'seq', pairs)  7.14 us
    ppermute x3, starting transfers between devices, y_shift(): return lax.ppermute(value, 'roll', pairs)  5.98 us
    unnamed x34, local copies, waits for them, and re-layouts  3.89 us
    ppermute x3, waiting for transfers between devices, y_shift(): return lax.ppermute(value, 'roll', pairs)  3.48 us
  transfers between devices with their start and end apart: 18, of which 13 were waited for; matrix products, arithmetic and copies ran while one was open for 2% of the time, Pallas kernels for 23%

profile of v1, /device:TPU:0, one launch (start us, length us, event | category | flops | bytes accessed | tf_op | source)
XLA Modules:
  0.0 96.0 jit_solution(5703800354562256078)
XLA Ops:
  6.5 0.0 all-gather.2.cloned.1.call-start
  6.5 0.7 all-gather.2.cloned.1.call-update
  7.3 1.7 %collective-permute-start.1 = (bf16[8,64,128]{2,1,0:T(8,128)(2,1)}, bf16[8,64,128]{2,1,0:T(8,128)(2,1)S(1)}, u32[]{:S(2)}, u32[]{:S(2)}) collective-permute-start(bf16[8,64,128]{2,1,0:T(8,128)(2,1)} %bitcast.9), channel_id=1, source_target_pairs={{0,32},{16,48},{32,64},{48,80},{64,96},{80,112},{96,0},{112,16},{1... | collective-permute-start | bytes 393224 | tf_op jit(solution)/shard_map/ppermute | solution.py:30
  9.0 2.9 %collective-permute-start.2 = (bf16[8,64,128]{2,1,0:T(8,128)(2,1)}, bf16[8,64,128]{2,1,0:T(8,128)(2,1)S(1)}, u32[]{:S(2)}, u32[]{:S(2)}) collective-permute-start(bf16[8,64,128]{2,1,0:T(8,128)(2,1)} %bitcast.10), channel_id=1, source_target_pairs={{0,64},{16,80},{32,96},{48,112},{64,0},{80,16},{96,32},{112,48},{1... | collective-permute-start | bytes 393224 | tf_op jit(solution)/shard_map/ppermute | solution.py:30
  11.9 1.3 %collective-permute-start.3 = (bf16[8,64,128]{2,1,0:T(8,128)(2,1)}, bf16[8,64,128]{2,1,0:T(8,128)(2,1)S(1)}, u32[]{:S(2)}, u32[]{:S(2)}) collective-permute-start(bf16[8,64,128]{2,1,0:T(8,128)(2,1)} %bitcast.11), channel_id=1, source_target_pairs={{0,96},{16,112},{32,0},{48,16},{64,32},{80,48},{96,64},{112,80},{1... | collective-permute-start | bytes 393224 | tf_op jit(solution)/shard_map/ppermute | solution.py:30
  13.2 0.0 collective-permute-start
  13.2 0.7 pad_add_fusion.place
  13.9 0.7 collective-permute-done.other
  14.6 0.0 copy-start.13
  14.6 0.0 collective-permute-done.1.kw1
  14.6 0.0 copy-start.4
  14.6 3.5 %collective-permute-done.2.kw2 = bf16[8,64,128]{2,1,0:T(8,128)(2,1)S(1)} collective-permute-done((bf16[8,64,128]{2,1,0:T(8,128)(2,1)}, bf16[8,64,128]{2,1,0:T(8,128)(2,1)S(1)}, u32[]{:S(2)}, u32[]{:S(2)}) %collective-permute-start.2) | collective-permute-done | bytes 131104 | tf_op jit(solution)/shard_map/ppermute | solution.py:30
  18.1 0.0 collective-permute-done.3.kw3
  18.1 0.0 copy-done.13
  18.1 0.0 copy-done.4
  18.1 0.6 copy-done.5
  18.8 0.7 copy-done.6
  19.4 2.4 %shard_map.55 = (bf16[8,4,576]{2,1,0:T(4,128)(2,1)}, bf16[8,4,576]{2,1,0:T(4,128)(2,1)}) custom-call(s32[2]{0:T(128)} %pad_add_fusion.place, bf16[4,8,192]{2,1,0:T(8,128)(2,1)} %bitcast.14, bf16[4,8,192]{2,1,0:T(8,128)(2,1)} %copy-done.13, bf16[8,64,128]{2,1,0:T(8,128)(2,1)} %bitcast.12, bf16[8,64,128]{2,1,0:T(8,128)(2,1)} %copy-done.4, ...), custom_call_target="tpu_custom_call" | custom-call | tf_op jit(solution)/shard_map/pallas_call | solution.py:96
  21.8 0.0 collective-permute-start.4
  21.8 1.4 %collective-permute-done.4 = bf16[8,4,576]{2,1,0:T(4,128)(2,1)S(1)} collective-permute-done((bf16[8,4,576]{2,1,0:T(4,128)(2,1)}, bf16[8,4,576]{2,1,0:T(4,128)(2,1)S(1)}, u32[]{:S(2)}, u32[]{:S(2)}) %collective-permute-start.4) | collective-permute-done | bytes 36896 | tf_op jit(solution)/shard_map/ppermute | solution.py:35
  23.2 0.8 add.9
  24.0 0.0 copy-start.3
  24.0 2.0 %collective-permute-start.5 = (bf16[32,576]{1,0:T(8,128)(2,1)S(1)}, bf16[32,576]{1,0:T(8,128)(2,1)S(1)}, u32[]{:S(2)}, u32[]{:S(2)}) collective-permute-start(bf16[32,576]{1,0:T(8,128)(2,1)S(1)} %reshape.3.a), channel_id=1, source_target_pairs={{0,4},{1,5},{2,6},{3,7},{4,8},{5,9},{6,10},{7,11},{8,12},{9,13},{1... | collective-permute-start | bytes 110600 | tf_op jit(solution)/shard_map/ppermute | solution.py:40
  26.0 3.6 %collective-permute-start.6 = (bf16[32,576]{1,0:T(8,128)(2,1)S(1)}, bf16[32,576]{1,0:T(8,128)(2,1)S(1)}, u32[]{:S(2)}, u32[]{:S(2)}) collective-permute-start(bf16[32,576]{1,0:T(8,128)(2,1)S(1)} %reshape.3.a), channel_id=1, source_target_pairs={{0,8},{1,9},{2,10},{3,11},{4,12},{5,13},{6,14},{7,15},{8,0},{9,1},... | collective-permute-start | bytes 110600 | tf_op jit(solution)/shard_map/ppermute | solution.py:40
  29.6 1.0 %collective-permute-start.7 = (bf16[32,576]{1,0:T(8,128)(2,1)S(1)}, bf16[32,576]{1,0:T(8,128)(2,1)S(1)}, u32[]{:S(2)}, u32[]{:S(2)}) collective-permute-start(bf16[32,576]{1,0:T(8,128)(2,1)S(1)} %reshape.3.a), channel_id=1, source_target_pairs={{0,12},{1,13},{2,14},{3,15},{4,0},{5,1},{6,2},{7,3},{8,4},{9,5},{1... | collective-permute-start | bytes 110600 | tf_op jit(solution)/shard_map/ppermute | solution.py:40
  30.6 0.0 collective-permute-done.5.b
  30.6 1.5 %collective-permute-done.6.c = bf16[32,576]{1,0:T(8,128)(2,1)S(1)} collective-permute-done((bf16[32,576]{1,0:T(8,128)(2,1)S(1)}, bf16[32,576]{1,0:T(8,128)(2,1)S(1)}, u32[]{:S(2)}, u32[]{:S(2)}) %collective-permute-start.6) | collective-permute-done | bytes 36896 | tf_op jit(solution)/shard_map/ppermute | solution.py:40
  32.1 1.5 %collective-permute-done.7.d = bf16[32,576]{1,0:T(8,128)(2,1)S(1)} collective-permute-done((bf16[32,576]{1,0:T(8,128)(2,1)S(1)}, bf16[32,576]{1,0:T(8,128)(2,1)S(1)}, u32[]{:S(2)}, u32[]{:S(2)}) %collective-permute-start.7) | collective-permute-done | bytes 36896 | tf_op jit(solution)/shard_map/ppermute | solution.py:40
  33.6 0.0 copy-done.3
  33.6 0.0 copy-done.10
  33.6 0.0 copy-done.11
  33.6 0.0 copy-start.12
  33.6 0.6 copy-done.12
  34.2 1.5 %shard_map.56.qa = bf16[128,576]{1,0:T(8,128)(2,1)} custom-call(bf16[32,576]{1,0:T(8,128)(2,1)} %copy-done.3, bf16[32,576]{1,0:T(8,128)(2,1)} %copy-done.10, bf16[32,576]{1,0:T(8,128)(2,1)} %copy-done.11, bf16[32,576]{1,0:T(8,128)(2,1)} %copy-done.12), custom_call_target="tpu_custom_call" | custom-call | tf_op jit(solution)/shard_map/pallas_call | solution.py:113
  35.8 2.8 %collective-permute-start.10 = (bf16[128,576]{1,0:T(8,128)(2,1)}, bf16[128,576]{1,0:T(8,128)(2,1)S(1)}, u32[]{:S(2)}, u32[]{:S(2)}) collective-permute-start(bf16[128,576]{1,0:T(8,128)(2,1)} %shard_map.56.qa), channel_id=1, source_target_pairs={{0,3},{1,0},{2,1},{3,2},{4,7},{5,4},{6,5},{7,6},{8,11},{9,8},{10,9... | collective-permute-start | bytes 442376 | tf_op jit(solution)/shard_map/ppermute | solution.py:45
  38.5 0.0 collective-permute-start.8
  38.5 2.3 %collective-permute-start.9 = (bf16[128,576]{1,0:T(8,128)(2,1)}, bf16[128,576]{1,0:T(8,128)(2,1)S(1)}, u32[]{:S(2)}, u32[]{:S(2)}) collective-permute-start(bf16[128,576]{1,0:T(8,128)(2,1)} %shard_map.56.qa), channel_id=1, source_target_pairs={{0,2},{1,3},{2,0},{3,1},{4,6},{5,7},{6,4},{7,5},{8,10},{9,11},{10,... | collective-permute-start | bytes 442376 | tf_op jit(solution)/shard_map/ppermute | solution.py:45
  41.5 2.0 %collective-permute-done.10.qd = bf16[128,576]{1,0:T(8,128)(2,1)S(1)} collective-permute-done((bf16[128,576]{1,0:T(8,128)(2,1)}, bf16[128,576]{1,0:T(8,128)(2,1)S(1)}, u32[]{:S(2)}, u32[]{:S(2)}) %collective-permute-start.10) | collective-permute-done | bytes 147488 | tf_op jit(solution)/shard_map/ppermute | solution.py:45
  43.5 4.7 %collective-permute-done.8.qb = bf16[128,576]{1,0:T(8,128)(2,1)S(1)} collective-permute-done((bf16[128,576]{1,0:T(8,128)(2,1)}, bf16[128,576]{1,0:T(8,128)(2,1)S(1)}, u32[]{:S(2)}, u32[]{:S(2)}) %collective-permute-start.8) | collective-permute-done | bytes 147488 | tf_op jit(solution)/shard_map/ppermute | solution.py:45
  48.1 0.0 collective-permute-done.9.qc
  48.1 0.0 copy-done.14
  48.1 0.6 copy-done.15
  48.8 0.1 copy-done.16
  48.8 16.4 %shard_map.57 = (bf16[128,640]{1,0:T(8,128)(2,1)}, bf16[128,640]{1,0:T(8,128)(2,1)}, bf16[128,640]{1,0:T(8,128)(2,1)}, bf16[128,640]{1,0:T(8,128)(2,1)}) custom-call(s32[1]{0:T(128)S(6)} %min.6.live_ref, bf16[128,576]{1,0:T(8,128)(2,1)} %shard_map.56.qa, bf16[128,576]{1,0:T(8,128)(2,1)} %copy-done.15, bf16[128,576]{1,0:T(8,128)(2,1)} %copy-done.16, ...), custom_call_target="tpu_custom_call" | custom-call | flops 9126805504 | bytes 9437184 | tf_op jit(solution)/shard_map/pallas_call | solution.py:198
  65.3 0.7 collective-permute-start.11
  66.0 0.5 collective-permute-start.12
  66.5 0.9 collective-permute-start.13
  67.4 3.5 %collective-permute-done.11.b = bf16[128,640]{1,0:T(8,128)(2,1)S(1)} collective-permute-done((bf16[128,640]{1,0:T(8,128)(2,1)}, bf16[128,640]{1,0:T(8,128)(2,1)S(1)}, u32[]{:S(2)}, u32[]{:S(2)}) %collective-permute-start.11) | collective-permute-done | bytes 163872 | tf_op jit(solution)/shard_map/ppermute | solution.py:45
  70.9 2.2 %collective-permute-done.12.c = bf16[128,640]{1,0:T(8,128)(2,1)S(1)} collective-permute-done((bf16[128,640]{1,0:T(8,128)(2,1)}, bf16[128,640]{1,0:T(8,128)(2,1)S(1)}, u32[]{:S(2)}, u32[]{:S(2)}) %collective-permute-start.12) | collective-permute-done | bytes 163872 | tf_op jit(solution)/shard_map/ppermute | solution.py:45
  73.1 1.6 %collective-permute-done.13.d = bf16[128,640]{1,0:T(8,128)(2,1)S(1)} collective-permute-done((bf16[128,640]{1,0:T(8,128)(2,1)}, bf16[128,640]{1,0:T(8,128)(2,1)S(1)}, u32[]{:S(2)}, u32[]{:S(2)}) %collective-permute-start.13) | collective-permute-done | bytes 163872 | tf_op jit(solution)/shard_map/ppermute | solution.py:45
  74.8 0.0 copy-done
  74.8 0.0 copy-done.1
  74.8 0.7 copy-done.2
  75.4 2.2 %shard_map.58 = (bf16[32,640]{1,0:T(8,128)(2,1)}, bf16[32,640]{1,0:T(8,128)(2,1)}, bf16[32,640]{1,0:T(8,128)(2,1)}, bf16[32,640]{1,0:T(8,128)(2,1)}) custom-call(bf16[128,640]{1,0:T(8,128)(2,1)} %get-tuple-element.17.a, bf16[128,640]{1,0:T(8,128)(2,1)} %copy-done, bf16[128,640]{1,0:T(8,128)(2,1)} %copy-done.1, bf16[128,640]{1,0:T(8,128)(2,1)} %copy-done.2), custom_call_target="tpu_custom_call" | custom-call | tf_op jit(solution)/shard_map/pallas_call | solution.py:231
  77.7 2.2 %collective-permute-start.14 = (bf16[32,640]{1,0:T(8,128)(2,1)}, bf16[32,640]{1,0:T(8,128)(2,1)S(1)}, u32[]{:S(2)}, u32[]{:S(2)}) collective-permute-start(bf16[32,640]{1,0:T(8,128)(2,1)} %get-tuple-element.22), channel_id=1, source_target_pairs={{0,12},{1,13},{2,14},{3,15},{4,0},{5,1},{6,2},{7,3},{8,4},{9,5},{1... | collective-permute-start | bytes 122888 | tf_op jit(solution)/shard_map/ppermute | solution.py:40
  79.9 0.4 collective-permute-start.15
  80.3 0.9 collective-permute-start.16
  81.2 0.7 collective-permute-done.14.b
  81.9 3.8 %collective-permute-done.15.c = bf16[32,640]{1,0:T(8,128)(2,1)S(1)} collective-permute-done((bf16[32,640]{1,0:T(8,128)(2,1)}, bf16[32,640]{1,0:T(8,128)(2,1)S(1)}, u32[]{:S(2)}, u32[]{:S(2)}) %collective-permute-start.15) | collective-permute-done | bytes 40992 | tf_op jit(solution)/shard_map/ppermute | solution.py:40
  85.6 0.4 collective-permute-done.16.d
  86.0 0.0 copy-done.7
  86.0 0.2 copy-done.8
  86.2 0.4 copy-done.9
  86.6 2.5 %shard_map.59 = bf16[4,8,128]{2,1,0:T(8,128)(2,1)} custom-call(bf16[32,640]{1,0:T(8,128)(2,1)} %get-tuple-element.21.a, bf16[32,640]{1,0:T(8,128)(2,1)} %copy-done.7, bf16[32,640]{1,0:T(8,128)(2,1)} %copy-done.8, bf16[32,640]{1,0:T(8,128)(2,1)} %copy-done.9, bf16[8,512,128]{2,1,0:T(8,128)(2,1)} %all-gather.2.cloned.1.call-done.weight), custom_call_target="tpu_custom_call" | custom-call | tf_op jit(solution)/shard_map/pallas_call | solution.py:250
  (15 shorter events, 0.0 us)
Async XLA Ops:
  6.5 79.5 %all-gather.2.cloned.1.call-start = ((), (), s32[]{:S(2)}) async-start(), calls=%async_computation | async-start | bytes 1179648 | tf_op jit(solution)/shard_map/all_gather | solution.py:266
  7.3 7.4 %collective-permute-start.1 = (bf16[8,64,128]{2,1,0:T(8,128)(2,1)}, bf16[8,64,128]{2,1,0:T(8,128)(2,1)S(1)}, u32[]{:S(2)}, u32[]{:S(2)}) collective-permute-start(bf16[8,64,128]{2,1,0:T(8,128)(2,1)} %bitcast.9), channel_id=1, source_target_pairs={{0,32},{16,48},{32,64},{48,80},{64,96},{80,112},{96,0},{112,16},{1... | collective-permute-start | bytes 393224 | tf_op jit(solution)/shard_map/ppermute | solution.py:30
  9.0 9.1 %collective-permute-start.2 = (bf16[8,64,128]{2,1,0:T(8,128)(2,1)}, bf16[8,64,128]{2,1,0:T(8,128)(2,1)S(1)}, u32[]{:S(2)}, u32[]{:S(2)}) collective-permute-start(bf16[8,64,128]{2,1,0:T(8,128)(2,1)} %bitcast.10), channel_id=1, source_target_pairs={{0,64},{16,80},{32,96},{48,112},{64,0},{80,16},{96,32},{112,48},{1... | collective-permute-start | bytes 393224 | tf_op jit(solution)/shard_map/ppermute | solution.py:30
  11.9 6.2 %collective-permute-start.3 = (bf16[8,64,128]{2,1,0:T(8,128)(2,1)}, bf16[8,64,128]{2,1,0:T(8,128)(2,1)S(1)}, u32[]{:S(2)}, u32[]{:S(2)}) collective-permute-start(bf16[8,64,128]{2,1,0:T(8,128)(2,1)} %bitcast.11), channel_id=1, source_target_pairs={{0,96},{16,112},{32,0},{48,16},{64,32},{80,48},{96,64},{112,80},{1... | collective-permute-start | bytes 393224 | tf_op jit(solution)/shard_map/ppermute | solution.py:30
  13.2 1.4 %collective-permute-start = (bf16[4,8,192]{2,1,0:T(8,128)(2,1)}, bf16[4,8,192]{2,1,0:T(8,128)(2,1)S(1)}, u32[]{:S(2)}, u32[]{:S(2)}) collective-permute-start(bf16[4,8,192]{2,1,0:T(8,128)(2,1)} %bitcast.13), channel_id=1, source_target_pairs={{0,16},{16,0},{32,48},{48,32},{64,80},{80,64},{96,112},{112,96},{1... | collective-permute-start | bytes 36872 | tf_op jit(solution)/shard_map/ppermute | solution.py:35
  14.6 3.5 %copy-start.13 = (bf16[4,8,192]{2,1,0:T(8,128)(2,1)}, bf16[4,8,192]{2,1,0:T(8,128)(2,1)S(1)}, u32[]{:S(2)}) copy-start(bf16[4,8,192]{2,1,0:T(8,128)(2,1)S(1)} %collective-permute-done.other) | copy-start | bytes 36868
  14.6 3.5 %copy-start.4 = (bf16[8,64,128]{2,1,0:T(8,128)(2,1)}, bf16[8,64,128]{2,1,0:T(8,128)(2,1)S(1)}, u32[]{:S(2)}) copy-start(bf16[8,64,128]{2,1,0:T(8,128)(2,1)S(1)} %collective-permute-done.1.kw1) | copy-start | bytes 393220
  18.1 0.6 copy-start.5
  18.8 0.7 copy-start.6
  21.8 1.4 %collective-permute-start.4 = (bf16[8,4,576]{2,1,0:T(4,128)(2,1)}, bf16[8,4,576]{2,1,0:T(4,128)(2,1)S(1)}, u32[]{:S(2)}, u32[]{:S(2)}) collective-permute-start(bf16[8,4,576]{2,1,0:T(4,128)(2,1)} %get-tuple-element.16), channel_id=1, source_target_pairs={{0,16},{16,0},{32,48},{48,32},{64,80},{80,64},{96,112},{112,96},{1... | collective-permute-start | bytes 110600 | tf_op jit(solution)/shard_map/ppermute | solution.py:35
  24.0 9.6 %copy-start.3 = (bf16[32,576]{1,0:T(8,128)(2,1)}, bf16[32,576]{1,0:T(8,128)(2,1)S(1)}, u32[]{:S(2)}) copy-start(bf16[32,576]{1,0:T(8,128)(2,1)S(1)} %reshape.3.a) | copy-start | bytes 110596
  24.0 6.6 %collective-permute-start.5 = (bf16[32,576]{1,0:T(8,128)(2,1)S(1)}, bf16[32,576]{1,0:T(8,128)(2,1)S(1)}, u32[]{:S(2)}, u32[]{:S(2)}) collective-permute-start(bf16[32,576]{1,0:T(8,128)(2,1)S(1)} %reshape.3.a), channel_id=1, source_target_pairs={{0,4},{1,5},{2,6},{3,7},{4,8},{5,9},{6,10},{7,11},{8,12},{9,13},{1... | collective-permute-start | bytes 110600 | tf_op jit(solution)/shard_map/ppermute | solution.py:40
  26.0 6.1 %collective-permute-start.6 = (bf16[32,576]{1,0:T(8,128)(2,1)S(1)}, bf16[32,576]{1,0:T(8,128)(2,1)S(1)}, u32[]{:S(2)}, u32[]{:S(2)}) collective-permute-start(bf16[32,576]{1,0:T(8,128)(2,1)S(1)} %reshape.3.a), channel_id=1, source_target_pairs={{0,8},{1,9},{2,10},{3,11},{4,12},{5,13},{6,14},{7,15},{8,0},{9,1},... | collective-permute-start | bytes 110600 | tf_op jit(solution)/shard_map/ppermute | solution.py:40
  29.6 4.0 %collective-permute-start.7 = (bf16[32,576]{1,0:T(8,128)(2,1)S(1)}, bf16[32,576]{1,0:T(8,128)(2,1)S(1)}, u32[]{:S(2)}, u32[]{:S(2)}) collective-permute-start(bf16[32,576]{1,0:T(8,128)(2,1)S(1)} %reshape.3.a), channel_id=1, source_target_pairs={{0,12},{1,13},{2,14},{3,15},{4,0},{5,1},{6,2},{7,3},{8,4},{9,5},{1... | collective-permute-start | bytes 110600 | tf_op jit(solution)/shard_map/ppermute | solution.py:40
  30.6 3.0 %copy-start.10 = (bf16[32,576]{1,0:T(8,128)(2,1)}, bf16[32,576]{1,0:T(8,128)(2,1)S(1)}, u32[]{:S(2)}) copy-start(bf16[32,576]{1,0:T(8,128)(2,1)S(1)} %collective-permute-done.5.b) | copy-start | bytes 110596
  32.1 1.5 %copy-start.11 = (bf16[32,576]{1,0:T(8,128)(2,1)}, bf16[32,576]{1,0:T(8,128)(2,1)S(1)}, u32[]{:S(2)}) copy-start(bf16[32,576]{1,0:T(8,128)(2,1)S(1)} %collective-permute-done.6.c) | copy-start | bytes 110596
  33.6 0.6 copy-start.12
  35.8 7.7 %collective-permute-start.10 = (bf16[128,576]{1,0:T(8,128)(2,1)}, bf16[128,576]{1,0:T(8,128)(2,1)S(1)}, u32[]{:S(2)}, u32[]{:S(2)}) collective-permute-start(bf16[128,576]{1,0:T(8,128)(2,1)} %shard_map.56.qa), channel_id=1, source_target_pairs={{0,3},{1,0},{2,1},{3,2},{4,7},{5,4},{6,5},{7,6},{8,11},{9,8},{10,9... | collective-permute-start | bytes 442376 | tf_op jit(solution)/shard_map/ppermute | solution.py:45
  38.5 9.6 %collective-permute-start.8 = (bf16[128,576]{1,0:T(8,128)(2,1)}, bf16[128,576]{1,0:T(8,128)(2,1)S(1)}, u32[]{:S(2)}, u32[]{:S(2)}) collective-permute-start(bf16[128,576]{1,0:T(8,128)(2,1)} %shard_map.56.qa), channel_id=1, source_target_pairs={{0,1},{1,2},{2,3},{3,0},{4,5},{5,6},{6,7},{7,4},{8,9},{9,10},{10,1... | collective-permute-start | bytes 442376 | tf_op jit(solution)/shard_map/ppermute | solution.py:45
  38.5 9.6 %collective-permute-start.9 = (bf16[128,576]{1,0:T(8,128)(2,1)}, bf16[128,576]{1,0:T(8,128)(2,1)S(1)}, u32[]{:S(2)}, u32[]{:S(2)}) collective-permute-start(bf16[128,576]{1,0:T(8,128)(2,1)} %shard_map.56.qa), channel_id=1, source_target_pairs={{0,2},{1,3},{2,0},{3,1},{4,6},{5,7},{6,4},{7,5},{8,10},{9,11},{10,... | collective-permute-start | bytes 442376 | tf_op jit(solution)/shard_map/ppermute | solution.py:45
  43.5 4.7 %copy-start.14 = (bf16[128,576]{1,0:T(8,128)(2,1)}, bf16[128,576]{1,0:T(8,128)(2,1)S(1)}, u32[]{:S(2)}) copy-start(bf16[128,576]{1,0:T(8,128)(2,1)S(1)} %collective-permute-done.10.qd) | copy-start | bytes 442372
  48.1 0.7 copy-start.15
  48.1 0.7 copy-start.16
  65.3 5.6 %collective-permute-start.11 = (bf16[128,640]{1,0:T(8,128)(2,1)}, bf16[128,640]{1,0:T(8,128)(2,1)S(1)}, u32[]{:S(2)}, u32[]{:S(2)}) collective-permute-start(bf16[128,640]{1,0:T(8,128)(2,1)} %get-tuple-element.18), channel_id=1, source_target_pairs={{0,3},{1,0},{2,1},{3,2},{4,7},{5,4},{6,5},{7,6},{8,11},{9,8},{10,9... | collective-permute-start | bytes 491528 | tf_op jit(solution)/shard_map/ppermute | solution.py:45
  66.0 7.1 %collective-permute-start.12 = (bf16[128,640]{1,0:T(8,128)(2,1)}, bf16[128,640]{1,0:T(8,128)(2,1)S(1)}, u32[]{:S(2)}, u32[]{:S(2)}) collective-permute-start(bf16[128,640]{1,0:T(8,128)(2,1)} %get-tuple-element.19), channel_id=1, source_target_pairs={{0,2},{1,3},{2,0},{3,1},{4,6},{5,7},{6,4},{7,5},{8,10},{9,11},{10,... | collective-permute-start | bytes 491528 | tf_op jit(solution)/shard_map/ppermute | solution.py:45
  66.5 8.3 %collective-permute-start.13 = (bf16[128,640]{1,0:T(8,128)(2,1)}, bf16[128,640]{1,0:T(8,128)(2,1)S(1)}, u32[]{:S(2)}, u32[]{:S(2)}) collective-permute-start(bf16[128,640]{1,0:T(8,128)(2,1)} %get-tuple-element.20), channel_id=1, source_target_pairs={{0,1},{1,2},{2,3},{3,0},{4,5},{5,6},{6,7},{7,4},{8,9},{9,10},{10,1... | collective-permute-start | bytes 491528 | tf_op jit(solution)/shard_map/ppermute | solution.py:45
  70.9 3.9 %copy-start = (bf16[128,640]{1,0:T(8,128)(2,1)}, bf16[128,640]{1,0:T(8,128)(2,1)S(1)}, u32[]{:S(2)}) copy-start(bf16[128,640]{1,0:T(8,128)(2,1)S(1)} %collective-permute-done.11.b) | copy-start | bytes 491524
  73.1 1.7 %copy-start.1 = (bf16[128,640]{1,0:T(8,128)(2,1)}, bf16[128,640]{1,0:T(8,128)(2,1)S(1)}, u32[]{:S(2)}) copy-start(bf16[128,640]{1,0:T(8,128)(2,1)S(1)} %collective-permute-done.12.c) | copy-start | bytes 491524
  74.8 0.7 copy-start.2
  77.7 4.2 %collective-permute-start.14 = (bf16[32,640]{1,0:T(8,128)(2,1)}, bf16[32,640]{1,0:T(8,128)(2,1)S(1)}, u32[]{:S(2)}, u32[]{:S(2)}) collective-permute-start(bf16[32,640]{1,0:T(8,128)(2,1)} %get-tuple-element.22), channel_id=1, source_target_pairs={{0,12},{1,13},{2,14},{3,15},{4,0},{5,1},{6,2},{7,3},{8,4},{9,5},{1... | collective-permute-start | bytes 122888 | tf_op jit(solution)/shard_map/ppermute | solution.py:40
  79.9 5.8 %collective-permute-start.15 = (bf16[32,640]{1,0:T(8,128)(2,1)}, bf16[32,640]{1,0:T(8,128)(2,1)S(1)}, u32[]{:S(2)}, u32[]{:S(2)}) collective-permute-start(bf16[32,640]{1,0:T(8,128)(2,1)} %get-tuple-element.23), channel_id=1, source_target_pairs={{0,8},{1,9},{2,10},{3,11},{4,12},{5,13},{6,14},{7,15},{8,0},{9,1},... | collective-permute-start | bytes 122888 | tf_op jit(solution)/shard_map/ppermute | solution.py:40
  80.3 5.7 %collective-permute-start.16 = (bf16[32,640]{1,0:T(8,128)(2,1)}, bf16[32,640]{1,0:T(8,128)(2,1)S(1)}, u32[]{:S(2)}, u32[]{:S(2)}) collective-permute-start(bf16[32,640]{1,0:T(8,128)(2,1)} %get-tuple-element.24), channel_id=1, source_target_pairs={{0,4},{1,5},{2,6},{3,7},{4,8},{5,9},{6,10},{7,11},{8,12},{9,13},{1... | collective-permute-start | bytes 122888 | tf_op jit(solution)/shard_map/ppermute | solution.py:40
  81.9 4.2 %copy-start.7 = (bf16[32,640]{1,0:T(8,128)(2,1)}, bf16[32,640]{1,0:T(8,128)(2,1)S(1)}, u32[]{:S(2)}) copy-start(bf16[32,640]{1,0:T(8,128)(2,1)S(1)} %collective-permute-done.14.b) | copy-start | bytes 122884
  85.6 0.6 copy-start.8
  86.0 0.6 copy-start.9
Sparse Core Ops, SparseCore 0:
  9.0 25.8 all-gather.1

commit v2 on v1

v2 whole, which is shorter than its diff:
```python
import functools

import jax
import jax.numpy as jnp
from jax import lax
from jax.experimental import pallas as pl
from jax.experimental.pallas import tpu as pltpu
from jax.sharding import PartitionSpec as P

NOPE = 128
ROPE = 64
LATENT = 512
WIDTH = LATENT + ROPE
PAYLOAD = LATENT + 128
RING = 4
CORES = 2

MASKED = -1e30
TO_LOG2 = (NOPE + ROPE) ** (-0.5) * 1.4426950408889634

VMEM = pl.BlockSpec(memory_space=pltpu.VMEM)
HBM = pl.BlockSpec(memory_space=pltpu.HBM)
SMEM = pl.BlockSpec(memory_space=pltpu.SMEM)
BF16 = jnp.bfloat16
F32 = jnp.float32


def exchange(value, move):
    pairs = []
    for y in range(RING):
        for core in range(CORES):
            for z in range(RING):
                for x in range(RING):
                    to_y, to_core, to_z, to_x = (at % size for at, size in zip(move(y, core, z, x), (RING, CORES, RING, RING)))
                    source = ((y * CORES + core) * RING + z) * RING + x
                    target = ((to_y * CORES + to_core) * RING + to_z) * RING + to_x
                    pairs.append((source, target))
    return lax.ppermute(value, ("roll", "seq"), pairs)


def core_swap(value):
    return exchange(value, lambda y, core, z, x: (y, core + 1, z, x))


def y_shift(value, hops):
    return exchange(value, lambda y, core, z, x: (y + hops, core, z, x))


def first_shift(value, hops):
    return exchange(value, lambda y, core, z, x: (y, core, z + hops * (1 - core), x + hops * core))


def second_shift(value, hops):
    return exchange(value, lambda y, core, z, x: (y, core, z + hops * core, x + hops * (1 - core)))


def two_terms(value):
    high = value.astype(BF16).astype(F32)
    return high, (value - high).astype(BF16).astype(F32)


def pack_stats(top, total):
    lane = lax.broadcasted_iota(jnp.int32, top.shape, 1)
    packed = jnp.zeros(top.shape, F32)
    for at, term in enumerate(two_terms(top) + two_terms(total)):
        packed = jnp.where(lane == at, term, packed)
    return packed.astype(BF16)


def spread(stats, first):
    row = lax.broadcasted_iota(jnp.int32, (128, 128), 0)
    chosen = ((row == first) | (row == first + 1)).astype(F32).astype(BF16)
    return jnp.dot(stats, chosen, preferred_element_type=F32)


def merge(parts):
    tops = [spread(part[:, LATENT:], 0) for part in parts]
    totals = [spread(part[:, LATENT:], 2) for part in parts]
    top = functools.reduce(jnp.maximum, tops)
    weights = [jnp.exp2(t - top) * n for t, n in zip(tops, totals)]
    total = functools.reduce(jnp.add, weights)
    inverse = jnp.where(total > 0, 1.0 / total, 0.0)
    weights = [w * inverse for w in weights]
    columns = []
    for at in range(0, LATENT, 128):
        terms = [part[:, at : at + 128].astype(F32) * w for part, w in zip(parts, weights)]
        columns.append(functools.reduce(jnp.add, terms))
    return columns, top, total


def load_kernel(cache, block, query, value, *refs):
    sources, targets, sems = (cache, block, query, value), refs[:4], refs[4]
    copies = [pltpu.make_async_copy(a, b, sems.at[i]) for i, (a, b) in enumerate(zip(sources, targets))]
    for copy in copies:
        copy.start()
    for copy in copies:
        copy.wait()


def load(*arrays):
    return pl.pallas_call(
        load_kernel,
        out_shape=[jax.ShapeDtypeStruct(a.shape, a.dtype) for a in arrays],
        in_specs=[HBM] * 4,
        out_specs=[VMEM] * 4,
        scratch_shapes=[pltpu.SemaphoreType.DMA((4,))],
        compiler_params=pltpu.CompilerParams(vmem_limit_bytes=16 * 2**20),
        cost_estimate=pl.CostEstimate(
            flops=0, bytes_accessed=2 * sum(a.size * 2 for a in arrays), transcendentals=0
        ),
    )(*arrays)


def absorb_kernel(mine, other, kw0, kw1, kw2, kw3, out_mine, out_other, weights):
    roll = lax.axis_index("roll")
    y, core = roll // CORES, lax.rem(roll, CORES)
    frames, heads, _ = mine.shape
    weights[...] = jnp.zeros_like(weights)
    for hops, block in enumerate((kw0, kw1, kw2, kw3)):
        chunk = lax.rem(y + RING - hops, RING) * CORES + core
        weights[:, pl.ds(pl.multiple_of(chunk * 64, 64), 64), :] = block[...]
    absorbed = []
    for h in range(heads):
        rows = jnp.concatenate([mine[:, h, :NOPE], other[:, h, :NOPE]], axis=0)
        absorbed.append(
            lax.dot_general(rows, weights[h], (((1,), (1,)), ((), ())), preferred_element_type=F32)
        )
    out_mine[:, :LATENT] = jnp.concatenate([a[:frames] for a in absorbed], axis=0).astype(BF16)
    out_other[:, :LATENT] = jnp.concatenate([a[frames:] for a in absorbed], axis=0).astype(BF16)
    out_other[:, LATENT:] = jnp.zeros((heads * frames, ROPE), BF16)
    rope = [mine[:, h, NOPE:].astype(F32) for h in range(heads)]
    out_mine[:, LATENT:] = jnp.concatenate(rope, axis=0).astype(BF16)


def absorb(mine, other, blocks):
    frames, heads, _ = mine.shape
    shape = jax.ShapeDtypeStruct((heads * frames, WIDTH), BF16)
    return pl.pallas_call(
        absorb_kernel,
        out_shape=[shape, shape],
        in_specs=[VMEM] * 6,
        out_specs=[VMEM, VMEM],
        scratch_shapes=[pltpu.VMEM((heads, LATENT, NOPE), BF16)],
    )(mine, other, *blocks)


def stack_kernel(a, b, c, d, out):
    rows = a.shape[0]
    for at, block in enumerate((a, b, c, d)):
        out[at * rows : (at + 1) * rows, :] = block[...]


def stack(blocks):
    rows, width = blocks[0].shape
    return pl.pallas_call(
        stack_kernel,
        out_shape=jax.ShapeDtypeStruct((4 * rows, width), BF16),
        in_specs=[VMEM] * 4,
        out_specs=VMEM,
    )(*blocks)


def fold(op, value):
    so_far = value[:, :128]
    for at in range(128, value.shape[1], 128):
        so_far = op(so_far, value[:, at : at + 128])
    return so_far


def attend_kernel(length, qa, qb, cache, oa, ob, query, scores, tops, totals, acc, *, block):
    span = cache.shape[1]
    blocks = span // block
    live = jnp.clip(length[0] - lax.axis_index("seq") * span, 0, span)
    group = qa.shape[0]
    query[:group, :] = qa[...]
    query[group:, :] = qb[...]

    def here(i):
        return pl.ds(i * block if isinstance(i, int) else pl.multiple_of(i * block, block), block)

    def score(i):
        return jnp.dot(query[...], cache[:, here(i)], preferred_element_type=F32)

    def weigh(i, p):
        return lax.dot_general(
            p.astype(BF16), cache[:LATENT, here(i)], (((1,), (1,)), ((), ())), preferred_element_type=F32
        )

    def largest(value):
        return jnp.broadcast_to(jnp.max(value, axis=1, keepdims=True), value.shape)

    def finish(top):
        total = jnp.broadcast_to(jnp.sum(totals[...], axis=1, keepdims=True), totals.shape)
        inverse = jnp.where(total > 0, 1.0 / total, 0.0)
        high, low = two_terms(top)
        sent = high + low
        stats = pack_stats(sent, total * jnp.exp2(top - sent))
        for at, out in enumerate((oa, ob)):
            rows = slice(at * group, (at + 1) * group)
            for column in range(0, LATENT, 128):
                lanes = slice(column, column + 128)
                out[:, lanes] = (acc[rows, lanes] * inverse[rows]).astype(BF16)
            out[:, LATENT:] = stats[rows]

    def scaled(value, factor):
        return jnp.concatenate([value[:, at : at + 128] * factor for at in range(0, LATENT, 128)], axis=1)

    @pl.when(live >= span)
    def _():
        scores[:, here(0)] = score(0)
        for i in range(blocks):
            s = scores[:, here(i % 2)]
            if i + 1 < blocks:
                scores[:, here((i + 1) % 2)] = score(i + 1)
            block_top = largest(fold(jnp.maximum, s)) * TO_LOG2
            top = block_top if i == 0 else jnp.maximum(tops[...], block_top)
            p = jnp.exp2(s * TO_LOG2 - top[:, :1])
            if i == 0:
                totals[...] = fold(jnp.add, p)
                acc[...] = weigh(i, p)
            else:
                factor = jnp.exp2(tops[...] - top)
                totals[...] = totals[...] * factor + fold(jnp.add, p)
                acc[...] = scaled(acc[...], factor) + weigh(i, p)
            tops[...] = top
        finish(tops[...])

    @pl.when(live < span)
    def _():
        whole = live // block
        some = (live + block - 1) // block
        tops[...] = jnp.full(tops.shape, MASKED, F32)
        totals[...] = jnp.zeros(totals.shape, F32)
        acc[...] = jnp.zeros(acc.shape, F32)

        def fill(i, masked):
            s = score(i)
            if masked:
                s = jnp.where(i * block + lax.broadcasted_iota(jnp.int32, s.shape, 1) < live, s, MASKED)
            scores[:, here(i)] = s
            tops[...] = jnp.maximum(tops[...], fold(jnp.maximum, s))

        def loop(first, last, body):
            lax.fori_loop(first, last, lambda i, c: (body(i), c)[1], 0)

        loop(0, whole, lambda i: fill(i, False))
        loop(whole, some, lambda i: fill(i, True))
        top = largest(tops[...]) * TO_LOG2

        def add(i):
            p = jnp.exp2(scores[:, here(i)] * TO_LOG2 - top[:, :1])
            totals[...] += fold(jnp.add, p)
            acc[...] += weigh(i, p)

        loop(0, some, add)
        finish(top)


def attend(length, parts, cache, block=1024):
    group = parts[0].shape[0]
    rows, span = group * len(parts), cache.shape[1]
    return pl.pallas_call(
        functools.partial(attend_kernel, block=block),
        out_shape=[jax.ShapeDtypeStruct((group, PAYLOAD), BF16)] * 2,
        in_specs=[SMEM] + [VMEM] * 3,
        out_specs=[VMEM] * 2,
        scratch_shapes=[
            pltpu.VMEM((rows, WIDTH), BF16),
            pltpu.VMEM((rows, span), F32),
            pltpu.VMEM((rows, 128), F32),
            pltpu.VMEM((rows, 128), F32),
            pltpu.VMEM((rows, LATENT), F32),
        ],
        compiler_params=pltpu.CompilerParams(vmem_limit_bytes=24 * 2**20),
        cost_estimate=pl.CostEstimate(
            flops=2 * rows * span * (WIDTH + LATENT), bytes_accessed=span * WIDTH * 2, transcendentals=rows * span
        ),
    )(length, *parts, cache)


def merge_kernel(a, b, c, d, oa, ob, oc, od):
    columns, top, total = merge([a, b, c, d])
    stats = pack_stats(top, total)
    rows = oa.shape[0]
    for at, part in enumerate((oa, ob, oc, od)):
        here = slice(at * rows, (at + 1) * rows)
        for j, column in enumerate(columns):
            part[:, j * 128 : (j + 1) * 128] = column[here].astype(BF16)
        part[:, LATENT:] = stats[here]


def merge_groups(parts):
    rows, width = parts[0].shape
    return pl.pallas_call(
        merge_kernel,
        out_shape=[jax.ShapeDtypeStruct((rows // 4, width), BF16)] * 4,
        in_specs=[VMEM] * 4,
        out_specs=[VMEM] * 4,
    )(*parts)


def pair_kernel(mine, other, out):
    core = lax.rem(lax.axis_index("roll"), CORES)
    out[core] = mine[...]
    out[1 - core] = other[...]


def pair(mine, other):
    return pl.pallas_call(
        pair_kernel,
        out_shape=jax.ShapeDtypeStruct((CORES,) + mine.shape, BF16),
        in_specs=[VMEM, VMEM],
        out_specs=VMEM,
    )(mine, other)


def finish_kernel(a, b, c, d, w0, w1, w2, w3, out, context, weight):
    y = lax.axis_index("roll") // CORES
    for hops, block in enumerate((w0, w1, w2, w3)):
        chunk = lax.rem(y + RING - hops, RING) * CORES
        for core in range(CORES):
            weight[:, pl.ds(pl.multiple_of((chunk + core) * 64, 64), 64), :] = block[core]
    for j, column in enumerate(merge([a, b, c, d])[0]):
        context[:, j * 128 : (j + 1) * 128] = column.astype(BF16)
    frames, heads, _ = out.shape
    for h in range(heads):
        out[:, h, :] = jnp.dot(
            context[h * frames : (h + 1) * frames, :], weight[h], preferred_element_type=F32
        ).astype(BF16)


def finish(parts, weights, frames):
    _, heads, _, vhead = weights[0].shape
    return pl.pallas_call(
        finish_kernel,
        out_shape=jax.ShapeDtypeStruct((frames, heads, vhead), BF16),
        in_specs=[VMEM] * 8,
        out_specs=VMEM,
        scratch_shapes=[
            pltpu.VMEM((frames * heads, LATENT), BF16),
            pltpu.VMEM((heads, LATENT, vhead), BF16),
        ],
    )(*parts, *weights)


def on_device(queries, latent_cache, lengths, key_weight, value_weight):
    frames = queries.shape[1]
    lengths = lengths.astype(jnp.int32)
    cache, block = latent_cache[0].T, jnp.swapaxes(key_weight, 1, 2)
    mine = queries[0]

    blocks = [y_shift(block, hops) for hops in (1, 2, 3)]
    other, value_other = core_swap(mine), core_swap(value_weight)
    cache, block, mine, value_mine = load(cache, block, mine, value_weight)
    own, others = absorb(mine, other, [block] + blocks)
    value_pair = pair(value_mine, value_other)
    local = own + core_swap(others)

    local, value_pair = lax.optimization_barrier((local, value_pair))
    near = stack([local] + [first_shift(local, hops) for hops in (1, 2, 3)])
    groups = [near] + [second_shift(near, hops) for hops in (1, 2, 3)]
    value_pairs = [value_pair] + [y_shift(value_pair, hops) for hops in (1, 2, 3)]

    early = attend(lengths, groups[:2], cache)
    groups, value_pairs = lax.optimization_barrier((groups, value_pairs))
    late = attend(lengths, groups[2:], cache)
    parts = list(early) + list(late)

    near = merge_groups([parts[0]] + [second_shift(parts[hops], -hops) for hops in (1, 2, 3)])
    last = [near[0]] + [first_shift(near[hops], -hops) for hops in (1, 2, 3)]
    return finish(last, value_pairs, frames)[None]


def solution(mesh):
    placed = (
        P("roll", None, "seq", None),
        P("roll", "seq", None),
        P("roll"),
        P("seq", None, "roll"),
        P("seq", "roll", None),
    )
    return jax.shard_map(
        on_device,
        mesh=mesh,
        in_specs=placed,
        out_specs=P("roll", None, "seq", None),
        check_vma=False,
    )
```

time: 95.5 us -> 88.5 us (0.927)
  local copies, waits for them, and re-layouts: 3.92 us -> 20.9 us
  between operations: 14.1 us -> 0.86 us
  waiting for transfers between devices: 28.2 us -> 15.8 us
  starting transfers between devices: 23.3 us -> 25.2 us
    unnamed x34 -> x58, local copies, waits for them, and re-layouts: 3.89 us -> 20.9 us
    ppermute x17 -> x21, waiting for transfers between devices: 27.5 us -> 15.8 us  [exchange(): return lax.ppermute(value, ('roll', 'seq'), pairs)]
    pallas_call x1 -> x2, Pallas kernels: 16.4 us -> 13.5 us  [attend(): pl.pallas_call(functools.partial(attend_kernel, block=block), out_shape=[...]
    pallas_call x1 -> x3, Pallas kernels: 2.35 us -> 5.04 us  [the longest x1 2.32 us: absorb(): pl.pallas_call(absorb_kernel, out_shape=[shape, shape], in_specs=[VMEM] *...]
    ppermute x17 -> x21, starting transfers between devices: 23.2 us -> 25.2 us  [exchange(): return lax.ppermute(value, ('roll', 'seq'), pairs)]
  transfers between devices with their start and end apart: 18 -> 21, of which waited for: 13 -> 7; matrix products, arithmetic and copies ran while one was open for 2% -> 0% of each run, Pallas kernels for 23% -> 21%
where the time goes in v2:
time: 88.5 us; the launch traced here: 88 us
  starting transfers between devices  25.2 us (28%)
  Pallas kernels  24.5 us (28%)
  local copies, waits for them, and re-layouts  20.9 us (24%)
  waiting for transfers between devices  15.8 us (18%)
    ppermute x21, starting transfers between devices, exchange(): return lax.ppermute(value, ('roll', 'seq'), pairs)  25.2 us
    unnamed x58, local copies, waits for them, and re-layouts  20.9 us
    ppermute x21, waiting for transfers between devices, exchange(): return lax.ppermute(value, ('roll', 'seq'), pairs)  15.8 us
    pallas_call x2, Pallas kernels, attend(): pl.pallas_call(functools.partial(attend_kernel, block=block), out_shape=[...  13.5 us
    pallas_call x1, Pallas kernels, finish(): pl.pallas_call(finish_kernel, out_shape=jax.ShapeDtypeStruct((frames, hea...  2.38 us
    pallas_call x1, Pallas kernels, absorb(): pl.pallas_call(absorb_kernel, out_shape=[shape, shape], in_specs=[VMEM] *...  2.32 us
    pallas_call x1, Pallas kernels, merge_groups(): pl.pallas_call(merge_kernel, out_shape=[jax.ShapeDtypeStruct((rows // 4,...  2.11 us
  transfers between devices with their start and end apart: 21, of which 7 were waited for; matrix products, arithmetic and copies ran while one was open for 0% of the time, Pallas kernels for 21%

profile of v2, /device:TPU:0, one launch (start us, length us, event | category | flops | bytes accessed | tf_op | source)
XLA Modules:
  0.0 88.0 jit_solution(10650264029313238845)
XLA Ops:
  0.0 3.1 %collective-permute-start.3 = (bf16[8,64,128]{2,1,0:T(8,128)(2,1)}, bf16[8,64,128]{2,1,0:T(8,128)(2,1)S(1)}, u32[]{:S(2)}, u32[]{:S(2)}) collective-permute-start(bf16[8,64,128]{2,1,0:T(8,128)(2,1)} %bitcast.7), channel_id=1, source_target_pairs={{0,96},{1,97},{2,98},{3,99},{4,100},{5,101},{6,102},{7,103},{8,104... | collective-permute-start | bytes 393224 | tf_op jit(solution)/shard_map/ppermute | solution.py:38
  3.1 0.6 collective-permute-start.2
  3.7 1.0 %collective-permute-start.1 = (bf16[8,64,128]{2,1,0:T(8,128)(2,1)}, bf16[8,64,128]{2,1,0:T(8,128)(2,1)S(1)}, u32[]{:S(2)}, u32[]{:S(2)}) collective-permute-start(bf16[8,64,128]{2,1,0:T(8,128)(2,1)} %bitcast.9), channel_id=1, source_target_pairs={{0,32},{1,33},{2,34},{3,35},{4,36},{5,37},{6,38},{7,39},{8,40},{9,... | collective-permute-start | bytes 393224 | tf_op jit(solution)/shard_map/ppermute | solution.py:38
  4.7 0.0 collective-permute-start.5
  4.7 0.5 collective-permute-start
  5.2 3.7 %copy-done = bf16[1,8192,576]{1,2,0:T(8,128)(2,1)S(1)} copy-done((bf16[1,8192,576]{1,2,0:T(8,128)(2,1)S(1)}, bf16[1,8192,576]{1,2,0:T(8,128)(2,1)}, u32[]{:S(2)}) %copy-start) | copy-done | bytes 9437208
  8.9 0.9 %copy-done.3 = bf16[8,128,64]{1,2,0:T(8,128)(2,1)S(1)} copy-done((bf16[8,128,64]{1,2,0:T(8,128)(2,1)S(1)}, bf16[8,128,64]{1,2,0:T(8,128)(2,1)}, u32[]{:S(2)}) %copy-start.3) | copy-done | bytes 131096
  9.8 0.9 %copy-done.4 = bf16[8,64,128]{2,1,0:T(8,128)(2,1)S(1)} copy-done((bf16[8,64,128]{2,1,0:T(8,128)(2,1)S(1)}, bf16[8,64,128]{2,1,0:T(8,128)(2,1)}, u32[]{:S(2)}) %copy-start.4) | copy-done | bytes 131096
  10.7 0.7 copy-done.7
  11.4 1.0 %shard_map.55 = (bf16[576,8192]{1,0:T(8,128)(2,1)S(1)}, bf16[8,64,128]{2,1,0:T(8,128)(2,1)S(1)}, bf16[4,8,192]{2,1,0:T(8,128)(2,1)S(1)}, bf16[8,64,128]{2,1,0:T(8,128)(2,1)S(1)}) custom-call(bf16[576,8192]{1,0:T(8,128)(2,1)S(1)} %bitcast.6, bf16[8,64,128]{2,1,0:T(8,128)(2,1)S(1)} %bitcast.10, bf16[4,8,192]{2,1,0:T(8,128)(2,1)S(1)} %bitcast.12, ...), custom_call_target="tpu_custom_call" | custom-call | bytes 19423232 | tf_op jit(solution)/shard_map/pallas_call | solution.py:101
  12.5 0.6 copy-done.5
  13.1 0.7 copy-done.6
  13.8 0.6 copy-done.8
  14.4 3.6 %copy-done.9 = bf16[576,8192]{1,0:T(8,128)(2,1)} copy-done((bf16[576,8192]{1,0:T(8,128)(2,1)}, bf16[576,8192]{1,0:T(8,128)(2,1)S(1)}, u32[]{:S(2)}) %copy-start.9) | copy-done | bytes 9437208
  18.0 0.0 collective-permute-done.other
  18.0 0.0 collective-permute-done.3.kw3
  18.0 0.0 collective-permute-done.2.kw2
  18.0 0.0 collective-permute-done.1.kw1
  18.1 0.5 copy-done.28
  18.6 0.1 copy-done.18
  18.7 0.1 copy-done.19
  18.7 0.1 copy-done.20
  18.8 2.3 %shard_map.56 = (bf16[32,576]{1,0:T(8,128)(2,1)}, bf16[32,576]{1,0:T(8,128)(2,1)}) custom-call(bf16[4,8,192]{2,1,0:T(8,128)(2,1)} %copy-done.8, bf16[4,8,192]{2,1,0:T(8,128)(2,1)} %copy-done.28, bf16[8,64,128]{2,1,0:T(8,128)(2,1)} %copy-done.5, bf16[8,64,128]{2,1,0:T(8,128)(2,1)} %copy-done.20, bf16[8,64,128]{2,1,0:T(8,128)(2,1)} %copy-done.19, ...), custom_call_target="tpu_custom_call" | custom-call | tf_op jit(solution)/shard_map/pallas_call | solution.py:138
  21.1 0.0 collective-permute-start.4
  21.1 0.6 copy-done.21
  21.8 1.7 %shard_map.57.w0 = bf16[2,8,64,128]{3,2,1,0:T(8,128)(2,1)} custom-call(bf16[8,64,128]{2,1,0:T(8,128)(2,1)} %copy-done.6, bf16[8,64,128]{2,1,0:T(8,128)(2,1)} %copy-done.21), custom_call_target="tpu_custom_call" | custom-call | tf_op jit(solution)/shard_map/pallas_call | solution.py:309
  23.5 0.0 collective-permute-done.4
  23.5 0.8 add.3.a
  24.3 4.1 %collective-permute-start.8 = (bf16[32,576]{1,0:T(8,128)(2,1)S(1)}, bf16[32,576]{1,0:T(8,128)(2,1)S(1)}, u32[]{:S(2)}, u32[]{:S(2)}) collective-permute-start(bf16[32,576]{1,0:T(8,128)(2,1)S(1)} %add.3.a), channel_id=1, source_target_pairs={{0,12},{1,13},{2,14},{3,15},{4,0},{5,1},{6,2},{7,3},{8,4},{9,5},{1... | collective-permute-start | bytes 110600 | tf_op jit(solution)/shard_map/ppermute | solution.py:38
  28.4 0.0 collective-permute-start.7
  28.4 1.3 %collective-permute-start.6 = (bf16[32,576]{1,0:T(8,128)(2,1)S(1)}, bf16[32,576]{1,0:T(8,128)(2,1)S(1)}, u32[]{:S(2)}, u32[]{:S(2)}) collective-permute-start(bf16[32,576]{1,0:T(8,128)(2,1)S(1)} %add.3.a), channel_id=1, source_target_pairs={{0,4},{1,5},{2,6},{3,7},{4,8},{5,9},{6,10},{7,11},{8,12},{9,13},{1... | collective-permute-start | bytes 110600 | tf_op jit(solution)/shard_map/ppermute | solution.py:38
  29.7 0.4 collective-permute-done.8.d
  30.1 3.9 %collective-permute-done.7.c = bf16[32,576]{1,0:T(8,128)(2,1)S(1)} collective-permute-done((bf16[32,576]{1,0:T(8,128)(2,1)S(1)}, bf16[32,576]{1,0:T(8,128)(2,1)S(1)}, u32[]{:S(2)}, u32[]{:S(2)}) %collective-permute-start.7) | collective-permute-done | bytes 36896 | tf_op jit(solution)/shard_map/ppermute | solution.py:38
  34.0 0.0 collective-permute-done.6.b
  34.1 0.6 copy-done.26
  34.6 0.6 copy-done.27
  35.2 1.5 %shard_map.58.qa = bf16[128,576]{1,0:T(8,128)(2,1)} custom-call(bf16[32,576]{1,0:T(8,128)(2,1)} %copy-done.17, bf16[32,576]{1,0:T(8,128)(2,1)} %copy-done.27, bf16[32,576]{1,0:T(8,128)(2,1)} %copy-done.26, bf16[32,576]{1,0:T(8,128)(2,1)} %copy-done.25), custom_call_target="tpu_custom_call" | custom-call | tf_op jit(solution)/shard_map/pallas_call | solution.py:155
  36.7 1.5 %collective-permute-start.9 = (bf16[128,576]{1,0:T(8,128)(2,1)}, bf16[128,576]{1,0:T(8,128)(2,1)S(1)}, u32[]{:S(2)}, u32[]{:S(2)}) collective-permute-start(bf16[128,576]{1,0:T(8,128)(2,1)} %shard_map.58.qa), channel_id=1, source_target_pairs={{0,1},{1,2},{2,3},{3,0},{4,5},{5,6},{6,7},{7,4},{8,9},{9,10},{10,1... | collective-permute-start | bytes 442376 | tf_op jit(solution)/shard_map/ppermute | solution.py:38
  38.9 2.3 %collective-permute-start.15 = (bf16[2,8,64,128]{3,2,1,0:T(8,128)(2,1)}, bf16[2,8,64,128]{3,2,1,0:T(8,128)(2,1)S(1)}, u32[]{:S(2)}, u32[]{:S(2)}) collective-permute-start(bf16[2,8,64,128]{3,2,1,0:T(8,128)(2,1)} %shard_map.57.w0), channel_id=1, source_target_pairs={{0,96},{1,97},{2,98},{3,99},{4,100},{5,101},{6,102},{7,103},{8,104... | collective-permute-start | bytes 786440 | tf_op jit(solution)/shard_map/ppermute | solution.py:38
  41.2 1.7 %collective-permute-start.14 = (bf16[2,8,64,128]{3,2,1,0:T(8,128)(2,1)}, bf16[2,8,64,128]{3,2,1,0:T(8,128)(2,1)S(1)}, u32[]{:S(2)}, u32[]{:S(2)}) collective-permute-start(bf16[2,8,64,128]{3,2,1,0:T(8,128)(2,1)} %shard_map.57.w0), channel_id=1, source_target_pairs={{0,64},{1,65},{2,66},{3,67},{4,68},{5,69},{6,70},{7,71},{8,72},{9,... | collective-permute-start | bytes 786440 | tf_op jit(solution)/shard_map/ppermute | solution.py:38
  42.9 1.7 %collective-permute-start.12 = (bf16[128,576]{1,0:T(8,128)(2,1)}, bf16[128,576]{1,0:T(8,128)(2,1)S(1)}, u32[]{:S(2)}, u32[]{:S(2)}) collective-permute-start(bf16[128,576]{1,0:T(8,128)(2,1)} %shard_map.58.qa), channel_id=1, source_target_pairs={{0,3},{1,0},{2,1},{3,2},{4,7},{5,4},{6,5},{7,6},{8,11},{9,8},{10,9... | collective-permute-start | bytes 442376 | tf_op jit(solution)/shard_map/ppermute | solution.py:38
  44.7 0.0 collective-permute-done.9.qb
  44.7 1.8 %collective-permute-start.11 = (bf16[128,576]{1,0:T(8,128)(2,1)}, bf16[128,576]{1,0:T(8,128)(2,1)S(1)}, u32[]{:S(2)}, u32[]{:S(2)}) collective-permute-start(bf16[128,576]{1,0:T(8,128)(2,1)} %shard_map.58.qa), channel_id=1, source_target_pairs={{0,2},{1,3},{2,0},{3,1},{4,6},{5,7},{6,4},{7,5},{8,10},{9,11},{10,... | collective-permute-start | bytes 442376 | tf_op jit(solution)/shard_map/ppermute | solution.py:38
  46.5 0.9 %copy-done.2 = bf16[128,576]{1,0:T(8,128)(2,1)S(1)} copy-done((bf16[128,576]{1,0:T(8,128)(2,1)S(1)}, bf16[128,576]{1,0:T(8,128)(2,1)}, u32[]{:S(2)}) %copy-start.2) | copy-done | bytes 147480
  47.4 3.7 %copy-done.10 = bf16[576,8192]{1,0:T(8,128)(2,1)S(1)} copy-done((bf16[576,8192]{1,0:T(8,128)(2,1)S(1)}, bf16[576,8192]{1,0:T(8,128)(2,1)}, u32[]{:S(2)}) %copy-start.10) | copy-done | bytes 9437208
  51.1 6.8 %shard_map.59 = (bf16[128,640]{1,0:T(8,128)(2,1)S(1)}, bf16[128,640]{1,0:T(8,128)(2,1)S(1)}) custom-call(s32[1]{0:T(128)S(6)} %copy.6.length, bf16[128,576]{1,0:T(8,128)(2,1)S(1)} %copy-done.2, bf16[128,576]{1,0:T(8,128)(2,1)S(1)} %collective-permute-done.9.qb, bf16[576,8192]{1,0:T(8,128)(2,1)S(1)} %copy-done.10), custom_call_target="tpu_custom_call" | custom-call | flops 4563402752 | bytes 9437184 | tf_op jit(solution)/shard_map/pallas_call | solution.py:262
  57.9 0.7 copy-done.1
  58.6 0.0 collective-permute-done.12.qb
  58.6 1.4 %collective-permute-start.10 = (bf16[128,640]{1,0:T(8,128)(2,1)S(1)}, bf16[128,640]{1,0:T(8,128)(2,1)S(1)}, u32[]{:S(2)}, u32[]{:S(2)}) collective-permute-start(bf16[128,640]{1,0:T(8,128)(2,1)S(1)} %get-tuple-element.35), channel_id=1, source_target_pairs={{0,3},{1,0},{2,1},{3,2},{4,7},{5,4},{6,5},{7,6},{8,11},{9,8},{10,9... | collective-permute-start | bytes 491528 | tf_op jit(solution)/shard_map/ppermute | solution.py:38
  60.0 0.0 collective-permute-done.14.w2
  60.0 6.6 %shard_map.60 = (bf16[128,640]{1,0:T(8,128)(2,1)S(1)}, bf16[128,640]{1,0:T(8,128)(2,1)S(1)}) custom-call(s32[1]{0:T(128)S(6)} %copy.6.length, bf16[128,576]{1,0:T(8,128)(2,1)S(1)} %collective-permute-done.11.qa, bf16[128,576]{1,0:T(8,128)(2,1)S(1)} %collective-permute-done.12.qb, bf16[576,8192]{1,0:T(8,128)(2,1)S(1)} %copy-done.10), custom_call_target="tpu_custom_call" | custom-call | flops 4563402752 | bytes 9437184 | tf_op jit(solution)/shard_map/pallas_call | solution.py:262
  66.7 1.4 %collective-permute-start.16 = (bf16[128,640]{1,0:T(8,128)(2,1)S(1)}, bf16[128,640]{1,0:T(8,128)(2,1)S(1)}, u32[]{:S(2)}, u32[]{:S(2)}) collective-permute-start(bf16[128,640]{1,0:T(8,128)(2,1)S(1)} %get-tuple-element.39), channel_id=1, source_target_pairs={{0,2},{1,3},{2,0},{3,1},{4,6},{5,7},{6,4},{7,5},{8,10},{9,11},{10,... | collective-permute-start | bytes 491528 | tf_op jit(solution)/shard_map/ppermute | solution.py:38
  68.1 0.7 collective-permute-start.17
  68.8 4.9 %collective-permute-done.16.c = bf16[128,640]{1,0:T(8,128)(2,1)S(1)} collective-permute-done((bf16[128,640]{1,0:T(8,128)(2,1)S(1)}, bf16[128,640]{1,0:T(8,128)(2,1)S(1)}, u32[]{:S(2)}, u32[]{:S(2)}) %collective-permute-start.16) | collective-permute-done | bytes 163872 | tf_op jit(solution)/shard_map/ppermute | solution.py:38
  73.7 1.7 %collective-permute-done.17.d = bf16[128,640]{1,0:T(8,128)(2,1)S(1)} collective-permute-done((bf16[128,640]{1,0:T(8,128)(2,1)S(1)}, bf16[128,640]{1,0:T(8,128)(2,1)S(1)}, u32[]{:S(2)}, u32[]{:S(2)}) %collective-permute-start.17) | collective-permute-done | bytes 163872 | tf_op jit(solution)/shard_map/ppermute | solution.py:38
  75.4 0.7 copy-done.16
  76.0 2.1 %shard_map.61 = (bf16[32,640]{1,0:T(8,128)(2,1)}, bf16[32,640]{1,0:T(8,128)(2,1)}, bf16[32,640]{1,0:T(8,128)(2,1)}, bf16[32,640]{1,0:T(8,128)(2,1)}) custom-call(bf16[128,640]{1,0:T(8,128)(2,1)} %copy-done.1, bf16[128,640]{1,0:T(8,128)(2,1)} %copy-done.14, bf16[128,640]{1,0:T(8,128)(2,1)} %copy-done.15, bf16[128,640]{1,0:T(8,128)(2,1)} %copy-done.16), custom_call_target="tpu_custom_call" | custom-call | tf_op jit(solution)/shard_map/pallas_call | solution.py:294
  78.1 0.0 collective-permute-start.19
  78.1 2.0 %collective-permute-start.20 = (bf16[32,640]{1,0:T(8,128)(2,1)}, bf16[32,640]{1,0:T(8,128)(2,1)S(1)}, u32[]{:S(2)}, u32[]{:S(2)}) collective-permute-start(bf16[32,640]{1,0:T(8,128)(2,1)} %get-tuple-element.44), channel_id=1, source_target_pairs={{0,4},{1,5},{2,6},{3,7},{4,8},{5,9},{6,10},{7,11},{8,12},{9,13},{1... | collective-permute-start | bytes 122888 | tf_op jit(solution)/shard_map/ppermute | solution.py:38
  80.2 2.2 %collective-permute-done.18.b = bf16[32,640]{1,0:T(8,128)(2,1)S(1)} collective-permute-done((bf16[32,640]{1,0:T(8,128)(2,1)}, bf16[32,640]{1,0:T(8,128)(2,1)S(1)}, u32[]{:S(2)}, u32[]{:S(2)}) %collective-permute-start.18) | collective-permute-done | bytes 40992 | tf_op jit(solution)/shard_map/ppermute | solution.py:38
  82.3 1.5 %collective-permute-done.19.c = bf16[32,640]{1,0:T(8,128)(2,1)S(1)} collective-permute-done((bf16[32,640]{1,0:T(8,128)(2,1)}, bf16[32,640]{1,0:T(8,128)(2,1)S(1)}, u32[]{:S(2)}, u32[]{:S(2)}) %collective-permute-start.19) | collective-permute-done | bytes 40992 | tf_op jit(solution)/shard_map/ppermute | solution.py:38
  83.8 1.2 %collective-permute-done.20.d = bf16[32,640]{1,0:T(8,128)(2,1)S(1)} collective-permute-done((bf16[32,640]{1,0:T(8,128)(2,1)}, bf16[32,640]{1,0:T(8,128)(2,1)S(1)}, u32[]{:S(2)}, u32[]{:S(2)}) %collective-permute-start.20) | collective-permute-done | bytes 40992 | tf_op jit(solution)/shard_map/ppermute | solution.py:38
  85.0 0.6 copy-done.24
  85.6 2.4 %shard_map.62 = bf16[4,8,128]{2,1,0:T(8,128)(2,1)} custom-call(bf16[32,640]{1,0:T(8,128)(2,1)} %get-tuple-element.41.a, bf16[32,640]{1,0:T(8,128)(2,1)} %copy-done.22, bf16[32,640]{1,0:T(8,128)(2,1)} %copy-done.23, bf16[32,640]{1,0:T(8,128)(2,1)} %copy-done.24, bf16[2,8,64,128]{3,2,1,0:T(8,128)(2,1)} %shard_map.57.w0, bf16[2,8,64,128]{3,2,1,0:T(8,128)(2,1)} %copy-done.13, ...), custom_call_target="tpu_custom_call" | custom-call | tf_op jit(solution)/shard_map/pallas_call | solution.py:334
  (45 shorter events, 0.1 us)
Async XLA Ops:
  0.0 18.0 %collective-permute-start.3 = (bf16[8,64,128]{2,1,0:T(8,128)(2,1)}, bf16[8,64,128]{2,1,0:T(8,128)(2,1)S(1)}, u32[]{:S(2)}, u32[]{:S(2)}) collective-permute-start(bf16[8,64,128]{2,1,0:T(8,128)(2,1)} %bitcast.7), channel_id=1, source_target_pairs={{0,96},{1,97},{2,98},{3,99},{4,100},{5,101},{6,102},{7,103},{8,104... | collective-permute-start | bytes 393224 | tf_op jit(solution)/shard_map/ppermute | solution.py:38
  3.1 14.9 %collective-permute-start.2 = (bf16[8,64,128]{2,1,0:T(8,128)(2,1)}, bf16[8,64,128]{2,1,0:T(8,128)(2,1)S(1)}, u32[]{:S(2)}, u32[]{:S(2)}) collective-permute-start(bf16[8,64,128]{2,1,0:T(8,128)(2,1)} %bitcast.8), channel_id=1, source_target_pairs={{0,64},{1,65},{2,66},{3,67},{4,68},{5,69},{6,70},{7,71},{8,72},{9,... | collective-permute-start | bytes 393224 | tf_op jit(solution)/shard_map/ppermute | solution.py:38
  3.7 14.3 %collective-permute-start.1 = (bf16[8,64,128]{2,1,0:T(8,128)(2,1)}, bf16[8,64,128]{2,1,0:T(8,128)(2,1)S(1)}, u32[]{:S(2)}, u32[]{:S(2)}) collective-permute-start(bf16[8,64,128]{2,1,0:T(8,128)(2,1)} %bitcast.9), channel_id=1, source_target_pairs={{0,32},{1,33},{2,34},{3,35},{4,36},{5,37},{6,38},{7,39},{8,40},{9,... | collective-permute-start | bytes 393224 | tf_op jit(solution)/shard_map/ppermute | solution.py:38
  4.7 16.4 %collective-permute-start.5 = (bf16[8,64,128]{2,1,0:T(8,128)(2,1)}, bf16[8,64,128]{2,1,0:T(8,128)(2,1)S(1)}, u32[]{:S(2)}, u32[]{:S(2)}) collective-permute-start(bf16[8,64,128]{2,1,0:T(8,128)(2,1)} %value.1), channel_id=1, source_target_pairs={{0,16},{1,17},{2,18},{3,19},{4,20},{5,21},{6,22},{7,23},{8,24},{9,... | collective-permute-start | bytes 393224 | tf_op jit(solution)/shard_map/ppermute | solution.py:38
  4.7 13.3 %collective-permute-start = (bf16[4,8,192]{2,1,0:T(8,128)(2,1)}, bf16[4,8,192]{2,1,0:T(8,128)(2,1)S(1)}, u32[]{:S(2)}, u32[]{:S(2)}) collective-permute-start(bf16[4,8,192]{2,1,0:T(8,128)(2,1)} %bitcast.11), channel_id=1, source_target_pairs={{0,16},{1,17},{2,18},{3,19},{4,20},{5,21},{6,22},{7,23},{8,24},{9,... | collective-permute-start | bytes 36872 | tf_op jit(solution)/shard_map/ppermute | solution.py:38
  5.2 3.7 %copy-start = (bf16[1,8192,576]{1,2,0:T(8,128)(2,1)S(1)}, bf16[1,8192,576]{1,2,0:T(8,128)(2,1)}, u32[]{:S(2)}) copy-start(bf16[1,8192,576]{1,2,0:T(8,128)(2,1)} %param.6) | copy-start | bytes 28311556
  8.9 0.9 %copy-start.3 = (bf16[8,128,64]{1,2,0:T(8,128)(2,1)S(1)}, bf16[8,128,64]{1,2,0:T(8,128)(2,1)}, u32[]{:S(2)}) copy-start(bf16[8,128,64]{1,2,0:T(8,128)(2,1)} %param.8) | copy-start | bytes 393220
  9.8 0.9 %copy-start.4 = (bf16[8,64,128]{2,1,0:T(8,128)(2,1)S(1)}, bf16[8,64,128]{2,1,0:T(8,128)(2,1)}, u32[]{:S(2)}) copy-start(bf16[8,64,128]{2,1,0:T(8,128)(2,1)} %value.1) | copy-start | bytes 393220
  10.7 0.7 copy-start.7
  12.4 0.7 copy-start.5
  13.1 0.7 copy-start.6
  13.8 0.6 copy-start.8
  14.4 3.6 %copy-start.9 = (bf16[576,8192]{1,0:T(8,128)(2,1)}, bf16[576,8192]{1,0:T(8,128)(2,1)S(1)}, u32[]{:S(2)}) copy-start(bf16[576,8192]{1,0:T(8,128)(2,1)S(1)} %get-tuple-element.33.cache) | copy-start | bytes 28311556
  18.0 0.6 copy-start.28
  18.0 0.7 copy-start.18
  18.0 0.7 copy-start.19
  18.1 0.7 copy-start.20
  21.1 2.4 %collective-permute-start.4 = (bf16[32,576]{1,0:T(8,128)(2,1)}, bf16[32,576]{1,0:T(8,128)(2,1)S(1)}, u32[]{:S(2)}, u32[]{:S(2)}) collective-permute-start(bf16[32,576]{1,0:T(8,128)(2,1)} %get-tuple-element.30), channel_id=1, source_target_pairs={{0,16},{1,17},{2,18},{3,19},{4,20},{5,21},{6,22},{7,23},{8,24},{9,... | collective-permute-start | bytes 110600 | tf_op jit(solution)/shard_map/ppermute | solution.py:38
  21.1 0.7 copy-start.21
  24.3 9.8 %copy-start.17 = (bf16[32,576]{1,0:T(8,128)(2,1)}, bf16[32,576]{1,0:T(8,128)(2,1)S(1)}, u32[]{:S(2)}) copy-start(bf16[32,576]{1,0:T(8,128)(2,1)S(1)} %add.3.a) | copy-start | bytes 110596
  24.3 5.8 %collective-permute-start.8 = (bf16[32,576]{1,0:T(8,128)(2,1)S(1)}, bf16[32,576]{1,0:T(8,128)(2,1)S(1)}, u32[]{:S(2)}, u32[]{:S(2)}) collective-permute-start(bf16[32,576]{1,0:T(8,128)(2,1)S(1)} %add.3.a), channel_id=1, source_target_pairs={{0,12},{1,13},{2,14},{3,15},{4,0},{5,1},{6,2},{7,3},{8,4},{9,5},{1... | collective-permute-start | bytes 110600 | tf_op jit(solution)/shard_map/ppermute | solution.py:38
  28.4 5.6 %collective-permute-start.7 = (bf16[32,576]{1,0:T(8,128)(2,1)S(1)}, bf16[32,576]{1,0:T(8,128)(2,1)S(1)}, u32[]{:S(2)}, u32[]{:S(2)}) collective-permute-start(bf16[32,576]{1,0:T(8,128)(2,1)S(1)} %add.3.a), channel_id=1, source_target_pairs={{0,8},{1,9},{2,10},{3,11},{4,12},{5,13},{6,14},{7,15},{8,0},{9,1},... | collective-permute-start | bytes 110600 | tf_op jit(solution)/shard_map/ppermute | solution.py:38
  28.4 5.7 %collective-permute-start.6 = (bf16[32,576]{1,0:T(8,128)(2,1)S(1)}, bf16[32,576]{1,0:T(8,128)(2,1)S(1)}, u32[]{:S(2)}, u32[]{:S(2)}) collective-permute-start(bf16[32,576]{1,0:T(8,128)(2,1)S(1)} %add.3.a), channel_id=1, source_target_pairs={{0,4},{1,5},{2,6},{3,7},{4,8},{5,9},{6,10},{7,11},{8,12},{9,13},{1... | collective-permute-start | bytes 110600 | tf_op jit(solution)/shard_map/ppermute | solution.py:38
  30.1 4.0 %copy-start.25 = (bf16[32,576]{1,0:T(8,128)(2,1)}, bf16[32,576]{1,0:T(8,128)(2,1)S(1)}, u32[]{:S(2)}) copy-start(bf16[32,576]{1,0:T(8,128)(2,1)S(1)} %collective-permute-done.8.d) | copy-start | bytes 110596
  34.0 0.6 copy-start.26
  34.6 0.6 copy-start.27
  36.7 7.9 %collective-permute-start.9 = (bf16[128,576]{1,0:T(8,128)(2,1)}, bf16[128,576]{1,0:T(8,128)(2,1)S(1)}, u32[]{:S(2)}, u32[]{:S(2)}) collective-permute-start(bf16[128,576]{1,0:T(8,128)(2,1)} %shard_map.58.qa), channel_id=1, source_target_pairs={{0,1},{1,2},{2,3},{3,0},{4,5},{5,6},{6,7},{7,4},{8,9},{9,10},{10,1... | collective-permute-start | bytes 442376 | tf_op jit(solution)/shard_map/ppermute | solution.py:38
  38.9 21.1 %collective-permute-start.15 = (bf16[2,8,64,128]{3,2,1,0:T(8,128)(2,1)}, bf16[2,8,64,128]{3,2,1,0:T(8,128)(2,1)S(1)}, u32[]{:S(2)}, u32[]{:S(2)}) collective-permute-start(bf16[2,8,64,128]{3,2,1,0:T(8,128)(2,1)} %shard_map.57.w0), channel_id=1, source_target_pairs={{0,96},{1,97},{2,98},{3,99},{4,100},{5,101},{6,102},{7,103},{8,104... | collective-permute-start | bytes 786440 | tf_op jit(solution)/shard_map/ppermute | solution.py:38
  41.2 18.8 %collective-permute-start.14 = (bf16[2,8,64,128]{3,2,1,0:T(8,128)(2,1)}, bf16[2,8,64,128]{3,2,1,0:T(8,128)(2,1)S(1)}, u32[]{:S(2)}, u32[]{:S(2)}) collective-permute-start(bf16[2,8,64,128]{3,2,1,0:T(8,128)(2,1)} %shard_map.57.w0), channel_id=1, source_target_pairs={{0,64},{1,65},{2,66},{3,67},{4,68},{5,69},{6,70},{7,71},{8,72},{9,... | collective-permute-start | bytes 786440 | tf_op jit(solution)/shard_map/ppermute | solution.py:38
  42.9 17.1 %collective-permute-start.13 = (bf16[2,8,64,128]{3,2,1,0:T(8,128)(2,1)}, bf16[2,8,64,128]{3,2,1,0:T(8,128)(2,1)S(1)}, u32[]{:S(2)}, u32[]{:S(2)}) collective-permute-start(bf16[2,8,64,128]{3,2,1,0:T(8,128)(2,1)} %shard_map.57.w0), channel_id=1, source_target_pairs={{0,32},{1,33},{2,34},{3,35},{4,36},{5,37},{6,38},{7,39},{8,40},{9,... | collective-permute-start | bytes 786440 | tf_op jit(solution)/shard_map/ppermute | solution.py:38
  42.9 15.7 %collective-permute-start.12 = (bf16[128,576]{1,0:T(8,128)(2,1)}, bf16[128,576]{1,0:T(8,128)(2,1)S(1)}, u32[]{:S(2)}, u32[]{:S(2)}) collective-permute-start(bf16[128,576]{1,0:T(8,128)(2,1)} %shard_map.58.qa), channel_id=1, source_target_pairs={{0,3},{1,0},{2,1},{3,2},{4,7},{5,4},{6,5},{7,6},{8,11},{9,8},{10,9... | collective-permute-start | bytes 442376 | tf_op jit(solution)/shard_map/ppermute | solution.py:38
  44.7 15.3 %collective-permute-start.11 = (bf16[128,576]{1,0:T(8,128)(2,1)}, bf16[128,576]{1,0:T(8,128)(2,1)S(1)}, u32[]{:S(2)}, u32[]{:S(2)}) collective-permute-start(bf16[128,576]{1,0:T(8,128)(2,1)} %shard_map.58.qa), channel_id=1, source_target_pairs={{0,2},{1,3},{2,0},{3,1},{4,6},{5,7},{6,4},{7,5},{8,10},{9,11},{10,... | collective-permute-start | bytes 442376 | tf_op jit(solution)/shard_map/ppermute | solution.py:38
  46.5 0.9 %copy-start.2 = (bf16[128,576]{1,0:T(8,128)(2,1)S(1)}, bf16[128,576]{1,0:T(8,128)(2,1)}, u32[]{:S(2)}) copy-start(bf16[128,576]{1,0:T(8,128)(2,1)} %shard_map.58.qa) | copy-start | bytes 442372
  47.4 3.7 %copy-start.10 = (bf16[576,8192]{1,0:T(8,128)(2,1)S(1)}, bf16[576,8192]{1,0:T(8,128)(2,1)}, u32[]{:S(2)}) copy-start(bf16[576,8192]{1,0:T(8,128)(2,1)} %copy-done.9) | copy-start | bytes 28311556
  57.9 0.7 copy-start.1
  58.6 10.2 %collective-permute-start.10 = (bf16[128,640]{1,0:T(8,128)(2,1)S(1)}, bf16[128,640]{1,0:T(8,128)(2,1)S(1)}, u32[]{:S(2)}, u32[]{:S(2)}) collective-permute-start(bf16[128,640]{1,0:T(8,128)(2,1)S(1)} %get-tuple-element.35), channel_id=1, source_target_pairs={{0,3},{1,0},{2,1},{3,2},{4,7},{5,4},{6,5},{7,6},{8,11},{9,8},{10,9... | collective-permute-start | bytes 491528 | tf_op jit(solution)/shard_map/ppermute | solution.py:38
  60.0 25.0 %copy-start.11 = (bf16[2,8,64,128]{3,2,1,0:T(8,128)(2,1)}, bf16[2,8,64,128]{3,2,1,0:T(8,128)(2,1)S(1)}, u32[]{:S(2)}) copy-start(bf16[2,8,64,128]{3,2,1,0:T(8,128)(2,1)S(1)} %collective-permute-done.15.w3) | copy-start | bytes 786436
  60.0 25.0 %copy-start.12 = (bf16[2,8,64,128]{3,2,1,0:T(8,128)(2,1)}, bf16[2,8,64,128]{3,2,1,0:T(8,128)(2,1)S(1)}, u32[]{:S(2)}) copy-start(bf16[2,8,64,128]{3,2,1,0:T(8,128)(2,1)S(1)} %collective-permute-done.14.w2) | copy-start | bytes 786436
  60.0 25.0 %copy-start.13 = (bf16[2,8,64,128]{3,2,1,0:T(8,128)(2,1)}, bf16[2,8,64,128]{3,2,1,0:T(8,128)(2,1)S(1)}, u32[]{:S(2)}) copy-start(bf16[2,8,64,128]{3,2,1,0:T(8,128)(2,1)S(1)} %collective-permute-done.13.w1) | copy-start | bytes 786436
  66.7 7.0 %collective-permute-start.16 = (bf16[128,640]{1,0:T(8,128)(2,1)S(1)}, bf16[128,640]{1,0:T(8,128)(2,1)S(1)}, u32[]{:S(2)}, u32[]{:S(2)}) collective-permute-start(bf16[128,640]{1,0:T(8,128)(2,1)S(1)} %get-tuple-element.39), channel_id=1, source_target_pairs={{0,2},{1,3},{2,0},{3,1},{4,6},{5,7},{6,4},{7,5},{8,10},{9,11},{10,... | collective-permute-start | bytes 491528 | tf_op jit(solution)/shard_map/ppermute | solution.py:38
  68.1 7.3 %collective-permute-start.17 = (bf16[128,640]{1,0:T(8,128)(2,1)S(1)}, bf16[128,640]{1,0:T(8,128)(2,1)S(1)}, u32[]{:S(2)}, u32[]{:S(2)}) collective-permute-start(bf16[128,640]{1,0:T(8,128)(2,1)S(1)} %get-tuple-element.40), channel_id=1, source_target_pairs={{0,1},{1,2},{2,3},{3,0},{4,5},{5,6},{6,7},{7,4},{8,9},{9,10},{10,1... | collective-permute-start | bytes 491528 | tf_op jit(solution)/shard_map/ppermute | solution.py:38
  68.8 6.6 %copy-start.14 = (bf16[128,640]{1,0:T(8,128)(2,1)}, bf16[128,640]{1,0:T(8,128)(2,1)S(1)}, u32[]{:S(2)}) copy-start(bf16[128,640]{1,0:T(8,128)(2,1)S(1)} %collective-permute-done.10.b) | copy-start | bytes 491524
  73.7 1.7 %copy-start.15 = (bf16[128,640]{1,0:T(8,128)(2,1)}, bf16[128,640]{1,0:T(8,128)(2,1)S(1)}, u32[]{:S(2)}) copy-start(bf16[128,640]{1,0:T(8,128)(2,1)S(1)} %collective-permute-done.16.c) | copy-start | bytes 491524
  75.3 0.7 copy-start.16
  78.1 4.2 %collective-permute-start.18 = (bf16[32,640]{1,0:T(8,128)(2,1)}, bf16[32,640]{1,0:T(8,128)(2,1)S(1)}, u32[]{:S(2)}, u32[]{:S(2)}) collective-permute-start(bf16[32,640]{1,0:T(8,128)(2,1)} %get-tuple-element.42), channel_id=1, source_target_pairs={{0,12},{1,13},{2,14},{3,15},{4,0},{5,1},{6,2},{7,3},{8,4},{9,5},{1... | collective-permute-start | bytes 122888 | tf_op jit(solution)/shard_map/ppermute | solution.py:38
  78.1 5.7 %collective-permute-start.19 = (bf16[32,640]{1,0:T(8,128)(2,1)}, bf16[32,640]{1,0:T(8,128)(2,1)S(1)}, u32[]{:S(2)}, u32[]{:S(2)}) collective-permute-start(bf16[32,640]{1,0:T(8,128)(2,1)} %get-tuple-element.43), channel_id=1, source_target_pairs={{0,8},{1,9},{2,10},{3,11},{4,12},{5,13},{6,14},{7,15},{8,0},{9,1},... | collective-permute-start | bytes 122888 | tf_op jit(solution)/shard_map/ppermute | solution.py:38
  78.1 6.9 %collective-permute-start.20 = (bf16[32,640]{1,0:T(8,128)(2,1)}, bf16[32,640]{1,0:T(8,128)(2,1)S(1)}, u32[]{:S(2)}, u32[]{:S(2)}) collective-permute-start(bf16[32,640]{1,0:T(8,128)(2,1)} %get-tuple-element.44), channel_id=1, source_target_pairs={{0,4},{1,5},{2,6},{3,7},{4,8},{5,9},{6,10},{7,11},{8,12},{9,13},{1... | collective-permute-start | bytes 122888 | tf_op jit(solution)/shard_map/ppermute | solution.py:38
  82.3 2.7 %copy-start.22 = (bf16[32,640]{1,0:T(8,128)(2,1)}, bf16[32,640]{1,0:T(8,128)(2,1)S(1)}, u32[]{:S(2)}) copy-start(bf16[32,640]{1,0:T(8,128)(2,1)S(1)} %collective-permute-done.18.b) | copy-start | bytes 122884
  83.8 1.2 %copy-start.23 = (bf16[32,640]{1,0:T(8,128)(2,1)}, bf16[32,640]{1,0:T(8,128)(2,1)S(1)}, u32[]{:S(2)}) copy-start(bf16[32,640]{1,0:T(8,128)(2,1)S(1)} %collective-permute-done.19.c) | copy-start | bytes 122884
  85.0 0.6 copy-start.24

commit v3 on v2

--- a/solution.py
+++ b/solution.py
@@ -19,8 +19,8 @@
 TO_LOG2 = (NOPE + ROPE) ** (-0.5) * 1.4426950408889634
 
 VMEM = pl.BlockSpec(memory_space=pltpu.VMEM)
-HBM = pl.BlockSpec(memory_space=pltpu.HBM)
 SMEM = pl.BlockSpec(memory_space=pltpu.SMEM)
+SMALL = pltpu.CompilerParams(vmem_limit_bytes=4 * 2**20)
 BF16 = jnp.bfloat16
 F32 = jnp.float32
 
@@ -44,6 +44,11 @@
 
 def y_shift(value, hops):
     return exchange(value, lambda y, core, z, x: (y + hops, core, z, x))
+
+
+def y_owners():
+    y = lax.axis_index("roll") // CORES
+    return [lax.rem(y + RING - hops, RING) for hops in range(RING)]
 
 
 def first_shift(value, hops):
@@ -88,9 +93,10 @@
     return columns, top, total
 
 
-def load_kernel(cache, block, query, value, *refs):
-    sources, targets, sems = (cache, block, query, value), refs[:4], refs[4]
-    copies = [pltpu.make_async_copy(a, b, sems.at[i]) for i, (a, b) in enumerate(zip(sources, targets))]
+def load_kernel(*refs):
+    count = len(refs) // 2
+    sems = refs[-1]
+    copies = [pltpu.make_async_copy(refs[i], refs[count + i], sems.at[i]) for i in range(count)]
     for copy in copies:
         copy.start()
     for copy in copies:
@@ -101,23 +107,22 @@
     return pl.pallas_call(
         load_kernel,
         out_shape=[jax.ShapeDtypeStruct(a.shape, a.dtype) for a in arrays],
-        in_specs=[HBM] * 4,
-        out_specs=[VMEM] * 4,
-        scratch_shapes=[pltpu.SemaphoreType.DMA((4,))],
-        compiler_params=pltpu.CompilerParams(vmem_limit_bytes=16 * 2**20),
+        in_specs=[pl.BlockSpec(memory_space=pltpu.HBM)] * len(arrays),
+        out_specs=[VMEM] * len(arrays),
+        scratch_shapes=[pltpu.SemaphoreType.DMA((len(arrays),))],
+        compiler_params=SMALL,
         cost_estimate=pl.CostEstimate(
             flops=0, bytes_accessed=2 * sum(a.size * 2 for a in arrays), transcendentals=0
         ),
-    )(*arrays)
+    )(*[pltpu.with_memory_space_constraint(a, pltpu.HBM) for a in arrays])
 
 
 def absorb_kernel(mine, other, kw0, kw1, kw2, kw3, out_mine, out_other, weights):
-    roll = lax.axis_index("roll")
-    y, core = roll // CORES, lax.rem(roll, CORES)
+    core = lax.rem(lax.axis_index("roll"), CORES)
     frames, heads, _ = mine.shape
     weights[...] = jnp.zeros_like(weights)
-    for hops, block in enumerate((kw0, kw1, kw2, kw3)):
-        chunk = lax.rem(y + RING - hops, RING) * CORES + core
+    for owner, block in zip(y_owners(), (kw0, kw1, kw2, kw3)):
+        chunk = owner * CORES + core
         weights[:, pl.ds(pl.multiple_of(chunk * 64, 64), 64), :] = block[...]
     absorbed = []
     for h in range(heads):
@@ -141,23 +146,26 @@
         in_specs=[VMEM] * 6,
         out_specs=[VMEM, VMEM],
         scratch_shapes=[pltpu.VMEM((heads, LATENT, NOPE), BF16)],
+        compiler_params=SMALL,
     )(mine, other, *blocks)
 
 
-def stack_kernel(a, b, c, d, out):
-    rows = a.shape[0]
-    for at, block in enumerate((a, b, c, d)):
-        out[at * rows : (at + 1) * rows, :] = block[...]
-
-
-def stack(blocks):
-    rows, width = blocks[0].shape
+def stack_kernel(*refs):
+    parts, out = refs[:-1], refs[-1]
+    rows = parts[0].shape[0]
+    for at, part in enumerate(parts):
+        out[at * rows : (at + 1) * rows, :] = part[...]
+
+
+def stack(parts):
+    rows, width = parts[0].shape
     return pl.pallas_call(
         stack_kernel,
-        out_shape=jax.ShapeDtypeStruct((4 * rows, width), BF16),
-        in_specs=[VMEM] * 4,
+        out_shape=jax.ShapeDtypeStruct((len(parts) * rows, width), BF16),
+        in_specs=[VMEM] * len(parts),
         out_specs=VMEM,
-    )(*blocks)
+        compiler_params=SMALL,
+    )(*parts)
 
 
 def fold(op, value):
@@ -167,13 +175,16 @@
     return so_far
 
 
-def attend_kernel(length, qa, qb, cache, oa, ob, query, scores, tops, totals, acc, *, block):
+def attend_kernel(length, cache, *refs, block):
+    count = (len(refs) - 5) // 2
+    parts, outs = refs[:count], refs[count : 2 * count]
+    query, scores, tops, totals, acc = refs[2 * count :]
     span = cache.shape[1]
     blocks = span // block
     live = jnp.clip(length[0] - lax.axis_index("seq") * span, 0, span)
-    group = qa.shape[0]
-    query[:group, :] = qa[...]
-    query[group:, :] = qb[...]
+    group = parts[0].shape[0]
+    for at, part in enumerate(parts):
+        query[at * group : (at + 1) * group, :] = part[...]
 
     def here(i):
         return pl.ds(i * block if isinstance(i, int) else pl.multiple_of(i * block, block), block)
@@ -195,7 +206,7 @@
         high, low = two_terms(top)
         sent = high + low
         stats = pack_stats(sent, total * jnp.exp2(top - sent))
-        for at, out in enumerate((oa, ob)):
+        for at, out in enumerate(outs):
             rows = slice(at * group, (at + 1) * group)
             for column in range(0, LATENT, 128):
                 lanes = slice(column, column + 128)
@@ -261,9 +272,9 @@
     rows, span = group * len(parts), cache.shape[1]
     return pl.pallas_call(
         functools.partial(attend_kernel, block=block),
-        out_shape=[jax.ShapeDtypeStruct((group, PAYLOAD), BF16)] * 2,
-        in_specs=[SMEM] + [VMEM] * 3,
-        out_specs=[VMEM] * 2,
+        out_shape=[jax.ShapeDtypeStruct((group, PAYLOAD), BF16)] * len(parts),
+        in_specs=[SMEM] + [VMEM] * (1 + len(parts)),
+        out_specs=[VMEM] * len(parts),
         scratch_shapes=[
             pltpu.VMEM((rows, WIDTH), BF16),
             pltpu.VMEM((rows, span), F32),
@@ -275,27 +286,29 @@
         cost_estimate=pl.CostEstimate(
             flops=2 * rows * span * (WIDTH + LATENT), bytes_accessed=span * WIDTH * 2, transcendentals=rows * span
         ),
-    )(length, *parts, cache)
-
-
-def merge_kernel(a, b, c, d, oa, ob, oc, od):
-    columns, top, total = merge([a, b, c, d])
+    )(length, cache, *parts)
+
+
+def merge_kernel(*refs):
+    parts, outs = refs[:RING], refs[RING:]
+    columns, top, total = merge(parts)
     stats = pack_stats(top, total)
-    rows = oa.shape[0]
-    for at, part in enumerate((oa, ob, oc, od)):
+    rows = outs[0].shape[0]
+    for at, out in enumerate(outs):
         here = slice(at * rows, (at + 1) * rows)
         for j, column in enumerate(columns):
-            part[:, j * 128 : (j + 1) * 128] = column[here].astype(BF16)
-        part[:, LATENT:] = stats[here]
+            out[:, j * 128 : (j + 1) * 128] = column[here].astype(BF16)
+        out[:, LATENT:] = stats[here]
 
 
 def merge_groups(parts):
     rows, width = parts[0].shape
     return pl.pallas_call(
         merge_kernel,
-        out_shape=[jax.ShapeDtypeStruct((rows // 4, width), BF16)] * 4,
-        in_specs=[VMEM] * 4,
-        out_specs=[VMEM] * 4,
+        out_shape=[jax.ShapeDtypeStruct((rows // RING, width), BF16)] * RING,
+        in_specs=[VMEM] * RING,
+        out_specs=[VMEM] * RING,
+        compiler_params=SMALL,
     )(*parts)
 
 
@@ -311,15 +324,14 @@
         out_shape=jax.ShapeDtypeStruct((CORES,) + mine.shape, BF16),
         in_specs=[VMEM, VMEM],
         out_specs=VMEM,
+        compiler_params=SMALL,
     )(mine, other)
 
 
 def finish_kernel(a, b, c, d, w0, w1, w2, w3, out, context, weight):
-    y = lax.axis_index("roll") // CORES
-    for hops, block in enumerate((w0, w1, w2, w3)):
-        chunk = lax.rem(y + RING - hops, RING) * CORES
+    for owner, block in zip(y_owners(), (w0, w1, w2, w3)):
         for core in range(CORES):
-            weight[:, pl.ds(pl.multiple_of((chunk + core) * 64, 64), 64), :] = block[core]
+            weight[:, pl.ds(pl.multiple_of((owner * CORES + core) * 64, 64), 64), :] = block[core]
     for j, column in enumerate(merge([a, b, c, d])[0]):
         context[:, j * 128 : (j + 1) * 128] = column.astype(BF16)
     frames, heads, _ = out.shape
@@ -340,6 +352,7 @@
             pltpu.VMEM((frames * heads, LATENT), BF16),
             pltpu.VMEM((heads, LATENT, vhead), BF16),
         ],
+        compiler_params=SMALL,
     )(*parts, *weights)
 
 
@@ -361,12 +374,13 @@
     groups = [near] + [second_shift(near, hops) for hops in (1, 2, 3)]
     value_pairs = [value_pair] + [y_shift(value_pair, hops) for hops in (1, 2, 3)]
 
-    early = attend(lengths, groups[:2], cache)
+    one, three = attend(lengths, [groups[1], groups[3]], cache)
     groups, value_pairs = lax.optimization_barrier((groups, value_pairs))
-    late = attend(lengths, groups[2:], cache)
-    parts = list(early) + list(late)
-
-    near = merge_groups([parts[0]] + [second_shift(parts[hops], -hops) for hops in (1, 2, 3)])
+    (two,) = attend(lengths, [groups[2]], cache)
+    (zero,) = attend(lengths, [groups[0]], cache)
+    parts = [zero] + [second_shift(part, -hops) for hops, part in ((1, one), (2, two), (3, three))]
+
+    near = merge_groups(parts)
     last = [near[0]] + [first_shift(near[hops], -hops) for hops in (1, 2, 3)]
     return finish(last, value_pairs, frames)[None]
 

time: 88.5 us -> 64.4 us (0.73)
  the two profiles are of different devices: /device:TPU:0 before, /device:TPU:18 now
where the time goes in v3:
time: 64.4 us; the launch traced here: 63.1 us
  starting transfers between devices  27.7 us (43%)
  Pallas kernels  22.4 us (35%)
  waiting for transfers between devices  12.2 us (19%)
  between operations  0.78 us (1%)
    ppermute x21, starting transfers between devices, exchange(): return lax.ppermute(value, ('roll', 'seq'), pairs)  27.7 us
    pallas_call x3, Pallas kernels, attend(): pl.pallas_call(functools.partial(attend_kernel, block=block), out_shape=[...  16.7 us
    ppermute x21, waiting for transfers between devices, exchange(): return lax.ppermute(value, ('roll', 'seq'), pairs)  12.2 us
    pallas_call x1, Pallas kernels, load(): pl.pallas_call(load_kernel, out_shape=[jax.ShapeDtypeStruct(a.shape, a.dt...  3.72 us
  transfers between devices with their start and end apart: 21, of which 9 were waited for; matrix products, arithmetic and copies ran while one was open for 0% of the time, Pallas kernels for 33%

profile of v3, /device:TPU:18, one launch (start us, length us, event | category | flops | bytes accessed | tf_op | source)
XLA Modules:
  0.0 63.1 jit_solution(15486355664264526871)
XLA Ops:
  0.0 0.4 collective-permute-start.3
  0.5 2.9 %collective-permute-start.2 = (bf16[8,64,128]{2,1,0:T(8,128)(2,1)}, bf16[8,64,128]{2,1,0:T(8,128)(2,1)S(1)}, u32[]{:S(2)}, u32[]{:S(2)}) collective-permute-start(bf16[8,64,128]{2,1,0:T(8,128)(2,1)} %bitcast.8), channel_id=1, source_target_pairs={{0,64},{1,65},{2,66},{3,67},{4,68},{5,69},{6,70},{7,71},{8,72},{9,... | collective-permute-start | bytes 393224 | tf_op jit(solution)/shard_map/ppermute | solution.py:38
  3.4 0.0 collective-permute-start.1
  3.4 0.0 collective-permute-start.5
  3.4 0.5 collective-permute-start
  3.9 3.7 %shard_map.55 = (bf16[576,8192]{1,0:T(8,128)(2,1)S(1)}, bf16[8,64,128]{2,1,0:T(8,128)(2,1)S(1)}, bf16[4,8,192]{2,1,0:T(8,128)(2,1)S(1)}, bf16[8,64,128]{2,1,0:T(8,128)(2,1)S(1)}) custom-call(bf16[576,8192]{1,0:T(8,128)(2,1)} %bitcast.6, bf16[8,64,128]{2,1,0:T(8,128)(2,1)} %bitcast.10, bf16[4,8,192]{2,1,0:T(8,128)(2,1)} %bitcast.12, bf16[8,64,128]{2,1,0:T(8,128)(2,1)} %refs_3_.1), custom_call_target="tpu_custom_call" | custom-call | bytes 19423232 | tf_op jit(solution)/shard_map/pallas_call | solution.py:107
  7.6 0.0 collective-permute-done.other
  7.6 0.0 collective-permute-done.3.kw3
  7.6 0.9 %collective-permute-done.2.kw2 = bf16[8,64,128]{2,1,0:T(8,128)(2,1)S(1)} collective-permute-done((bf16[8,64,128]{2,1,0:T(8,128)(2,1)}, bf16[8,64,128]{2,1,0:T(8,128)(2,1)S(1)}, u32[]{:S(2)}, u32[]{:S(2)}) %collective-permute-start.2) | collective-permute-done | bytes 131104 | tf_op jit(solution)/shard_map/ppermute | solution.py:38
  8.5 1.4 %collective-permute-done.1.kw1 = bf16[8,64,128]{2,1,0:T(8,128)(2,1)S(1)} collective-permute-done((bf16[8,64,128]{2,1,0:T(8,128)(2,1)}, bf16[8,64,128]{2,1,0:T(8,128)(2,1)S(1)}, u32[]{:S(2)}, u32[]{:S(2)}) %collective-permute-start.1) | collective-permute-done | bytes 131104 | tf_op jit(solution)/shard_map/ppermute | solution.py:38
  9.9 0.5 shard_map.56
  10.5 0.0 collective-permute-start.4
  10.5 0.0 collective-permute-done.5.other
  10.6 1.2 %collective-permute-done.4 = bf16[32,576]{1,0:T(8,128)(2,1)S(1)} collective-permute-done((bf16[32,576]{1,0:T(8,128)(2,1)S(1)}, bf16[32,576]{1,0:T(8,128)(2,1)S(1)}, u32[]{:S(2)}, u32[]{:S(2)}) %collective-permute-start.4) | collective-permute-done | bytes 36896 | tf_op jit(solution)/shard_map/ppermute | solution.py:38
  11.8 4.1 %collective-permute-start.8 = (bf16[32,576]{1,0:T(8,128)(2,1)S(1)}, bf16[32,576]{1,0:T(8,128)(2,1)S(1)}, u32[]{:S(2)}, u32[]{:S(2)}) collective-permute-start(bf16[32,576]{1,0:T(8,128)(2,1)S(1)} %add.3.refs_0_), channel_id=1, source_target_pairs={{0,12},{1,13},{2,14},{3,15},{4,0},{5,1},{6,2},{7,3},{8,4},{9,5},{1... | collective-permute-start | bytes 110600 | tf_op jit(solution)/shard_map/ppermute | solution.py:38
  15.9 0.0 collective-permute-start.7
  15.9 1.3 %collective-permute-start.6 = (bf16[32,576]{1,0:T(8,128)(2,1)S(1)}, bf16[32,576]{1,0:T(8,128)(2,1)S(1)}, u32[]{:S(2)}, u32[]{:S(2)}) collective-permute-start(bf16[32,576]{1,0:T(8,128)(2,1)S(1)} %add.3.refs_0_), channel_id=1, source_target_pairs={{0,4},{1,5},{2,6},{3,7},{4,8},{5,9},{6,10},{7,11},{8,12},{9,13},{1... | collective-permute-start | bytes 110600 | tf_op jit(solution)/shard_map/ppermute | solution.py:38
  17.1 0.4 collective-permute-done.8.refs_3_
  17.5 3.9 %collective-permute-done.7.refs_2_ = bf16[32,576]{1,0:T(8,128)(2,1)S(1)} collective-permute-done((bf16[32,576]{1,0:T(8,128)(2,1)S(1)}, bf16[32,576]{1,0:T(8,128)(2,1)S(1)}, u32[]{:S(2)}, u32[]{:S(2)}) %collective-permute-start.7) | collective-permute-done | bytes 36896 | tf_op jit(solution)/shard_map/ppermute | solution.py:38
  21.5 0.0 collective-permute-done.6.refs_1_
  21.5 0.6 collective-permute-start.11
  22.1 1.5 %collective-permute-start.9 = (bf16[128,576]{1,0:T(8,128)(2,1)S(1)}, bf16[128,576]{1,0:T(8,128)(2,1)S(1)}, u32[]{:S(2)}, u32[]{:S(2)}) collective-permute-start(bf16[128,576]{1,0:T(8,128)(2,1)S(1)} %shard_map.58.refs_0_), channel_id=1, source_target_pairs={{0,1},{1,2},{2,3},{3,0},{4,5},{5,6},{6,7},{7,4},{8,9},{9,10},{10,1... | collective-permute-start | bytes 442376 | tf_op jit(solution)/shard_map/ppermute | solution.py:38
  24.3 0.6 %collective-permute-start.14 = (bf16[2,8,64,128]{3,2,1,0:T(8,128)(2,1)S(1)}, bf16[2,8,64,128]{3,2,1,0:T(8,128)(2,1)S(1)}, u32[]{:S(2)}, u32[]{:S(2)}) collective-permute-start(bf16[2,8,64,128]{3,2,1,0:T(8,128)(2,1)S(1)} %shard_map.57.w0), channel_id=1, source_target_pairs={{0,96},{1,97},{2,98},{3,99},{4,100},{5,101},{6,102},{7,103},{8,104... | collective-permute-start | bytes 786440 | tf_op jit(solution)/shard_map/ppermute | solution.py:38
  24.9 2.9 %collective-permute-start.13 = (bf16[2,8,64,128]{3,2,1,0:T(8,128)(2,1)S(1)}, bf16[2,8,64,128]{3,2,1,0:T(8,128)(2,1)S(1)}, u32[]{:S(2)}, u32[]{:S(2)}) collective-permute-start(bf16[2,8,64,128]{3,2,1,0:T(8,128)(2,1)S(1)} %shard_map.57.w0), channel_id=1, source_target_pairs={{0,64},{1,65},{2,66},{3,67},{4,68},{5,69},{6,70},{7,71},{8,72},{9,... | collective-permute-start | bytes 786440 | tf_op jit(solution)/shard_map/ppermute | solution.py:38
  27.8 2.1 %collective-permute-start.12 = (bf16[2,8,64,128]{3,2,1,0:T(8,128)(2,1)S(1)}, bf16[2,8,64,128]{3,2,1,0:T(8,128)(2,1)S(1)}, u32[]{:S(2)}, u32[]{:S(2)}) collective-permute-start(bf16[2,8,64,128]{3,2,1,0:T(8,128)(2,1)S(1)} %shard_map.57.w0), channel_id=1, source_target_pairs={{0,32},{1,33},{2,34},{3,35},{4,36},{5,37},{6,38},{7,39},{8,40},{9,... | collective-permute-start | bytes 786440 | tf_op jit(solution)/shard_map/ppermute | solution.py:38
  29.9 0.0 collective-permute-done.11.refs_1_
  29.9 3.3 %collective-permute-start.10 = (bf16[128,576]{1,0:T(8,128)(2,1)S(1)}, bf16[128,576]{1,0:T(8,128)(2,1)S(1)}, u32[]{:S(2)}, u32[]{:S(2)}) collective-permute-start(bf16[128,576]{1,0:T(8,128)(2,1)S(1)} %shard_map.58.refs_0_), channel_id=1, source_target_pairs={{0,2},{1,3},{2,0},{3,1},{4,6},{5,7},{6,4},{7,5},{8,10},{9,11},{10,... | collective-permute-start | bytes 442376 | tf_op jit(solution)/shard_map/ppermute | solution.py:38
  33.2 0.0 collective-permute-done.9.refs_0_
  33.2 6.8 %shard_map.60 = (bf16[128,640]{1,0:T(8,128)(2,1)S(1)}, bf16[128,640]{1,0:T(8,128)(2,1)S(1)}) custom-call(s32[1]{0:T(128)S(6)} %copy.6.length, bf16[576,8192]{1,0:T(8,128)(2,1)S(1)} %get-tuple-element.25.cache, bf16[128,576]{1,0:T(8,128)(2,1)S(1)} %collective-permute-done.9.refs_0_, bf16[128,576]{1,0:T(8,128)(2,1)S(1)} %collective-permute-done.11.refs_1_), custom_call_target="tpu_custom_call" | custom-call | flops 4563402752 | bytes 9437184 | tf_op jit(solution)/shard_map/pallas_call | solution.py:273
  40.0 0.3 collective-permute-start.15
  40.3 0.0 collective-permute-done.10.refs_0_
  40.3 1.8 %collective-permute-start.17 = (bf16[128,640]{1,0:T(8,128)(2,1)S(1)}, bf16[128,640]{1,0:T(8,128)(2,1)S(1)}, u32[]{:S(2)}, u32[]{:S(2)}) collective-permute-start(bf16[128,640]{1,0:T(8,128)(2,1)S(1)} %get-tuple-element.36), channel_id=1, source_target_pairs={{0,1},{1,2},{2,3},{3,0},{4,5},{5,6},{6,7},{7,4},{8,9},{9,10},{10,1... | collective-permute-start | bytes 491528 | tf_op jit(solution)/shard_map/ppermute | solution.py:38
  42.1 0.0 collective-permute-done.14.w3
  42.1 0.0 collective-permute-done.13.w2
  42.2 0.0 collective-permute-done.12.w1
  42.2 4.9 %shard_map.61 = bf16[128,640]{1,0:T(8,128)(2,1)S(1)} custom-call(s32[1]{0:T(128)S(6)} %copy.6.length, bf16[576,8192]{1,0:T(8,128)(2,1)S(1)} %get-tuple-element.25.cache, bf16[128,576]{1,0:T(8,128)(2,1)S(1)} %collective-permute-done.10.refs_0_), custom_call_target="tpu_custom_call" | custom-call | flops 2281701376 | bytes 9437184 | tf_op jit(solution)/shard_map/pallas_call | solution.py:273
  47.1 1.5 %collective-permute-start.16 = (bf16[128,640]{1,0:T(8,128)(2,1)S(1)}, bf16[128,640]{1,0:T(8,128)(2,1)S(1)}, u32[]{:S(2)}, u32[]{:S(2)}) collective-permute-start(bf16[128,640]{1,0:T(8,128)(2,1)S(1)} %shard_map.61), channel_id=1, source_target_pairs={{0,2},{1,3},{2,0},{3,1},{4,6},{5,7},{6,4},{7,5},{8,10},{9,11},{10,... | collective-permute-start | bytes 491528 | tf_op jit(solution)/shard_map/ppermute | solution.py:38
  48.6 4.9 %shard_map.59.refs_0_ = bf16[128,640]{1,0:T(8,128)(2,1)S(1)} custom-call(s32[1]{0:T(128)S(6)} %copy.6.length, bf16[576,8192]{1,0:T(8,128)(2,1)S(1)} %get-tuple-element.25.cache, bf16[128,576]{1,0:T(8,128)(2,1)S(1)} %shard_map.58.refs_0_), custom_call_target="tpu_custom_call" | custom-call | flops 2281701376 | bytes 9437184 | tf_op jit(solution)/shard_map/pallas_call | solution.py:273
  53.5 0.0 collective-permute-done.15.refs_1_
  53.5 0.0 collective-permute-done.17.refs_3_
  53.5 0.4 collective-permute-done.16.refs_2_
  54.0 0.3 shard_map.62
  54.3 0.1 collective-permute-start.18
  54.4 2.4 %collective-permute-start.19 = (bf16[32,640]{1,0:T(8,128)(2,1)S(1)}, bf16[32,640]{1,0:T(8,128)(2,1)S(1)}, u32[]{:S(2)}, u32[]{:S(2)}) collective-permute-start(bf16[32,640]{1,0:T(8,128)(2,1)S(1)} %get-tuple-element.39), channel_id=1, source_target_pairs={{0,8},{1,9},{2,10},{3,11},{4,12},{5,13},{6,14},{7,15},{8,0},{9,1},... | collective-permute-start | bytes 122888 | tf_op jit(solution)/shard_map/ppermute | solution.py:38
  56.8 1.3 %collective-permute-start.20 = (bf16[32,640]{1,0:T(8,128)(2,1)S(1)}, bf16[32,640]{1,0:T(8,128)(2,1)S(1)}, u32[]{:S(2)}, u32[]{:S(2)}) collective-permute-start(bf16[32,640]{1,0:T(8,128)(2,1)S(1)} %get-tuple-element.40), channel_id=1, source_target_pairs={{0,4},{1,5},{2,6},{3,7},{4,8},{5,9},{6,10},{7,11},{8,12},{9,13},{1... | collective-permute-start | bytes 122888 | tf_op jit(solution)/shard_map/ppermute | solution.py:38
  58.2 0.3 collective-permute-done.18.b
  58.4 1.6 %collective-permute-done.19.c = bf16[32,640]{1,0:T(8,128)(2,1)S(1)} collective-permute-done((bf16[32,640]{1,0:T(8,128)(2,1)S(1)}, bf16[32,640]{1,0:T(8,128)(2,1)S(1)}, u32[]{:S(2)}, u32[]{:S(2)}) %collective-permute-start.19) | collective-permute-done | bytes 40992 | tf_op jit(solution)/shard_map/ppermute | solution.py:38
  60.0 2.0 %collective-permute-done.20.d = bf16[32,640]{1,0:T(8,128)(2,1)S(1)} collective-permute-done((bf16[32,640]{1,0:T(8,128)(2,1)S(1)}, bf16[32,640]{1,0:T(8,128)(2,1)S(1)}, u32[]{:S(2)}, u32[]{:S(2)}) %collective-permute-start.20) | collective-permute-done | bytes 40992 | tf_op jit(solution)/shard_map/ppermute | solution.py:38
  62.0 1.1 %shard_map.63 = bf16[4,8,128]{2,1,0:T(8,128)(2,1)} custom-call(bf16[32,640]{1,0:T(8,128)(2,1)S(1)} %get-tuple-element.37.a, bf16[32,640]{1,0:T(8,128)(2,1)S(1)} %collective-permute-done.18.b, bf16[32,640]{1,0:T(8,128)(2,1)S(1)} %collective-permute-done.19.c, bf16[32,640]{1,0:T(8,128)(2,1)S(1)} %collective-permute-done.20.d, ...), custom_call_target="tpu_custom_call" | custom-call | tf_op jit(solution)/shard_map/pallas_call | solution.py:346
  (3 shorter events, 0.1 us)
Async XLA Ops:
  0.0 7.6 %collective-permute-start.3 = (bf16[8,64,128]{2,1,0:T(8,128)(2,1)}, bf16[8,64,128]{2,1,0:T(8,128)(2,1)S(1)}, u32[]{:S(2)}, u32[]{:S(2)}) collective-permute-start(bf16[8,64,128]{2,1,0:T(8,128)(2,1)} %bitcast.7), channel_id=1, source_target_pairs={{0,96},{1,97},{2,98},{3,99},{4,100},{5,101},{6,102},{7,103},{8,104... | collective-permute-start | bytes 393224 | tf_op jit(solution)/shard_map/ppermute | solution.py:38
  0.5 8.1 %collective-permute-start.2 = (bf16[8,64,128]{2,1,0:T(8,128)(2,1)}, bf16[8,64,128]{2,1,0:T(8,128)(2,1)S(1)}, u32[]{:S(2)}, u32[]{:S(2)}) collective-permute-start(bf16[8,64,128]{2,1,0:T(8,128)(2,1)} %bitcast.8), channel_id=1, source_target_pairs={{0,64},{1,65},{2,66},{3,67},{4,68},{5,69},{6,70},{7,71},{8,72},{9,... | collective-permute-start | bytes 393224 | tf_op jit(solution)/shard_map/ppermute | solution.py:38
  3.4 6.6 %collective-permute-start.1 = (bf16[8,64,128]{2,1,0:T(8,128)(2,1)}, bf16[8,64,128]{2,1,0:T(8,128)(2,1)S(1)}, u32[]{:S(2)}, u32[]{:S(2)}) collective-permute-start(bf16[8,64,128]{2,1,0:T(8,128)(2,1)} %bitcast.9), channel_id=1, source_target_pairs={{0,32},{1,33},{2,34},{3,35},{4,36},{5,37},{6,38},{7,39},{8,40},{9,... | collective-permute-start | bytes 393224 | tf_op jit(solution)/shard_map/ppermute | solution.py:38
  3.4 7.2 %collective-permute-start.5 = (bf16[8,64,128]{2,1,0:T(8,128)(2,1)}, bf16[8,64,128]{2,1,0:T(8,128)(2,1)S(1)}, u32[]{:S(2)}, u32[]{:S(2)}) collective-permute-start(bf16[8,64,128]{2,1,0:T(8,128)(2,1)} %refs_3_.1), channel_id=1, source_target_pairs={{0,16},{1,17},{2,18},{3,19},{4,20},{5,21},{6,22},{7,23},{8,24},{9,... | collective-permute-start | bytes 393224 | tf_op jit(solution)/shard_map/ppermute | solution.py:38
  3.4 4.2 %collective-permute-start = (bf16[4,8,192]{2,1,0:T(8,128)(2,1)}, bf16[4,8,192]{2,1,0:T(8,128)(2,1)S(1)}, u32[]{:S(2)}, u32[]{:S(2)}) collective-permute-start(bf16[4,8,192]{2,1,0:T(8,128)(2,1)} %bitcast.11), channel_id=1, source_target_pairs={{0,16},{1,17},{2,18},{3,19},{4,20},{5,21},{6,22},{7,23},{8,24},{9,... | collective-permute-start | bytes 36872 | tf_op jit(solution)/shard_map/ppermute | solution.py:38
  10.5 1.3 %collective-permute-start.4 = (bf16[32,576]{1,0:T(8,128)(2,1)S(1)}, bf16[32,576]{1,0:T(8,128)(2,1)S(1)}, u32[]{:S(2)}, u32[]{:S(2)}) collective-permute-start(bf16[32,576]{1,0:T(8,128)(2,1)S(1)} %get-tuple-element.29), channel_id=1, source_target_pairs={{0,16},{1,17},{2,18},{3,19},{4,20},{5,21},{6,22},{7,23},{8,24},{9,... | collective-permute-start | bytes 110600 | tf_op jit(solution)/shard_map/ppermute | solution.py:38
  11.8 5.8 %collective-permute-start.8 = (bf16[32,576]{1,0:T(8,128)(2,1)S(1)}, bf16[32,576]{1,0:T(8,128)(2,1)S(1)}, u32[]{:S(2)}, u32[]{:S(2)}) collective-permute-start(bf16[32,576]{1,0:T(8,128)(2,1)S(1)} %add.3.refs_0_), channel_id=1, source_target_pairs={{0,12},{1,13},{2,14},{3,15},{4,0},{5,1},{6,2},{7,3},{8,4},{9,5},{1... | collective-permute-start | bytes 110600 | tf_op jit(solution)/shard_map/ppermute | solution.py:38
  15.9 5.6 %collective-permute-start.7 = (bf16[32,576]{1,0:T(8,128)(2,1)S(1)}, bf16[32,576]{1,0:T(8,128)(2,1)S(1)}, u32[]{:S(2)}, u32[]{:S(2)}) collective-permute-start(bf16[32,576]{1,0:T(8,128)(2,1)S(1)} %add.3.refs_0_), channel_id=1, source_target_pairs={{0,8},{1,9},{2,10},{3,11},{4,12},{5,13},{6,14},{7,15},{8,0},{9,1},... | collective-permute-start | bytes 110600 | tf_op jit(solution)/shard_map/ppermute | solution.py:38
  15.9 5.7 %collective-permute-start.6 = (bf16[32,576]{1,0:T(8,128)(2,1)S(1)}, bf16[32,576]{1,0:T(8,128)(2,1)S(1)}, u32[]{:S(2)}, u32[]{:S(2)}) collective-permute-start(bf16[32,576]{1,0:T(8,128)(2,1)S(1)} %add.3.refs_0_), channel_id=1, source_target_pairs={{0,4},{1,5},{2,6},{3,7},{4,8},{5,9},{6,10},{7,11},{8,12},{9,13},{1... | collective-permute-start | bytes 110600 | tf_op jit(solution)/shard_map/ppermute | solution.py:38
  21.5 8.4 %collective-permute-start.11 = (bf16[128,576]{1,0:T(8,128)(2,1)S(1)}, bf16[128,576]{1,0:T(8,128)(2,1)S(1)}, u32[]{:S(2)}, u32[]{:S(2)}) collective-permute-start(bf16[128,576]{1,0:T(8,128)(2,1)S(1)} %shard_map.58.refs_0_), channel_id=1, source_target_pairs={{0,3},{1,0},{2,1},{3,2},{4,7},{5,4},{6,5},{7,6},{8,11},{9,8},{10,9... | collective-permute-start | bytes 442376 | tf_op jit(solution)/shard_map/ppermute | solution.py:38
  22.1 11.1 %collective-permute-start.9 = (bf16[128,576]{1,0:T(8,128)(2,1)S(1)}, bf16[128,576]{1,0:T(8,128)(2,1)S(1)}, u32[]{:S(2)}, u32[]{:S(2)}) collective-permute-start(bf16[128,576]{1,0:T(8,128)(2,1)S(1)} %shard_map.58.refs_0_), channel_id=1, source_target_pairs={{0,1},{1,2},{2,3},{3,0},{4,5},{5,6},{6,7},{7,4},{8,9},{9,10},{10,1... | collective-permute-start | bytes 442376 | tf_op jit(solution)/shard_map/ppermute | solution.py:38
  24.3 17.9 %collective-permute-start.14 = (bf16[2,8,64,128]{3,2,1,0:T(8,128)(2,1)S(1)}, bf16[2,8,64,128]{3,2,1,0:T(8,128)(2,1)S(1)}, u32[]{:S(2)}, u32[]{:S(2)}) collective-permute-start(bf16[2,8,64,128]{3,2,1,0:T(8,128)(2,1)S(1)} %shard_map.57.w0), channel_id=1, source_target_pairs={{0,96},{1,97},{2,98},{3,99},{4,100},{5,101},{6,102},{7,103},{8,104... | collective-permute-start | bytes 786440 | tf_op jit(solution)/shard_map/ppermute | solution.py:38
  24.9 17.2 %collective-permute-start.13 = (bf16[2,8,64,128]{3,2,1,0:T(8,128)(2,1)S(1)}, bf16[2,8,64,128]{3,2,1,0:T(8,128)(2,1)S(1)}, u32[]{:S(2)}, u32[]{:S(2)}) collective-permute-start(bf16[2,8,64,128]{3,2,1,0:T(8,128)(2,1)S(1)} %shard_map.57.w0), channel_id=1, source_target_pairs={{0,64},{1,65},{2,66},{3,67},{4,68},{5,69},{6,70},{7,71},{8,72},{9,... | collective-permute-start | bytes 786440 | tf_op jit(solution)/shard_map/ppermute | solution.py:38
  27.8 14.3 %collective-permute-start.12 = (bf16[2,8,64,128]{3,2,1,0:T(8,128)(2,1)S(1)}, bf16[2,8,64,128]{3,2,1,0:T(8,128)(2,1)S(1)}, u32[]{:S(2)}, u32[]{:S(2)}) collective-permute-start(bf16[2,8,64,128]{3,2,1,0:T(8,128)(2,1)S(1)} %shard_map.57.w0), channel_id=1, source_target_pairs={{0,32},{1,33},{2,34},{3,35},{4,36},{5,37},{6,38},{7,39},{8,40},{9,... | collective-permute-start | bytes 786440 | tf_op jit(solution)/shard_map/ppermute | solution.py:38
  29.9 10.5 %collective-permute-start.10 = (bf16[128,576]{1,0:T(8,128)(2,1)S(1)}, bf16[128,576]{1,0:T(8,128)(2,1)S(1)}, u32[]{:S(2)}, u32[]{:S(2)}) collective-permute-start(bf16[128,576]{1,0:T(8,128)(2,1)S(1)} %shard_map.58.refs_0_), channel_id=1, source_target_pairs={{0,2},{1,3},{2,0},{3,1},{4,6},{5,7},{6,4},{7,5},{8,10},{9,11},{10,... | collective-permute-start | bytes 442376 | tf_op jit(solution)/shard_map/ppermute | solution.py:38
  40.0 13.5 %collective-permute-start.15 = (bf16[128,640]{1,0:T(8,128)(2,1)S(1)}, bf16[128,640]{1,0:T(8,128)(2,1)S(1)}, u32[]{:S(2)}, u32[]{:S(2)}) collective-permute-start(bf16[128,640]{1,0:T(8,128)(2,1)S(1)} %get-tuple-element.34), channel_id=1, source_target_pairs={{0,3},{1,0},{2,1},{3,2},{4,7},{5,4},{6,5},{7,6},{8,11},{9,8},{10,9... | collective-permute-start | bytes 491528 | tf_op jit(solution)/shard_map/ppermute | solution.py:38
  40.3 13.2 %collective-permute-start.17 = (bf16[128,640]{1,0:T(8,128)(2,1)S(1)}, bf16[128,640]{1,0:T(8,128)(2,1)S(1)}, u32[]{:S(2)}, u32[]{:S(2)}) collective-permute-start(bf16[128,640]{1,0:T(8,128)(2,1)S(1)} %get-tuple-element.36), channel_id=1, source_target_pairs={{0,1},{1,2},{2,3},{3,0},{4,5},{5,6},{6,7},{7,4},{8,9},{9,10},{10,1... | collective-permute-start | bytes 491528 | tf_op jit(solution)/shard_map/ppermute | solution.py:38
  47.1 6.9 %collective-permute-start.16 = (bf16[128,640]{1,0:T(8,128)(2,1)S(1)}, bf16[128,640]{1,0:T(8,128)(2,1)S(1)}, u32[]{:S(2)}, u32[]{:S(2)}) collective-permute-start(bf16[128,640]{1,0:T(8,128)(2,1)S(1)} %shard_map.61), channel_id=1, source_target_pairs={{0,2},{1,3},{2,0},{3,1},{4,6},{5,7},{6,4},{7,5},{8,10},{9,11},{10,... | collective-permute-start | bytes 491528 | tf_op jit(solution)/shard_map/ppermute | solution.py:38
  54.3 4.1 %collective-permute-start.18 = (bf16[32,640]{1,0:T(8,128)(2,1)S(1)}, bf16[32,640]{1,0:T(8,128)(2,1)S(1)}, u32[]{:S(2)}, u32[]{:S(2)}) collective-permute-start(bf16[32,640]{1,0:T(8,128)(2,1)S(1)} %get-tuple-element.38), channel_id=1, source_target_pairs={{0,12},{1,13},{2,14},{3,15},{4,0},{5,1},{6,2},{7,3},{8,4},{9,5},{1... | collective-permute-start | bytes 122888 | tf_op jit(solution)/shard_map/ppermute | solution.py:38
  54.4 5.6 %collective-permute-start.19 = (bf16[32,640]{1,0:T(8,128)(2,1)S(1)}, bf16[32,640]{1,0:T(8,128)(2,1)S(1)}, u32[]{:S(2)}, u32[]{:S(2)}) collective-permute-start(bf16[32,640]{1,0:T(8,128)(2,1)S(1)} %get-tuple-element.39), channel_id=1, source_target_pairs={{0,8},{1,9},{2,10},{3,11},{4,12},{5,13},{6,14},{7,15},{8,0},{9,1},... | collective-permute-start | bytes 122888 | tf_op jit(solution)/shard_map/ppermute | solution.py:38
  56.8 5.2 %collective-permute-start.20 = (bf16[32,640]{1,0:T(8,128)(2,1)S(1)}, bf16[32,640]{1,0:T(8,128)(2,1)S(1)}, u32[]{:S(2)}, u32[]{:S(2)}) collective-permute-start(bf16[32,640]{1,0:T(8,128)(2,1)S(1)} %get-tuple-element.40), channel_id=1, source_target_pairs={{0,4},{1,5},{2,6},{3,7},{4,8},{5,9},{6,10},{7,11},{8,12},{9,13},{1... | collective-permute-start | bytes 122888 | tf_op jit(solution)/shard_map/ppermute | solution.py:38

commit v4 on v3

--- a/solution.py
+++ b/solution.py
@@ -15,7 +15,7 @@
 RING = 4
 CORES = 2
 
-MASKED = -1e30
+MASKED = -(2.0**100)
 TO_LOG2 = (NOPE + ROPE) ** (-0.5) * 1.4426950408889634
 
 VMEM = pl.BlockSpec(memory_space=pltpu.VMEM)
@@ -216,13 +216,15 @@
     def scaled(value, factor):
         return jnp.concatenate([value[:, at : at + 128] * factor for at in range(0, LATENT, 128)], axis=1)
 
-    @pl.when(live >= span)
-    def _():
+    def one_pass(masked):
         scores[:, here(0)] = score(0)
         for i in range(blocks):
             s = scores[:, here(i % 2)]
             if i + 1 < blocks:
                 scores[:, here((i + 1) % 2)] = score(i + 1)
+            if masked:
+                column = lax.broadcasted_iota(jnp.int32, s.shape, 1)
+                s = jnp.where(column < live - i * block, s, MASKED)
             block_top = largest(fold(jnp.maximum, s)) * TO_LOG2
             top = block_top if i == 0 else jnp.maximum(tops[...], block_top)
             p = jnp.exp2(s * TO_LOG2 - top[:, :1])
@@ -236,35 +238,19 @@
             tops[...] = top
         finish(tops[...])
 
-    @pl.when(live < span)
+    @pl.when(live >= span)
     def _():
-        whole = live // block
-        some = (live + block - 1) // block
-        tops[...] = jnp.full(tops.shape, MASKED, F32)
+        one_pass(False)
+
+    @pl.when((live > 0) & (live < span))
+    def _():
+        one_pass(True)
+
+    @pl.when(live <= 0)
+    def _():
         totals[...] = jnp.zeros(totals.shape, F32)
         acc[...] = jnp.zeros(acc.shape, F32)
-
-        def fill(i, masked):
-            s = score(i)
-            if masked:
-                s = jnp.where(i * block + lax.broadcasted_iota(jnp.int32, s.shape, 1) < live, s, MASKED)
-            scores[:, here(i)] = s
-            tops[...] = jnp.maximum(tops[...], fold(jnp.maximum, s))
-
-        def loop(first, last, body):
-            lax.fori_loop(first, last, lambda i, c: (body(i), c)[1], 0)
-
-        loop(0, whole, lambda i: fill(i, False))
-        loop(whole, some, lambda i: fill(i, True))
-        top = largest(tops[...]) * TO_LOG2
-
-        def add(i):
-            p = jnp.exp2(scores[:, here(i)] * TO_LOG2 - top[:, :1])
-            totals[...] += fold(jnp.add, p)
-            acc[...] += weigh(i, p)
-
-        loop(0, some, add)
-        finish(top)
+        finish(jnp.full(tops.shape, MASKED, F32))
 
 
 def attend(length, parts, cache, block=1024):
@@ -277,12 +263,12 @@
         out_specs=[VMEM] * len(parts),
         scratch_shapes=[
             pltpu.VMEM((rows, WIDTH), BF16),
-            pltpu.VMEM((rows, span), F32),
+            pltpu.VMEM((rows, 2 * block), F32),
             pltpu.VMEM((rows, 128), F32),
             pltpu.VMEM((rows, 128), F32),
             pltpu.VMEM((rows, LATENT), F32),
         ],
-        compiler_params=pltpu.CompilerParams(vmem_limit_bytes=24 * 2**20),
+        compiler_params=pltpu.CompilerParams(vmem_limit_bytes=16 * 2**20),
         cost_estimate=pl.CostEstimate(
             flops=2 * rows * span * (WIDTH + LATENT), bytes_accessed=span * WIDTH * 2, transcendentals=rows * span
         ),
@@ -374,11 +360,10 @@
     groups = [near] + [second_shift(near, hops) for hops in (1, 2, 3)]
     value_pairs = [value_pair] + [y_shift(value_pair, hops) for hops in (1, 2, 3)]
 
-    one, three = attend(lengths, [groups[1], groups[3]], cache)
+    away = attend(lengths, groups[1:], cache)
     groups, value_pairs = lax.optimization_barrier((groups, value_pairs))
-    (two,) = attend(lengths, [groups[2]], cache)
-    (zero,) = attend(lengths, [groups[0]], cache)
-    parts = [zero] + [second_shift(part, -hops) for hops, part in ((1, one), (2, two), (3, three))]
+    (zero,) = attend(lengths, groups[:1], cache)
+    parts = [zero] + [second_shift(part, -hops) for hops, part in enumerate(away, 1)]
 
     near = merge_groups(parts)
     last = [near[0]] + [first_shift(near[hops], -hops) for hops in (1, 2, 3)]

time: 64.4 us -> 63 us (0.978)
  the two profiles are of different devices: /device:TPU:18 before, /device:TPU:0 now
where the time goes in v4:
time: 63 us; the launch traced here: 62.6 us
  Pallas kernels  21 us (33%)
  starting transfers between devices  20.6 us (33%)
  waiting for transfers between devices  20.2 us (32%)
  between operations  0.78 us (1%)
    ppermute x21, starting transfers between devices, exchange(): return lax.ppermute(value, ('roll', 'seq'), pairs)  20.6 us
    ppermute x21, waiting for transfers between devices, exchange(): return lax.ppermute(value, ('roll', 'seq'), pairs)  20.2 us
    pallas_call x2, Pallas kernels, attend(): pl.pallas_call(functools.partial(attend_kernel, block=block), out_shape=[...  15.3 us
    pallas_call x1, Pallas kernels, load(): pl.pallas_call(load_kernel, out_shape=[jax.ShapeDtypeStruct(a.shape, a.dt...  3.72 us
  transfers between devices with their start and end apart: 21, of which 12 were waited for; matrix products, arithmetic and copies ran while one was open for 0% of the time, Pallas kernels for 31%

profile of v4, /device:TPU:0, one launch (start us, length us, event | category | flops | bytes accessed | tf_op | source)
XLA Modules:
  0.0 62.6 jit_solution(11455142549664318952)
XLA Ops:
  0.0 3.1 %collective-permute-start.3 = (bf16[8,64,128]{2,1,0:T(8,128)(2,1)}, bf16[8,64,128]{2,1,0:T(8,128)(2,1)S(1)}, u32[]{:S(2)}, u32[]{:S(2)}) collective-permute-start(bf16[8,64,128]{2,1,0:T(8,128)(2,1)} %bitcast.7), channel_id=1, source_target_pairs={{0,96},{1,97},{2,98},{3,99},{4,100},{5,101},{6,102},{7,103},{8,104... | collective-permute-start | bytes 393224 | tf_op jit(solution)/shard_map/ppermute | solution.py:38
  3.1 0.6 %collective-permute-start.2 = (bf16[8,64,128]{2,1,0:T(8,128)(2,1)}, bf16[8,64,128]{2,1,0:T(8,128)(2,1)S(1)}, u32[]{:S(2)}, u32[]{:S(2)}) collective-permute-start(bf16[8,64,128]{2,1,0:T(8,128)(2,1)} %bitcast.8), channel_id=1, source_target_pairs={{0,64},{1,65},{2,66},{3,67},{4,68},{5,69},{6,70},{7,71},{8,72},{9,... | collective-permute-start | bytes 393224 | tf_op jit(solution)/shard_map/ppermute | solution.py:38
  3.7 1.0 %collective-permute-start.1 = (bf16[8,64,128]{2,1,0:T(8,128)(2,1)}, bf16[8,64,128]{2,1,0:T(8,128)(2,1)S(1)}, u32[]{:S(2)}, u32[]{:S(2)}) collective-permute-start(bf16[8,64,128]{2,1,0:T(8,128)(2,1)} %bitcast.9), channel_id=1, source_target_pairs={{0,32},{1,33},{2,34},{3,35},{4,36},{5,37},{6,38},{7,39},{8,40},{9,... | collective-permute-start | bytes 393224 | tf_op jit(solution)/shard_map/ppermute | solution.py:38
  4.7 0.0 collective-permute-start.5
  4.7 0.5 collective-permute-start
  5.2 3.7 %shard_map.55 = (bf16[576,8192]{1,0:T(8,128)(2,1)S(1)}, bf16[8,64,128]{2,1,0:T(8,128)(2,1)S(1)}, bf16[4,8,192]{2,1,0:T(8,128)(2,1)S(1)}, bf16[8,64,128]{2,1,0:T(8,128)(2,1)S(1)}) custom-call(bf16[576,8192]{1,0:T(8,128)(2,1)} %bitcast.6, bf16[8,64,128]{2,1,0:T(8,128)(2,1)} %bitcast.10, bf16[4,8,192]{2,1,0:T(8,128)(2,1)} %bitcast.12, bf16[8,64,128]{2,1,0:T(8,128)(2,1)} %refs_3_.1), custom_call_target="tpu_custom_call" | custom-call | bytes 19423232 | tf_op jit(solution)/shard_map/pallas_call | solution.py:107
  8.9 0.0 collective-permute-done.other
  8.9 0.0 collective-permute-done.3.kw3
  9.0 2.2 %collective-permute-done.2.kw2 = bf16[8,64,128]{2,1,0:T(8,128)(2,1)S(1)} collective-permute-done((bf16[8,64,128]{2,1,0:T(8,128)(2,1)}, bf16[8,64,128]{2,1,0:T(8,128)(2,1)S(1)}, u32[]{:S(2)}, u32[]{:S(2)}) %collective-permute-start.2) | collective-permute-done | bytes 131104 | tf_op jit(solution)/shard_map/ppermute | solution.py:38
  11.2 1.4 %collective-permute-done.1.kw1 = bf16[8,64,128]{2,1,0:T(8,128)(2,1)S(1)} collective-permute-done((bf16[8,64,128]{2,1,0:T(8,128)(2,1)}, bf16[8,64,128]{2,1,0:T(8,128)(2,1)S(1)}, u32[]{:S(2)}, u32[]{:S(2)}) %collective-permute-start.1) | collective-permute-done | bytes 131104 | tf_op jit(solution)/shard_map/ppermute | solution.py:38
  12.6 0.5 shard_map.56
  13.1 0.0 collective-permute-start.4
  13.2 0.0 collective-permute-done.5.other
  13.2 1.2 %collective-permute-done.4 = bf16[32,576]{1,0:T(8,128)(2,1)S(1)} collective-permute-done((bf16[32,576]{1,0:T(8,128)(2,1)S(1)}, bf16[32,576]{1,0:T(8,128)(2,1)S(1)}, u32[]{:S(2)}, u32[]{:S(2)}) %collective-permute-start.4) | collective-permute-done | bytes 36896 | tf_op jit(solution)/shard_map/ppermute | solution.py:38
  14.4 4.1 %collective-permute-start.8 = (bf16[32,576]{1,0:T(8,128)(2,1)S(1)}, bf16[32,576]{1,0:T(8,128)(2,1)S(1)}, u32[]{:S(2)}, u32[]{:S(2)}) collective-permute-start(bf16[32,576]{1,0:T(8,128)(2,1)S(1)} %add.3.refs_0_), channel_id=1, source_target_pairs={{0,12},{1,13},{2,14},{3,15},{4,0},{5,1},{6,2},{7,3},{8,4},{9,5},{1... | collective-permute-start | bytes 110600 | tf_op jit(solution)/shard_map/ppermute | solution.py:38
  18.5 0.0 collective-permute-start.7
  18.5 1.3 %collective-permute-start.6 = (bf16[32,576]{1,0:T(8,128)(2,1)S(1)}, bf16[32,576]{1,0:T(8,128)(2,1)S(1)}, u32[]{:S(2)}, u32[]{:S(2)}) collective-permute-start(bf16[32,576]{1,0:T(8,128)(2,1)S(1)} %add.3.refs_0_), channel_id=1, source_target_pairs={{0,4},{1,5},{2,6},{3,7},{4,8},{5,9},{6,10},{7,11},{8,12},{9,13},{1... | collective-permute-start | bytes 110600 | tf_op jit(solution)/shard_map/ppermute | solution.py:38
  19.8 0.4 collective-permute-done.8.refs_3_
  20.2 3.9 %collective-permute-done.7.refs_2_ = bf16[32,576]{1,0:T(8,128)(2,1)S(1)} collective-permute-done((bf16[32,576]{1,0:T(8,128)(2,1)S(1)}, bf16[32,576]{1,0:T(8,128)(2,1)S(1)}, u32[]{:S(2)}, u32[]{:S(2)}) %collective-permute-start.7) | collective-permute-done | bytes 36896 | tf_op jit(solution)/shard_map/ppermute | solution.py:38
  24.1 0.0 collective-permute-done.6.refs_1_
  24.2 2.8 %collective-permute-start.11 = (bf16[128,576]{1,0:T(8,128)(2,1)S(1)}, bf16[128,576]{1,0:T(8,128)(2,1)S(1)}, u32[]{:S(2)}, u32[]{:S(2)}) collective-permute-start(bf16[128,576]{1,0:T(8,128)(2,1)S(1)} %shard_map.58.refs_0_), channel_id=1, source_target_pairs={{0,3},{1,0},{2,1},{3,2},{4,7},{5,4},{6,5},{7,6},{8,11},{9,8},{10,9... | collective-permute-start | bytes 442376 | tf_op jit(solution)/shard_map/ppermute | solution.py:38
  27.0 0.8 %collective-permute-start.10 = (bf16[128,576]{1,0:T(8,128)(2,1)S(1)}, bf16[128,576]{1,0:T(8,128)(2,1)S(1)}, u32[]{:S(2)}, u32[]{:S(2)}) collective-permute-start(bf16[128,576]{1,0:T(8,128)(2,1)S(1)} %shard_map.58.refs_0_), channel_id=1, source_target_pairs={{0,2},{1,3},{2,0},{3,1},{4,6},{5,7},{6,4},{7,5},{8,10},{9,11},{10,... | collective-permute-start | bytes 442376 | tf_op jit(solution)/shard_map/ppermute | solution.py:38
  27.8 0.9 %collective-permute-start.9 = (bf16[128,576]{1,0:T(8,128)(2,1)S(1)}, bf16[128,576]{1,0:T(8,128)(2,1)S(1)}, u32[]{:S(2)}, u32[]{:S(2)}) collective-permute-start(bf16[128,576]{1,0:T(8,128)(2,1)S(1)} %shard_map.58.refs_0_), channel_id=1, source_target_pairs={{0,1},{1,2},{2,3},{3,0},{4,5},{5,6},{6,7},{7,4},{8,9},{9,10},{10,1... | collective-permute-start | bytes 442376 | tf_op jit(solution)/shard_map/ppermute | solution.py:38
  29.3 0.6 %collective-permute-start.14 = (bf16[2,8,64,128]{3,2,1,0:T(8,128)(2,1)S(1)}, bf16[2,8,64,128]{3,2,1,0:T(8,128)(2,1)S(1)}, u32[]{:S(2)}, u32[]{:S(2)}) collective-permute-start(bf16[2,8,64,128]{3,2,1,0:T(8,128)(2,1)S(1)} %shard_map.57.w0), channel_id=1, source_target_pairs={{0,96},{1,97},{2,98},{3,99},{4,100},{5,101},{6,102},{7,103},{8,104... | collective-permute-start | bytes 786440 | tf_op jit(solution)/shard_map/ppermute | solution.py:38
  30.0 0.6 %collective-permute-start.13 = (bf16[2,8,64,128]{3,2,1,0:T(8,128)(2,1)S(1)}, bf16[2,8,64,128]{3,2,1,0:T(8,128)(2,1)S(1)}, u32[]{:S(2)}, u32[]{:S(2)}) collective-permute-start(bf16[2,8,64,128]{3,2,1,0:T(8,128)(2,1)S(1)} %shard_map.57.w0), channel_id=1, source_target_pairs={{0,64},{1,65},{2,66},{3,67},{4,68},{5,69},{6,70},{7,71},{8,72},{9,... | collective-permute-start | bytes 786440 | tf_op jit(solution)/shard_map/ppermute | solution.py:38
  30.6 1.0 %collective-permute-done.11.refs_2_ = bf16[128,576]{1,0:T(8,128)(2,1)S(1)} collective-permute-done((bf16[128,576]{1,0:T(8,128)(2,1)S(1)}, bf16[128,576]{1,0:T(8,128)(2,1)S(1)}, u32[]{:S(2)}, u32[]{:S(2)}) %collective-permute-start.11) | collective-permute-done | bytes 147488 | tf_op jit(solution)/shard_map/ppermute | solution.py:38
  31.6 0.0 collective-permute-start.12
  31.6 2.3 %collective-permute-done.10.refs_1_ = bf16[128,576]{1,0:T(8,128)(2,1)S(1)} collective-permute-done((bf16[128,576]{1,0:T(8,128)(2,1)S(1)}, bf16[128,576]{1,0:T(8,128)(2,1)S(1)}, u32[]{:S(2)}, u32[]{:S(2)}) %collective-permute-start.10) | collective-permute-done | bytes 147488 | tf_op jit(solution)/shard_map/ppermute | solution.py:38
  33.9 1.7 %collective-permute-done.9.refs_0_ = bf16[128,576]{1,0:T(8,128)(2,1)S(1)} collective-permute-done((bf16[128,576]{1,0:T(8,128)(2,1)S(1)}, bf16[128,576]{1,0:T(8,128)(2,1)S(1)}, u32[]{:S(2)}, u32[]{:S(2)}) %collective-permute-start.9) | collective-permute-done | bytes 147488 | tf_op jit(solution)/shard_map/ppermute | solution.py:38
  35.6 10.1 %shard_map.60 = (bf16[128,640]{1,0:T(8,128)(2,1)S(1)}, bf16[128,640]{1,0:T(8,128)(2,1)S(1)}, bf16[128,640]{1,0:T(8,128)(2,1)S(1)}) custom-call(s32[1]{0:T(128)S(6)} %copy.6.length, bf16[576,8192]{1,0:T(8,128)(2,1)S(1)} %get-tuple-element.25.cache, bf16[128,576]{1,0:T(8,128)(2,1)S(1)} %collective-permute-done.9.refs_0_, ...), custom_call_target="tpu_custom_call" | custom-call | flops 6845104128 | bytes 9437184 | tf_op jit(solution)/shard_map/pallas_call | solution.py:259
  45.7 0.1 collective-permute-start.15
  45.8 1.4 %collective-permute-start.16 = (bf16[128,640]{1,0:T(8,128)(2,1)S(1)}, bf16[128,640]{1,0:T(8,128)(2,1)S(1)}, u32[]{:S(2)}, u32[]{:S(2)}) collective-permute-start(bf16[128,640]{1,0:T(8,128)(2,1)S(1)} %get-tuple-element.35), channel_id=1, source_target_pairs={{0,2},{1,3},{2,0},{3,1},{4,6},{5,7},{6,4},{7,5},{8,10},{9,11},{10,... | collective-permute-start | bytes 491528 | tf_op jit(solution)/shard_map/ppermute | solution.py:38
  47.1 0.0 collective-permute-done.14.w3
  47.1 0.7 %collective-permute-start.17 = (bf16[128,640]{1,0:T(8,128)(2,1)S(1)}, bf16[128,640]{1,0:T(8,128)(2,1)S(1)}, u32[]{:S(2)}, u32[]{:S(2)}) collective-permute-start(bf16[128,640]{1,0:T(8,128)(2,1)S(1)} %get-tuple-element.36), channel_id=1, source_target_pairs={{0,1},{1,2},{2,3},{3,0},{4,5},{5,6},{6,7},{7,4},{8,9},{9,10},{10,1... | collective-permute-start | bytes 491528 | tf_op jit(solution)/shard_map/ppermute | solution.py:38
  47.8 0.0 collective-permute-done.13.w2
  47.8 0.0 collective-permute-done.12.w1
  47.8 5.2 %shard_map.59.refs_0_ = bf16[128,640]{1,0:T(8,128)(2,1)S(1)} custom-call(s32[1]{0:T(128)S(6)} %copy.6.length, bf16[576,8192]{1,0:T(8,128)(2,1)S(1)} %get-tuple-element.25.cache, bf16[128,576]{1,0:T(8,128)(2,1)S(1)} %shard_map.58.refs_0_), custom_call_target="tpu_custom_call" | custom-call | flops 2281701376 | bytes 9437184 | tf_op jit(solution)/shard_map/pallas_call | solution.py:259
  53.0 0.0 collective-permute-done.15.refs_1_
  53.0 0.0 collective-permute-done.16.refs_2_
  53.0 1.4 %collective-permute-done.17.refs_3_ = bf16[128,640]{1,0:T(8,128)(2,1)S(1)} collective-permute-done((bf16[128,640]{1,0:T(8,128)(2,1)S(1)}, bf16[128,640]{1,0:T(8,128)(2,1)S(1)}, u32[]{:S(2)}, u32[]{:S(2)}) %collective-permute-start.17) | collective-permute-done | bytes 163872 | tf_op jit(solution)/shard_map/ppermute | solution.py:38
  54.4 0.3 shard_map.61
  54.8 0.1 collective-permute-start.18
  54.9 0.1 collective-permute-start.19
  54.9 1.9 %collective-permute-start.20 = (bf16[32,640]{1,0:T(8,128)(2,1)S(1)}, bf16[32,640]{1,0:T(8,128)(2,1)S(1)}, u32[]{:S(2)}, u32[]{:S(2)}) collective-permute-start(bf16[32,640]{1,0:T(8,128)(2,1)S(1)} %get-tuple-element.40), channel_id=1, source_target_pairs={{0,4},{1,5},{2,6},{3,7},{4,8},{5,9},{6,10},{7,11},{8,12},{9,13},{1... | collective-permute-start | bytes 122888 | tf_op jit(solution)/shard_map/ppermute | solution.py:38
  56.9 2.0 %collective-permute-done.18.b = bf16[32,640]{1,0:T(8,128)(2,1)S(1)} collective-permute-done((bf16[32,640]{1,0:T(8,128)(2,1)S(1)}, bf16[32,640]{1,0:T(8,128)(2,1)S(1)}, u32[]{:S(2)}, u32[]{:S(2)}) %collective-permute-start.18) | collective-permute-done | bytes 40992 | tf_op jit(solution)/shard_map/ppermute | solution.py:38
  58.8 1.6 %collective-permute-done.19.c = bf16[32,640]{1,0:T(8,128)(2,1)S(1)} collective-permute-done((bf16[32,640]{1,0:T(8,128)(2,1)S(1)}, bf16[32,640]{1,0:T(8,128)(2,1)S(1)}, u32[]{:S(2)}, u32[]{:S(2)}) %collective-permute-start.19) | collective-permute-done | bytes 40992 | tf_op jit(solution)/shard_map/ppermute | solution.py:38
  60.4 1.1 %collective-permute-done.20.d = bf16[32,640]{1,0:T(8,128)(2,1)S(1)} collective-permute-done((bf16[32,640]{1,0:T(8,128)(2,1)S(1)}, bf16[32,640]{1,0:T(8,128)(2,1)S(1)}, u32[]{:S(2)}, u32[]{:S(2)}) %collective-permute-start.20) | collective-permute-done | bytes 40992 | tf_op jit(solution)/shard_map/ppermute | solution.py:38
  61.5 1.1 %shard_map.62 = bf16[4,8,128]{2,1,0:T(8,128)(2,1)} custom-call(bf16[32,640]{1,0:T(8,128)(2,1)S(1)} %get-tuple-element.37.a, bf16[32,640]{1,0:T(8,128)(2,1)S(1)} %collective-permute-done.18.b, bf16[32,640]{1,0:T(8,128)(2,1)S(1)} %collective-permute-done.19.c, bf16[32,640]{1,0:T(8,128)(2,1)S(1)} %collective-permute-done.20.d, ...), custom_call_target="tpu_custom_call" | custom-call | tf_op jit(solution)/shard_map/pallas_call | solution.py:332
  (3 shorter events, 0.1 us)
Async XLA Ops:
  0.0 9.0 %collective-permute-start.3 = (bf16[8,64,128]{2,1,0:T(8,128)(2,1)}, bf16[8,64,128]{2,1,0:T(8,128)(2,1)S(1)}, u32[]{:S(2)}, u32[]{:S(2)}) collective-permute-start(bf16[8,64,128]{2,1,0:T(8,128)(2,1)} %bitcast.7), channel_id=1, source_target_pairs={{0,96},{1,97},{2,98},{3,99},{4,100},{5,101},{6,102},{7,103},{8,104... | collective-permute-start | bytes 393224 | tf_op jit(solution)/shard_map/ppermute | solution.py:38
  3.1 8.1 %collective-permute-start.2 = (bf16[8,64,128]{2,1,0:T(8,128)(2,1)}, bf16[8,64,128]{2,1,0:T(8,128)(2,1)S(1)}, u32[]{:S(2)}, u32[]{:S(2)}) collective-permute-start(bf16[8,64,128]{2,1,0:T(8,128)(2,1)} %bitcast.8), channel_id=1, source_target_pairs={{0,64},{1,65},{2,66},{3,67},{4,68},{5,69},{6,70},{7,71},{8,72},{9,... | collective-permute-start | bytes 393224 | tf_op jit(solution)/shard_map/ppermute | solution.py:38
  3.7 8.9 %collective-permute-start.1 = (bf16[8,64,128]{2,1,0:T(8,128)(2,1)}, bf16[8,64,128]{2,1,0:T(8,128)(2,1)S(1)}, u32[]{:S(2)}, u32[]{:S(2)}) collective-permute-start(bf16[8,64,128]{2,1,0:T(8,128)(2,1)} %bitcast.9), channel_id=1, source_target_pairs={{0,32},{1,33},{2,34},{3,35},{4,36},{5,37},{6,38},{7,39},{8,40},{9,... | collective-permute-start | bytes 393224 | tf_op jit(solution)/shard_map/ppermute | solution.py:38
  4.7 8.5 %collective-permute-start.5 = (bf16[8,64,128]{2,1,0:T(8,128)(2,1)}, bf16[8,64,128]{2,1,0:T(8,128)(2,1)S(1)}, u32[]{:S(2)}, u32[]{:S(2)}) collective-permute-start(bf16[8,64,128]{2,1,0:T(8,128)(2,1)} %refs_3_.1), channel_id=1, source_target_pairs={{0,16},{1,17},{2,18},{3,19},{4,20},{5,21},{6,22},{7,23},{8,24},{9,... | collective-permute-start | bytes 393224 | tf_op jit(solution)/shard_map/ppermute | solution.py:38
  4.7 4.2 %collective-permute-start = (bf16[4,8,192]{2,1,0:T(8,128)(2,1)}, bf16[4,8,192]{2,1,0:T(8,128)(2,1)S(1)}, u32[]{:S(2)}, u32[]{:S(2)}) collective-permute-start(bf16[4,8,192]{2,1,0:T(8,128)(2,1)} %bitcast.11), channel_id=1, source_target_pairs={{0,16},{1,17},{2,18},{3,19},{4,20},{5,21},{6,22},{7,23},{8,24},{9,... | collective-permute-start | bytes 36872 | tf_op jit(solution)/shard_map/ppermute | solution.py:38
  13.1 1.3 %collective-permute-start.4 = (bf16[32,576]{1,0:T(8,128)(2,1)S(1)}, bf16[32,576]{1,0:T(8,128)(2,1)S(1)}, u32[]{:S(2)}, u32[]{:S(2)}) collective-permute-start(bf16[32,576]{1,0:T(8,128)(2,1)S(1)} %get-tuple-element.29), channel_id=1, source_target_pairs={{0,16},{1,17},{2,18},{3,19},{4,20},{5,21},{6,22},{7,23},{8,24},{9,... | collective-permute-start | bytes 110600 | tf_op jit(solution)/shard_map/ppermute | solution.py:38
  14.4 5.8 %collective-permute-start.8 = (bf16[32,576]{1,0:T(8,128)(2,1)S(1)}, bf16[32,576]{1,0:T(8,128)(2,1)S(1)}, u32[]{:S(2)}, u32[]{:S(2)}) collective-permute-start(bf16[32,576]{1,0:T(8,128)(2,1)S(1)} %add.3.refs_0_), channel_id=1, source_target_pairs={{0,12},{1,13},{2,14},{3,15},{4,0},{5,1},{6,2},{7,3},{8,4},{9,5},{1... | collective-permute-start | bytes 110600 | tf_op jit(solution)/shard_map/ppermute | solution.py:38
  18.5 5.6 %collective-permute-start.7 = (bf16[32,576]{1,0:T(8,128)(2,1)S(1)}, bf16[32,576]{1,0:T(8,128)(2,1)S(1)}, u32[]{:S(2)}, u32[]{:S(2)}) collective-permute-start(bf16[32,576]{1,0:T(8,128)(2,1)S(1)} %add.3.refs_0_), channel_id=1, source_target_pairs={{0,8},{1,9},{2,10},{3,11},{4,12},{5,13},{6,14},{7,15},{8,0},{9,1},... | collective-permute-start | bytes 110600 | tf_op jit(solution)/shard_map/ppermute | solution.py:38
  18.5 5.7 %collective-permute-start.6 = (bf16[32,576]{1,0:T(8,128)(2,1)S(1)}, bf16[32,576]{1,0:T(8,128)(2,1)S(1)}, u32[]{:S(2)}, u32[]{:S(2)}) collective-permute-start(bf16[32,576]{1,0:T(8,128)(2,1)S(1)} %add.3.refs_0_), channel_id=1, source_target_pairs={{0,4},{1,5},{2,6},{3,7},{4,8},{5,9},{6,10},{7,11},{8,12},{9,13},{1... | collective-permute-start | bytes 110600 | tf_op jit(solution)/shard_map/ppermute | solution.py:38
  24.2 7.5 %collective-permute-start.11 = (bf16[128,576]{1,0:T(8,128)(2,1)S(1)}, bf16[128,576]{1,0:T(8,128)(2,1)S(1)}, u32[]{:S(2)}, u32[]{:S(2)}) collective-permute-start(bf16[128,576]{1,0:T(8,128)(2,1)S(1)} %shard_map.58.refs_0_), channel_id=1, source_target_pairs={{0,3},{1,0},{2,1},{3,2},{4,7},{5,4},{6,5},{7,6},{8,11},{9,8},{10,9... | collective-permute-start | bytes 442376 | tf_op jit(solution)/shard_map/ppermute | solution.py:38
  27.0 6.9 %collective-permute-start.10 = (bf16[128,576]{1,0:T(8,128)(2,1)S(1)}, bf16[128,576]{1,0:T(8,128)(2,1)S(1)}, u32[]{:S(2)}, u32[]{:S(2)}) collective-permute-start(bf16[128,576]{1,0:T(8,128)(2,1)S(1)} %shard_map.58.refs_0_), channel_id=1, source_target_pairs={{0,2},{1,3},{2,0},{3,1},{4,6},{5,7},{6,4},{7,5},{8,10},{9,11},{10,... | collective-permute-start | bytes 442376 | tf_op jit(solution)/shard_map/ppermute | solution.py:38
  27.8 7.8 %collective-permute-start.9 = (bf16[128,576]{1,0:T(8,128)(2,1)S(1)}, bf16[128,576]{1,0:T(8,128)(2,1)S(1)}, u32[]{:S(2)}, u32[]{:S(2)}) collective-permute-start(bf16[128,576]{1,0:T(8,128)(2,1)S(1)} %shard_map.58.refs_0_), channel_id=1, source_target_pairs={{0,1},{1,2},{2,3},{3,0},{4,5},{5,6},{6,7},{7,4},{8,9},{9,10},{10,1... | collective-permute-start | bytes 442376 | tf_op jit(solution)/shard_map/ppermute | solution.py:38
  29.3 17.8 %collective-permute-start.14 = (bf16[2,8,64,128]{3,2,1,0:T(8,128)(2,1)S(1)}, bf16[2,8,64,128]{3,2,1,0:T(8,128)(2,1)S(1)}, u32[]{:S(2)}, u32[]{:S(2)}) collective-permute-start(bf16[2,8,64,128]{3,2,1,0:T(8,128)(2,1)S(1)} %shard_map.57.w0), channel_id=1, source_target_pairs={{0,96},{1,97},{2,98},{3,99},{4,100},{5,101},{6,102},{7,103},{8,104... | collective-permute-start | bytes 786440 | tf_op jit(solution)/shard_map/ppermute | solution.py:38
  30.0 17.8 %collective-permute-start.13 = (bf16[2,8,64,128]{3,2,1,0:T(8,128)(2,1)S(1)}, bf16[2,8,64,128]{3,2,1,0:T(8,128)(2,1)S(1)}, u32[]{:S(2)}, u32[]{:S(2)}) collective-permute-start(bf16[2,8,64,128]{3,2,1,0:T(8,128)(2,1)S(1)} %shard_map.57.w0), channel_id=1, source_target_pairs={{0,64},{1,65},{2,66},{3,67},{4,68},{5,69},{6,70},{7,71},{8,72},{9,... | collective-permute-start | bytes 786440 | tf_op jit(solution)/shard_map/ppermute | solution.py:38
  31.6 16.1 %collective-permute-start.12 = (bf16[2,8,64,128]{3,2,1,0:T(8,128)(2,1)S(1)}, bf16[2,8,64,128]{3,2,1,0:T(8,128)(2,1)S(1)}, u32[]{:S(2)}, u32[]{:S(2)}) collective-permute-start(bf16[2,8,64,128]{3,2,1,0:T(8,128)(2,1)S(1)} %shard_map.57.w0), channel_id=1, source_target_pairs={{0,32},{1,33},{2,34},{3,35},{4,36},{5,37},{6,38},{7,39},{8,40},{9,... | collective-permute-start | bytes 786440 | tf_op jit(solution)/shard_map/ppermute | solution.py:38
  45.7 7.3 %collective-permute-start.15 = (bf16[128,640]{1,0:T(8,128)(2,1)S(1)}, bf16[128,640]{1,0:T(8,128)(2,1)S(1)}, u32[]{:S(2)}, u32[]{:S(2)}) collective-permute-start(bf16[128,640]{1,0:T(8,128)(2,1)S(1)} %get-tuple-element.34), channel_id=1, source_target_pairs={{0,3},{1,0},{2,1},{3,2},{4,7},{5,4},{6,5},{7,6},{8,11},{9,8},{10,9... | collective-permute-start | bytes 491528 | tf_op jit(solution)/shard_map/ppermute | solution.py:38
  45.8 7.2 %collective-permute-start.16 = (bf16[128,640]{1,0:T(8,128)(2,1)S(1)}, bf16[128,640]{1,0:T(8,128)(2,1)S(1)}, u32[]{:S(2)}, u32[]{:S(2)}) collective-permute-start(bf16[128,640]{1,0:T(8,128)(2,1)S(1)} %get-tuple-element.35), channel_id=1, source_target_pairs={{0,2},{1,3},{2,0},{3,1},{4,6},{5,7},{6,4},{7,5},{8,10},{9,11},{10,... | collective-permute-start | bytes 491528 | tf_op jit(solution)/shard_map/ppermute | solution.py:38
  47.1 7.3 %collective-permute-start.17 = (bf16[128,640]{1,0:T(8,128)(2,1)S(1)}, bf16[128,640]{1,0:T(8,128)(2,1)S(1)}, u32[]{:S(2)}, u32[]{:S(2)}) collective-permute-start(bf16[128,640]{1,0:T(8,128)(2,1)S(1)} %get-tuple-element.36), channel_id=1, source_target_pairs={{0,1},{1,2},{2,3},{3,0},{4,5},{5,6},{6,7},{7,4},{8,9},{9,10},{10,1... | collective-permute-start | bytes 491528 | tf_op jit(solution)/shard_map/ppermute | solution.py:38
  54.8 4.1 %collective-permute-start.18 = (bf16[32,640]{1,0:T(8,128)(2,1)S(1)}, bf16[32,640]{1,0:T(8,128)(2,1)S(1)}, u32[]{:S(2)}, u32[]{:S(2)}) collective-permute-start(bf16[32,640]{1,0:T(8,128)(2,1)S(1)} %get-tuple-element.38), channel_id=1, source_target_pairs={{0,12},{1,13},{2,14},{3,15},{4,0},{5,1},{6,2},{7,3},{8,4},{9,5},{1... | collective-permute-start | bytes 122888 | tf_op jit(solution)/shard_map/ppermute | solution.py:38
  54.9 5.6 %collective-permute-start.19 = (bf16[32,640]{1,0:T(8,128)(2,1)S(1)}, bf16[32,640]{1,0:T(8,128)(2,1)S(1)}, u32[]{:S(2)}, u32[]{:S(2)}) collective-permute-start(bf16[32,640]{1,0:T(8,128)(2,1)S(1)} %get-tuple-element.39), channel_id=1, source_target_pairs={{0,8},{1,9},{2,10},{3,11},{4,12},{5,13},{6,14},{7,15},{8,0},{9,1},... | collective-permute-start | bytes 122888 | tf_op jit(solution)/shard_map/ppermute | solution.py:38
  54.9 6.6 %collective-permute-start.20 = (bf16[32,640]{1,0:T(8,128)(2,1)S(1)}, bf16[32,640]{1,0:T(8,128)(2,1)S(1)}, u32[]{:S(2)}, u32[]{:S(2)}) collective-permute-start(bf16[32,640]{1,0:T(8,128)(2,1)S(1)} %get-tuple-element.40), channel_id=1, source_target_pairs={{0,4},{1,5},{2,6},{3,7},{4,8},{5,9},{6,10},{7,11},{8,12},{9,13},{1... | collective-permute-start | bytes 122888 | tf_op jit(solution)/shard_map/ppermute | solution.py:38

commit v5 on v4

--- a/solution.py
+++ b/solution.py
@@ -175,7 +175,8 @@
     return so_far
 
 
-def attend_kernel(length, cache, *refs, block):
+def attend_kernel(length, cache, *refs, block, first):
+    turned, refs = (refs[-6], refs[:-6] + refs[-5:]) if first else (refs[0], refs[1:])
     count = (len(refs) - 5) // 2
     parts, outs = refs[:count], refs[count : 2 * count]
     query, scores, tops, totals, acc = refs[2 * count :]
@@ -193,9 +194,9 @@
         return jnp.dot(query[...], cache[:, here(i)], preferred_element_type=F32)
 
     def weigh(i, p):
-        return lax.dot_general(
-            p.astype(BF16), cache[:LATENT, here(i)], (((1,), (1,)), ((), ())), preferred_element_type=F32
-        )
+        if first:
+            turned[here(i), :] = cache[:LATENT, here(i)].T
+        return jnp.dot(p.astype(BF16), turned[here(i), :], preferred_element_type=F32)
 
     def largest(value):
         return jnp.broadcast_to(jnp.max(value, axis=1, keepdims=True), value.shape)
@@ -253,14 +254,19 @@
         finish(jnp.full(tops.shape, MASKED, F32))
 
 
-def attend(length, parts, cache, block=1024):
+def attend(length, parts, cache, turned=None, block=1024):
     group = parts[0].shape[0]
     rows, span = group * len(parts), cache.shape[1]
-    return pl.pallas_call(
-        functools.partial(attend_kernel, block=block),
-        out_shape=[jax.ShapeDtypeStruct((group, PAYLOAD), BF16)] * len(parts),
-        in_specs=[SMEM] + [VMEM] * (1 + len(parts)),
-        out_specs=[VMEM] * len(parts),
+    first = turned is None
+    out_shape = [jax.ShapeDtypeStruct((group, PAYLOAD), BF16)] * len(parts)
+    if first:
+        out_shape.append(jax.ShapeDtypeStruct((span, LATENT), BF16))
+    operands = [length, cache, *([] if first else [turned]), *parts]
+    outs = pl.pallas_call(
+        functools.partial(attend_kernel, block=block, first=first),
+        out_shape=out_shape,
+        in_specs=[SMEM] + [VMEM] * (len(operands) - 1),
+        out_specs=[VMEM] * len(out_shape),
         scratch_shapes=[
             pltpu.VMEM((rows, WIDTH), BF16),
             pltpu.VMEM((rows, 2 * block), F32),
@@ -272,7 +278,8 @@
         cost_estimate=pl.CostEstimate(
             flops=2 * rows * span * (WIDTH + LATENT), bytes_accessed=span * WIDTH * 2, transcendentals=rows * span
         ),
-    )(length, cache, *parts)
+    )(*operands)
+    return (outs[:-1], outs[-1]) if first else (outs, turned)
 
 
 def merge_kernel(*refs):
@@ -360,10 +367,11 @@
     groups = [near] + [second_shift(near, hops) for hops in (1, 2, 3)]
     value_pairs = [value_pair] + [y_shift(value_pair, hops) for hops in (1, 2, 3)]
 
-    away = attend(lengths, groups[1:], cache)
+    (one, three), turned = attend(lengths, [groups[1], groups[3]], cache)
     groups, value_pairs = lax.optimization_barrier((groups, value_pairs))
-    (zero,) = attend(lengths, groups[:1], cache)
-    parts = [zero] + [second_shift(part, -hops) for hops, part in enumerate(away, 1)]
+    (two,), _ = attend(lengths, groups[2:3], cache, turned)
+    (zero,), _ = attend(lengths, groups[:1], cache, turned)
+    parts = [zero] + [second_shift(part, -hops) for hops, part in ((1, one), (2, two), (3, three))]
 
     near = merge_groups(parts)
     last = [near[0]] + [first_shift(near[hops], -hops) for hops in (1, 2, 3)]

time: 63 us -> 63 us (level)
  starting transfers between devices: 20.6 us -> 24.8 us
  waiting for transfers between devices: 20.2 us -> 17.1 us
  Pallas kernels: 21 us -> 20.2 us
    ppermute x21, starting transfers between devices: 20.6 us -> 24.8 us  [exchange(): return lax.ppermute(value, ('roll', 'seq'), pairs)]
    ppermute x21, waiting for transfers between devices: 20.2 us -> 17.1 us  [exchange(): return lax.ppermute(value, ('roll', 'seq'), pairs)]
    pallas_call x2 -> x3, Pallas kernels: 15.3 us -> 14.5 us  [attend(): pl.pallas_call(functools.partial(attend_kernel, block=block, first=first)...]
  transfers between devices with their start and end apart: 21 -> 21, of which waited for: 12 -> 10; matrix products, arithmetic and copies ran while one was open for 0% -> 0% of each run, Pallas kernels for 31% -> 30%
where the time goes in v5:
time: 63 us; the launch traced here: 62.9 us
  starting transfers between devices  24.8 us (39%)
  Pallas kernels  20.2 us (32%)
  waiting for transfers between devices  17.1 us (27%)
  between operations  0.77 us (1%)
    ppermute x21, starting transfers between devices, exchange(): return lax.ppermute(value, ('roll', 'seq'), pairs)  24.8 us
    ppermute x21, waiting for transfers between devices, exchange(): return lax.ppermute(value, ('roll', 'seq'), pairs)  17.1 us
    pallas_call x3, Pallas kernels, attend(): pl.pallas_call(functools.partial(attend_kernel, block=block, first=first)...  14.5 us
    pallas_call x1, Pallas kernels, load(): pl.pallas_call(load_kernel, out_shape=[jax.ShapeDtypeStruct(a.shape, a.dt...  3.72 us
  transfers between devices with their start and end apart: 21, of which 10 were waited for; matrix products, arithmetic and copies ran while one was open for 0% of the time, Pallas kernels for 30%

profile of v5, /device:TPU:0, one launch (start us, length us, event | category | flops | bytes accessed | tf_op | source)
XLA Modules:
  0.0 62.9 jit_solution(629024280499386779)
XLA Ops:
  0.0 3.1 %collective-permute-start.3 = (bf16[8,64,128]{2,1,0:T(8,128)(2,1)}, bf16[8,64,128]{2,1,0:T(8,128)(2,1)S(1)}, u32[]{:S(2)}, u32[]{:S(2)}) collective-permute-start(bf16[8,64,128]{2,1,0:T(8,128)(2,1)} %bitcast.7), channel_id=1, source_target_pairs={{0,96},{1,97},{2,98},{3,99},{4,100},{5,101},{6,102},{7,103},{8,104... | collective-permute-start | bytes 393224 | tf_op jit(solution)/shard_map/ppermute | solution.py:38
  3.1 0.6 %collective-permute-start.2 = (bf16[8,64,128]{2,1,0:T(8,128)(2,1)}, bf16[8,64,128]{2,1,0:T(8,128)(2,1)S(1)}, u32[]{:S(2)}, u32[]{:S(2)}) collective-permute-start(bf16[8,64,128]{2,1,0:T(8,128)(2,1)} %bitcast.8), channel_id=1, source_target_pairs={{0,64},{1,65},{2,66},{3,67},{4,68},{5,69},{6,70},{7,71},{8,72},{9,... | collective-permute-start | bytes 393224 | tf_op jit(solution)/shard_map/ppermute | solution.py:38
  3.7 1.0 %collective-permute-start.1 = (bf16[8,64,128]{2,1,0:T(8,128)(2,1)}, bf16[8,64,128]{2,1,0:T(8,128)(2,1)S(1)}, u32[]{:S(2)}, u32[]{:S(2)}) collective-permute-start(bf16[8,64,128]{2,1,0:T(8,128)(2,1)} %bitcast.9), channel_id=1, source_target_pairs={{0,32},{1,33},{2,34},{3,35},{4,36},{5,37},{6,38},{7,39},{8,40},{9,... | collective-permute-start | bytes 393224 | tf_op jit(solution)/shard_map/ppermute | solution.py:38
  4.7 0.0 collective-permute-start.5
  4.7 0.5 collective-permute-start
  5.2 3.7 %shard_map.55 = (bf16[576,8192]{1,0:T(8,128)(2,1)S(1)}, bf16[8,64,128]{2,1,0:T(8,128)(2,1)S(1)}, bf16[4,8,192]{2,1,0:T(8,128)(2,1)S(1)}, bf16[8,64,128]{2,1,0:T(8,128)(2,1)S(1)}) custom-call(bf16[576,8192]{1,0:T(8,128)(2,1)} %bitcast.6, bf16[8,64,128]{2,1,0:T(8,128)(2,1)} %bitcast.10, bf16[4,8,192]{2,1,0:T(8,128)(2,1)} %bitcast.12, bf16[8,64,128]{2,1,0:T(8,128)(2,1)} %refs_3_.1), custom_call_target="tpu_custom_call" | custom-call | bytes 19423232 | tf_op jit(solution)/shard_map/pallas_call | solution.py:107
  8.9 0.0 collective-permute-done.other
  8.9 0.0 collective-permute-done.3.kw3
  9.0 2.2 %collective-permute-done.2.kw2 = bf16[8,64,128]{2,1,0:T(8,128)(2,1)S(1)} collective-permute-done((bf16[8,64,128]{2,1,0:T(8,128)(2,1)}, bf16[8,64,128]{2,1,0:T(8,128)(2,1)S(1)}, u32[]{:S(2)}, u32[]{:S(2)}) %collective-permute-start.2) | collective-permute-done | bytes 131104 | tf_op jit(solution)/shard_map/ppermute | solution.py:38
  11.2 1.4 %collective-permute-done.1.kw1 = bf16[8,64,128]{2,1,0:T(8,128)(2,1)S(1)} collective-permute-done((bf16[8,64,128]{2,1,0:T(8,128)(2,1)}, bf16[8,64,128]{2,1,0:T(8,128)(2,1)S(1)}, u32[]{:S(2)}, u32[]{:S(2)}) %collective-permute-start.1) | collective-permute-done | bytes 131104 | tf_op jit(solution)/shard_map/ppermute | solution.py:38
  12.6 0.5 shard_map.56
  13.1 0.0 collective-permute-start.4
  13.2 0.0 collective-permute-done.5.other
  13.2 1.2 %collective-permute-done.4 = bf16[32,576]{1,0:T(8,128)(2,1)S(1)} collective-permute-done((bf16[32,576]{1,0:T(8,128)(2,1)S(1)}, bf16[32,576]{1,0:T(8,128)(2,1)S(1)}, u32[]{:S(2)}, u32[]{:S(2)}) %collective-permute-start.4) | collective-permute-done | bytes 36896 | tf_op jit(solution)/shard_map/ppermute | solution.py:38
  14.4 4.1 %collective-permute-start.8 = (bf16[32,576]{1,0:T(8,128)(2,1)S(1)}, bf16[32,576]{1,0:T(8,128)(2,1)S(1)}, u32[]{:S(2)}, u32[]{:S(2)}) collective-permute-start(bf16[32,576]{1,0:T(8,128)(2,1)S(1)} %add.3.refs_0_), channel_id=1, source_target_pairs={{0,12},{1,13},{2,14},{3,15},{4,0},{5,1},{6,2},{7,3},{8,4},{9,5},{1... | collective-permute-start | bytes 110600 | tf_op jit(solution)/shard_map/ppermute | solution.py:38
  18.5 0.0 collective-permute-start.7
  18.5 1.3 %collective-permute-start.6 = (bf16[32,576]{1,0:T(8,128)(2,1)S(1)}, bf16[32,576]{1,0:T(8,128)(2,1)S(1)}, u32[]{:S(2)}, u32[]{:S(2)}) collective-permute-start(bf16[32,576]{1,0:T(8,128)(2,1)S(1)} %add.3.refs_0_), channel_id=1, source_target_pairs={{0,4},{1,5},{2,6},{3,7},{4,8},{5,9},{6,10},{7,11},{8,12},{9,13},{1... | collective-permute-start | bytes 110600 | tf_op jit(solution)/shard_map/ppermute | solution.py:38
  19.8 0.4 collective-permute-done.8.refs_3_
  20.2 3.9 %collective-permute-done.7.refs_2_ = bf16[32,576]{1,0:T(8,128)(2,1)S(1)} collective-permute-done((bf16[32,576]{1,0:T(8,128)(2,1)S(1)}, bf16[32,576]{1,0:T(8,128)(2,1)S(1)}, u32[]{:S(2)}, u32[]{:S(2)}) %collective-permute-start.7) | collective-permute-done | bytes 36896 | tf_op jit(solution)/shard_map/ppermute | solution.py:38
  24.1 0.0 collective-permute-done.6.refs_1_
  24.2 2.8 %collective-permute-start.10 = (bf16[128,576]{1,0:T(8,128)(2,1)S(1)}, bf16[128,576]{1,0:T(8,128)(2,1)S(1)}, u32[]{:S(2)}, u32[]{:S(2)}) collective-permute-start(bf16[128,576]{1,0:T(8,128)(2,1)S(1)} %shard_map.58.refs_1_), channel_id=1, source_target_pairs={{0,3},{1,0},{2,1},{3,2},{4,7},{5,4},{6,5},{7,6},{8,11},{9,8},{10,9... | collective-permute-start | bytes 442376 | tf_op jit(solution)/shard_map/ppermute | solution.py:38
  27.0 0.0 collective-permute-start.9
  27.7 0.6 %collective-permute-start.14 = (bf16[2,8,64,128]{3,2,1,0:T(8,128)(2,1)S(1)}, bf16[2,8,64,128]{3,2,1,0:T(8,128)(2,1)S(1)}, u32[]{:S(2)}, u32[]{:S(2)}) collective-permute-start(bf16[2,8,64,128]{3,2,1,0:T(8,128)(2,1)S(1)} %shard_map.57.w0), channel_id=1, source_target_pairs={{0,96},{1,97},{2,98},{3,99},{4,100},{5,101},{6,102},{7,103},{8,104... | collective-permute-start | bytes 786440 | tf_op jit(solution)/shard_map/ppermute | solution.py:38
  28.3 0.6 %collective-permute-start.13 = (bf16[2,8,64,128]{3,2,1,0:T(8,128)(2,1)S(1)}, bf16[2,8,64,128]{3,2,1,0:T(8,128)(2,1)S(1)}, u32[]{:S(2)}, u32[]{:S(2)}) collective-permute-start(bf16[2,8,64,128]{3,2,1,0:T(8,128)(2,1)S(1)} %shard_map.57.w0), channel_id=1, source_target_pairs={{0,64},{1,65},{2,66},{3,67},{4,68},{5,69},{6,70},{7,71},{8,72},{9,... | collective-permute-start | bytes 786440 | tf_op jit(solution)/shard_map/ppermute | solution.py:38
  28.9 0.9 %collective-permute-start.12 = (bf16[2,8,64,128]{3,2,1,0:T(8,128)(2,1)S(1)}, bf16[2,8,64,128]{3,2,1,0:T(8,128)(2,1)S(1)}, u32[]{:S(2)}, u32[]{:S(2)}) collective-permute-start(bf16[2,8,64,128]{3,2,1,0:T(8,128)(2,1)S(1)} %shard_map.57.w0), channel_id=1, source_target_pairs={{0,32},{1,33},{2,34},{3,35},{4,36},{5,37},{6,38},{7,39},{8,40},{9,... | collective-permute-start | bytes 786440 | tf_op jit(solution)/shard_map/ppermute | solution.py:38
  29.8 0.1 collective-permute-done.10.refs_1_
  29.8 2.7 %collective-permute-start.11 = (bf16[128,576]{1,0:T(8,128)(2,1)S(1)}, bf16[128,576]{1,0:T(8,128)(2,1)S(1)}, u32[]{:S(2)}, u32[]{:S(2)}) collective-permute-start(bf16[128,576]{1,0:T(8,128)(2,1)S(1)} %shard_map.58.refs_1_), channel_id=1, source_target_pairs={{0,2},{1,3},{2,0},{3,1},{4,6},{5,7},{6,4},{7,5},{8,10},{9,11},{10,... | collective-permute-start | bytes 442376 | tf_op jit(solution)/shard_map/ppermute | solution.py:38
  32.6 0.9 %collective-permute-done.9.refs_0_ = bf16[128,576]{1,0:T(8,128)(2,1)S(1)} collective-permute-done((bf16[128,576]{1,0:T(8,128)(2,1)S(1)}, bf16[128,576]{1,0:T(8,128)(2,1)S(1)}, u32[]{:S(2)}, u32[]{:S(2)}) %collective-permute-start.9) | collective-permute-done | bytes 147488 | tf_op jit(solution)/shard_map/ppermute | solution.py:38
  33.5 7.2 %shard_map.59 = (bf16[128,640]{1,0:T(8,128)(2,1)S(1)}, bf16[128,640]{1,0:T(8,128)(2,1)S(1)}, bf16[8192,512]{1,0:T(8,128)(2,1)S(1)}) custom-call(s32[1]{0:T(128)S(6)} %copy.6.length, bf16[576,8192]{1,0:T(8,128)(2,1)S(1)} %get-tuple-element.26.cache, bf16[128,576]{1,0:T(8,128)(2,1)S(1)} %collective-permute-done.9.refs_0_, ...), custom_call_target="tpu_custom_call" | custom-call | flops 4563402752 | bytes 9437184 | tf_op jit(solution)/shard_map/pallas_call | solution.py:265
  40.7 0.3 collective-permute-start.15
  41.0 0.0 collective-permute-done.11.refs_1_
  41.0 1.8 %collective-permute-start.17 = (bf16[128,640]{1,0:T(8,128)(2,1)S(1)}, bf16[128,640]{1,0:T(8,128)(2,1)S(1)}, u32[]{:S(2)}, u32[]{:S(2)}) collective-permute-start(bf16[128,640]{1,0:T(8,128)(2,1)S(1)} %get-tuple-element.38), channel_id=1, source_target_pairs={{0,1},{1,2},{2,3},{3,0},{4,5},{5,6},{6,7},{7,4},{8,9},{9,10},{10,1... | collective-permute-start | bytes 491528 | tf_op jit(solution)/shard_map/ppermute | solution.py:38
  42.8 0.0 collective-permute-done.14.w3
  42.8 0.0 collective-permute-done.13.w2
  42.8 0.0 collective-permute-done.12.w1
  42.8 3.8 %shard_map.61 = bf16[128,640]{1,0:T(8,128)(2,1)S(1)} custom-call(s32[1]{0:T(128)S(6)} %copy.6.length, bf16[576,8192]{1,0:T(8,128)(2,1)S(1)} %get-tuple-element.26.cache, bf16[8192,512]{1,0:T(8,128)(2,1)S(1)} %get-tuple-element.33.refs_0_, bf16[128,576]{1,0:T(8,128)(2,1)S(1)} %collective-permute-done.11.refs_1_), custom_call_target="tpu_custom_call" | custom-call | flops 2281701376 | bytes 9437184 | tf_op jit(solution)/shard_map/pallas_call | solution.py:265
  46.6 1.0 %collective-permute-start.16 = (bf16[128,640]{1,0:T(8,128)(2,1)S(1)}, bf16[128,640]{1,0:T(8,128)(2,1)S(1)}, u32[]{:S(2)}, u32[]{:S(2)}) collective-permute-start(bf16[128,640]{1,0:T(8,128)(2,1)S(1)} %shard_map.61), channel_id=1, source_target_pairs={{0,2},{1,3},{2,0},{3,1},{4,6},{5,7},{6,4},{7,5},{8,10},{9,11},{10,... | collective-permute-start | bytes 491528 | tf_op jit(solution)/shard_map/ppermute | solution.py:38
  47.6 3.5 %shard_map.60.refs_0_ = bf16[128,640]{1,0:T(8,128)(2,1)S(1)} custom-call(s32[1]{0:T(128)S(6)} %copy.6.length, bf16[576,8192]{1,0:T(8,128)(2,1)S(1)} %get-tuple-element.26.cache, bf16[8192,512]{1,0:T(8,128)(2,1)S(1)} %get-tuple-element.33.refs_0_, bf16[128,576]{1,0:T(8,128)(2,1)S(1)} %shard_map.58.refs_1_), custom_call_target="tpu_custom_call" | custom-call | flops 2281701376 | bytes 9437184 | tf_op jit(solution)/shard_map/pallas_call | solution.py:265
  51.2 0.0 collective-permute-done.15.refs_1_
  51.2 0.0 collective-permute-done.17.refs_3_
  51.2 2.3 %collective-permute-done.16.refs_2_ = bf16[128,640]{1,0:T(8,128)(2,1)S(1)} collective-permute-done((bf16[128,640]{1,0:T(8,128)(2,1)S(1)}, bf16[128,640]{1,0:T(8,128)(2,1)S(1)}, u32[]{:S(2)}, u32[]{:S(2)}) %collective-permute-start.16) | collective-permute-done | bytes 163872 | tf_op jit(solution)/shard_map/ppermute | solution.py:38
  53.5 0.3 shard_map.62
  53.9 2.3 %collective-permute-start.18 = (bf16[32,640]{1,0:T(8,128)(2,1)S(1)}, bf16[32,640]{1,0:T(8,128)(2,1)S(1)}, u32[]{:S(2)}, u32[]{:S(2)}) collective-permute-start(bf16[32,640]{1,0:T(8,128)(2,1)S(1)} %get-tuple-element.40), channel_id=1, source_target_pairs={{0,12},{1,13},{2,14},{3,15},{4,0},{5,1},{6,2},{7,3},{8,4},{9,5},{1... | collective-permute-start | bytes 122888 | tf_op jit(solution)/shard_map/ppermute | solution.py:38
  56.2 0.0 collective-permute-start.19
  56.2 1.1 %collective-permute-start.20 = (bf16[32,640]{1,0:T(8,128)(2,1)S(1)}, bf16[32,640]{1,0:T(8,128)(2,1)S(1)}, u32[]{:S(2)}, u32[]{:S(2)}) collective-permute-start(bf16[32,640]{1,0:T(8,128)(2,1)S(1)} %get-tuple-element.42), channel_id=1, source_target_pairs={{0,4},{1,5},{2,6},{3,7},{4,8},{5,9},{6,10},{7,11},{8,12},{9,13},{1... | collective-permute-start | bytes 122888 | tf_op jit(solution)/shard_map/ppermute | solution.py:38
  57.3 0.7 %collective-permute-done.18.b = bf16[32,640]{1,0:T(8,128)(2,1)S(1)} collective-permute-done((bf16[32,640]{1,0:T(8,128)(2,1)S(1)}, bf16[32,640]{1,0:T(8,128)(2,1)S(1)}, u32[]{:S(2)}, u32[]{:S(2)}) %collective-permute-start.18) | collective-permute-done | bytes 40992 | tf_op jit(solution)/shard_map/ppermute | solution.py:38
  58.0 3.8 %collective-permute-done.19.c = bf16[32,640]{1,0:T(8,128)(2,1)S(1)} collective-permute-done((bf16[32,640]{1,0:T(8,128)(2,1)S(1)}, bf16[32,640]{1,0:T(8,128)(2,1)S(1)}, u32[]{:S(2)}, u32[]{:S(2)}) %collective-permute-start.19) | collective-permute-done | bytes 40992 | tf_op jit(solution)/shard_map/ppermute | solution.py:38
  61.8 0.0 collective-permute-done.20.d
  61.8 1.1 %shard_map.63 = bf16[4,8,128]{2,1,0:T(8,128)(2,1)} custom-call(bf16[32,640]{1,0:T(8,128)(2,1)S(1)} %get-tuple-element.39.a, bf16[32,640]{1,0:T(8,128)(2,1)S(1)} %collective-permute-done.18.b, bf16[32,640]{1,0:T(8,128)(2,1)S(1)} %collective-permute-done.19.c, bf16[32,640]{1,0:T(8,128)(2,1)S(1)} %collective-permute-done.20.d, ...), custom_call_target="tpu_custom_call" | custom-call | tf_op jit(solution)/shard_map/pallas_call | solution.py:339
  (3 shorter events, 0.1 us)
Async XLA Ops:
  0.0 9.0 %collective-permute-start.3 = (bf16[8,64,128]{2,1,0:T(8,128)(2,1)}, bf16[8,64,128]{2,1,0:T(8,128)(2,1)S(1)}, u32[]{:S(2)}, u32[]{:S(2)}) collective-permute-start(bf16[8,64,128]{2,1,0:T(8,128)(2,1)} %bitcast.7), channel_id=1, source_target_pairs={{0,96},{1,97},{2,98},{3,99},{4,100},{5,101},{6,102},{7,103},{8,104... | collective-permute-start | bytes 393224 | tf_op jit(solution)/shard_map/ppermute | solution.py:38
  3.1 8.1 %collective-permute-start.2 = (bf16[8,64,128]{2,1,0:T(8,128)(2,1)}, bf16[8,64,128]{2,1,0:T(8,128)(2,1)S(1)}, u32[]{:S(2)}, u32[]{:S(2)}) collective-permute-start(bf16[8,64,128]{2,1,0:T(8,128)(2,1)} %bitcast.8), channel_id=1, source_target_pairs={{0,64},{1,65},{2,66},{3,67},{4,68},{5,69},{6,70},{7,71},{8,72},{9,... | collective-permute-start | bytes 393224 | tf_op jit(solution)/shard_map/ppermute | solution.py:38
  3.7 8.9 %collective-permute-start.1 = (bf16[8,64,128]{2,1,0:T(8,128)(2,1)}, bf16[8,64,128]{2,1,0:T(8,128)(2,1)S(1)}, u32[]{:S(2)}, u32[]{:S(2)}) collective-permute-start(bf16[8,64,128]{2,1,0:T(8,128)(2,1)} %bitcast.9), channel_id=1, source_target_pairs={{0,32},{1,33},{2,34},{3,35},{4,36},{5,37},{6,38},{7,39},{8,40},{9,... | collective-permute-start | bytes 393224 | tf_op jit(solution)/shard_map/ppermute | solution.py:38
  4.7 8.5 %collective-permute-start.5 = (bf16[8,64,128]{2,1,0:T(8,128)(2,1)}, bf16[8,64,128]{2,1,0:T(8,128)(2,1)S(1)}, u32[]{:S(2)}, u32[]{:S(2)}) collective-permute-start(bf16[8,64,128]{2,1,0:T(8,128)(2,1)} %refs_3_.1), channel_id=1, source_target_pairs={{0,16},{1,17},{2,18},{3,19},{4,20},{5,21},{6,22},{7,23},{8,24},{9,... | collective-permute-start | bytes 393224 | tf_op jit(solution)/shard_map/ppermute | solution.py:38
  4.7 4.2 %collective-permute-start = (bf16[4,8,192]{2,1,0:T(8,128)(2,1)}, bf16[4,8,192]{2,1,0:T(8,128)(2,1)S(1)}, u32[]{:S(2)}, u32[]{:S(2)}) collective-permute-start(bf16[4,8,192]{2,1,0:T(8,128)(2,1)} %bitcast.11), channel_id=1, source_target_pairs={{0,16},{1,17},{2,18},{3,19},{4,20},{5,21},{6,22},{7,23},{8,24},{9,... | collective-permute-start | bytes 36872 | tf_op jit(solution)/shard_map/ppermute | solution.py:38
  13.1 1.3 %collective-permute-start.4 = (bf16[32,576]{1,0:T(8,128)(2,1)S(1)}, bf16[32,576]{1,0:T(8,128)(2,1)S(1)}, u32[]{:S(2)}, u32[]{:S(2)}) collective-permute-start(bf16[32,576]{1,0:T(8,128)(2,1)S(1)} %get-tuple-element.30), channel_id=1, source_target_pairs={{0,16},{1,17},{2,18},{3,19},{4,20},{5,21},{6,22},{7,23},{8,24},{9,... | collective-permute-start | bytes 110600 | tf_op jit(solution)/shard_map/ppermute | solution.py:38
  14.4 5.8 %collective-permute-start.8 = (bf16[32,576]{1,0:T(8,128)(2,1)S(1)}, bf16[32,576]{1,0:T(8,128)(2,1)S(1)}, u32[]{:S(2)}, u32[]{:S(2)}) collective-permute-start(bf16[32,576]{1,0:T(8,128)(2,1)S(1)} %add.3.refs_0_), channel_id=1, source_target_pairs={{0,12},{1,13},{2,14},{3,15},{4,0},{5,1},{6,2},{7,3},{8,4},{9,5},{1... | collective-permute-start | bytes 110600 | tf_op jit(solution)/shard_map/ppermute | solution.py:38
  18.5 5.6 %collective-permute-start.7 = (bf16[32,576]{1,0:T(8,128)(2,1)S(1)}, bf16[32,576]{1,0:T(8,128)(2,1)S(1)}, u32[]{:S(2)}, u32[]{:S(2)}) collective-permute-start(bf16[32,576]{1,0:T(8,128)(2,1)S(1)} %add.3.refs_0_), channel_id=1, source_target_pairs={{0,8},{1,9},{2,10},{3,11},{4,12},{5,13},{6,14},{7,15},{8,0},{9,1},... | collective-permute-start | bytes 110600 | tf_op jit(solution)/shard_map/ppermute | solution.py:38
  18.5 5.7 %collective-permute-start.6 = (bf16[32,576]{1,0:T(8,128)(2,1)S(1)}, bf16[32,576]{1,0:T(8,128)(2,1)S(1)}, u32[]{:S(2)}, u32[]{:S(2)}) collective-permute-start(bf16[32,576]{1,0:T(8,128)(2,1)S(1)} %add.3.refs_0_), channel_id=1, source_target_pairs={{0,4},{1,5},{2,6},{3,7},{4,8},{5,9},{6,10},{7,11},{8,12},{9,13},{1... | collective-permute-start | bytes 110600 | tf_op jit(solution)/shard_map/ppermute | solution.py:38
  24.2 5.7 %collective-permute-start.10 = (bf16[128,576]{1,0:T(8,128)(2,1)S(1)}, bf16[128,576]{1,0:T(8,128)(2,1)S(1)}, u32[]{:S(2)}, u32[]{:S(2)}) collective-permute-start(bf16[128,576]{1,0:T(8,128)(2,1)S(1)} %shard_map.58.refs_1_), channel_id=1, source_target_pairs={{0,3},{1,0},{2,1},{3,2},{4,7},{5,4},{6,5},{7,6},{8,11},{9,8},{10,9... | collective-permute-start | bytes 442376 | tf_op jit(solution)/shard_map/ppermute | solution.py:38
  27.0 6.5 %collective-permute-start.9 = (bf16[128,576]{1,0:T(8,128)(2,1)S(1)}, bf16[128,576]{1,0:T(8,128)(2,1)S(1)}, u32[]{:S(2)}, u32[]{:S(2)}) collective-permute-start(bf16[128,576]{1,0:T(8,128)(2,1)S(1)} %shard_map.58.refs_1_), channel_id=1, source_target_pairs={{0,1},{1,2},{2,3},{3,0},{4,5},{5,6},{6,7},{7,4},{8,9},{9,10},{10,1... | collective-permute-start | bytes 442376 | tf_op jit(solution)/shard_map/ppermute | solution.py:38
  27.7 15.2 %collective-permute-start.14 = (bf16[2,8,64,128]{3,2,1,0:T(8,128)(2,1)S(1)}, bf16[2,8,64,128]{3,2,1,0:T(8,128)(2,1)S(1)}, u32[]{:S(2)}, u32[]{:S(2)}) collective-permute-start(bf16[2,8,64,128]{3,2,1,0:T(8,128)(2,1)S(1)} %shard_map.57.w0), channel_id=1, source_target_pairs={{0,96},{1,97},{2,98},{3,99},{4,100},{5,101},{6,102},{7,103},{8,104... | collective-permute-start | bytes 786440 | tf_op jit(solution)/shard_map/ppermute | solution.py:38
  28.3 14.5 %collective-permute-start.13 = (bf16[2,8,64,128]{3,2,1,0:T(8,128)(2,1)S(1)}, bf16[2,8,64,128]{3,2,1,0:T(8,128)(2,1)S(1)}, u32[]{:S(2)}, u32[]{:S(2)}) collective-permute-start(bf16[2,8,64,128]{3,2,1,0:T(8,128)(2,1)S(1)} %shard_map.57.w0), channel_id=1, source_target_pairs={{0,64},{1,65},{2,66},{3,67},{4,68},{5,69},{6,70},{7,71},{8,72},{9,... | collective-permute-start | bytes 786440 | tf_op jit(solution)/shard_map/ppermute | solution.py:38
  28.9 13.9 %collective-permute-start.12 = (bf16[2,8,64,128]{3,2,1,0:T(8,128)(2,1)S(1)}, bf16[2,8,64,128]{3,2,1,0:T(8,128)(2,1)S(1)}, u32[]{:S(2)}, u32[]{:S(2)}) collective-permute-start(bf16[2,8,64,128]{3,2,1,0:T(8,128)(2,1)S(1)} %shard_map.57.w0), channel_id=1, source_target_pairs={{0,32},{1,33},{2,34},{3,35},{4,36},{5,37},{6,38},{7,39},{8,40},{9,... | collective-permute-start | bytes 786440 | tf_op jit(solution)/shard_map/ppermute | solution.py:38
  29.8 11.2 %collective-permute-start.11 = (bf16[128,576]{1,0:T(8,128)(2,1)S(1)}, bf16[128,576]{1,0:T(8,128)(2,1)S(1)}, u32[]{:S(2)}, u32[]{:S(2)}) collective-permute-start(bf16[128,576]{1,0:T(8,128)(2,1)S(1)} %shard_map.58.refs_1_), channel_id=1, source_target_pairs={{0,2},{1,3},{2,0},{3,1},{4,6},{5,7},{6,4},{7,5},{8,10},{9,11},{10,... | collective-permute-start | bytes 442376 | tf_op jit(solution)/shard_map/ppermute | solution.py:38
  40.7 10.4 %collective-permute-start.15 = (bf16[128,640]{1,0:T(8,128)(2,1)S(1)}, bf16[128,640]{1,0:T(8,128)(2,1)S(1)}, u32[]{:S(2)}, u32[]{:S(2)}) collective-permute-start(bf16[128,640]{1,0:T(8,128)(2,1)S(1)} %get-tuple-element.36), channel_id=1, source_target_pairs={{0,3},{1,0},{2,1},{3,2},{4,7},{5,4},{6,5},{7,6},{8,11},{9,8},{10,9... | collective-permute-start | bytes 491528 | tf_op jit(solution)/shard_map/ppermute | solution.py:38
  41.0 10.2 %collective-permute-start.17 = (bf16[128,640]{1,0:T(8,128)(2,1)S(1)}, bf16[128,640]{1,0:T(8,128)(2,1)S(1)}, u32[]{:S(2)}, u32[]{:S(2)}) collective-permute-start(bf16[128,640]{1,0:T(8,128)(2,1)S(1)} %get-tuple-element.38), channel_id=1, source_target_pairs={{0,1},{1,2},{2,3},{3,0},{4,5},{5,6},{6,7},{7,4},{8,9},{9,10},{10,1... | collective-permute-start | bytes 491528 | tf_op jit(solution)/shard_map/ppermute | solution.py:38
  46.6 6.9 %collective-permute-start.16 = (bf16[128,640]{1,0:T(8,128)(2,1)S(1)}, bf16[128,640]{1,0:T(8,128)(2,1)S(1)}, u32[]{:S(2)}, u32[]{:S(2)}) collective-permute-start(bf16[128,640]{1,0:T(8,128)(2,1)S(1)} %shard_map.61), channel_id=1, source_target_pairs={{0,2},{1,3},{2,0},{3,1},{4,6},{5,7},{6,4},{7,5},{8,10},{9,11},{10,... | collective-permute-start | bytes 491528 | tf_op jit(solution)/shard_map/ppermute | solution.py:38
  53.9 4.1 %collective-permute-start.18 = (bf16[32,640]{1,0:T(8,128)(2,1)S(1)}, bf16[32,640]{1,0:T(8,128)(2,1)S(1)}, u32[]{:S(2)}, u32[]{:S(2)}) collective-permute-start(bf16[32,640]{1,0:T(8,128)(2,1)S(1)} %get-tuple-element.40), channel_id=1, source_target_pairs={{0,12},{1,13},{2,14},{3,15},{4,0},{5,1},{6,2},{7,3},{8,4},{9,5},{1... | collective-permute-start | bytes 122888 | tf_op jit(solution)/shard_map/ppermute | solution.py:38
  56.2 5.6 %collective-permute-start.19 = (bf16[32,640]{1,0:T(8,128)(2,1)S(1)}, bf16[32,640]{1,0:T(8,128)(2,1)S(1)}, u32[]{:S(2)}, u32[]{:S(2)}) collective-permute-start(bf16[32,640]{1,0:T(8,128)(2,1)S(1)} %get-tuple-element.41), channel_id=1, source_target_pairs={{0,8},{1,9},{2,10},{3,11},{4,12},{5,13},{6,14},{7,15},{8,0},{9,1},... | collective-permute-start | bytes 122888 | tf_op jit(solution)/shard_map/ppermute | solution.py:38
  56.2 5.7 %collective-permute-start.20 = (bf16[32,640]{1,0:T(8,128)(2,1)S(1)}, bf16[32,640]{1,0:T(8,128)(2,1)S(1)}, u32[]{:S(2)}, u32[]{:S(2)}) collective-permute-start(bf16[32,640]{1,0:T(8,128)(2,1)S(1)} %get-tuple-element.42), channel_id=1, source_target_pairs={{0,4},{1,5},{2,6},{3,7},{4,8},{5,9},{6,10},{7,11},{8,12},{9,13},{1... | collective-permute-start | bytes 122888 | tf_op jit(solution)/shard_map/ppermute | solution.py:38

commit v6 on v5

--- a/solution.py
+++ b/solution.py
@@ -254,7 +254,7 @@
         finish(jnp.full(tops.shape, MASKED, F32))
 
 
-def attend(length, parts, cache, turned=None, block=1024):
+def attend(length, parts, cache, turned=None, block=2048):
     group = parts[0].shape[0]
     rows, span = group * len(parts), cache.shape[1]
     first = turned is None
@@ -321,10 +321,24 @@
     )(mine, other)
 
 
-def finish_kernel(a, b, c, d, w0, w1, w2, w3, out, context, weight):
+def arrange_kernel(w0, w1, w2, w3, out):
     for owner, block in zip(y_owners(), (w0, w1, w2, w3)):
         for core in range(CORES):
-            weight[:, pl.ds(pl.multiple_of((owner * CORES + core) * 64, 64), 64), :] = block[core]
+            out[:, pl.ds(pl.multiple_of((owner * CORES + core) * 64, 64), 64), :] = block[core]
+
+
+def arrange(blocks):
+    _, heads, _, vhead = blocks[0].shape
+    return pl.pallas_call(
+        arrange_kernel,
+        out_shape=jax.ShapeDtypeStruct((heads, LATENT, vhead), BF16),
+        in_specs=[VMEM] * 4,
+        out_specs=VMEM,
+        compiler_params=SMALL,
+    )(*blocks)
+
+
+def finish_kernel(a, b, c, d, weight, out, context):
     for j, column in enumerate(merge([a, b, c, d])[0]):
         context[:, j * 128 : (j + 1) * 128] = column.astype(BF16)
     frames, heads, _ = out.shape
@@ -334,19 +348,16 @@
         ).astype(BF16)
 
 
-def finish(parts, weights, frames):
-    _, heads, _, vhead = weights[0].shape
+def finish(parts, weight, frames):
+    heads, _, vhead = weight.shape
     return pl.pallas_call(
         finish_kernel,
         out_shape=jax.ShapeDtypeStruct((frames, heads, vhead), BF16),
-        in_specs=[VMEM] * 8,
+        in_specs=[VMEM] * 5,
         out_specs=VMEM,
-        scratch_shapes=[
-            pltpu.VMEM((frames * heads, LATENT), BF16),
-            pltpu.VMEM((heads, LATENT, vhead), BF16),
-        ],
-        compiler_params=SMALL,
-    )(*parts, *weights)
+        scratch_shapes=[pltpu.VMEM((frames * heads, LATENT), BF16)],
+        compiler_params=SMALL,
+    )(*parts, weight)
 
 
 def on_device(queries, latent_cache, lengths, key_weight, value_weight):
@@ -367,15 +378,15 @@
     groups = [near] + [second_shift(near, hops) for hops in (1, 2, 3)]
     value_pairs = [value_pair] + [y_shift(value_pair, hops) for hops in (1, 2, 3)]
 
-    (one, three), turned = attend(lengths, [groups[1], groups[3]], cache)
+    (one, two), turned = attend(lengths, [groups[1], groups[2]], cache)
     groups, value_pairs = lax.optimization_barrier((groups, value_pairs))
-    (two,), _ = attend(lengths, groups[2:3], cache, turned)
+    (three,), _ = attend(lengths, groups[3:4], cache, turned)
     (zero,), _ = attend(lengths, groups[:1], cache, turned)
     parts = [zero] + [second_shift(part, -hops) for hops, part in ((1, one), (2, two), (3, three))]
 
     near = merge_groups(parts)
     last = [near[0]] + [first_shift(near[hops], -hops) for hops in (1, 2, 3)]
-    return finish(last, value_pairs, frames)[None]
+    return finish(last, arrange(value_pairs), frames)[None]
 
 
 def solution(mesh):

time: 63 us -> 63 us (level)
  no operation moved by 1% of the time
where the time goes in v6:
time: 63 us; the launch traced here: 62.7 us
  starting transfers between devices  25.4 us (40%)
  Pallas kernels  20 us (32%)
  waiting for transfers between devices  16.6 us (26%)
  between operations  0.78 us (1%)
    ppermute x21, starting transfers between devices, exchange(): return lax.ppermute(value, ('roll', 'seq'), pairs)  25.4 us
    ppermute x21, waiting for transfers between devices, exchange(): return lax.ppermute(value, ('roll', 'seq'), pairs)  16.6 us
    pallas_call x3, Pallas kernels, attend(): pl.pallas_call(functools.partial(attend_kernel, block=block, first=first)...  14.2 us
    pallas_call x1, Pallas kernels, load(): pl.pallas_call(load_kernel, out_shape=[jax.ShapeDtypeStruct(a.shape, a.dt...  3.72 us
  transfers between devices with their start and end apart: 21, of which 10 were waited for; matrix products, arithmetic and copies ran while one was open for 0% of the time, Pallas kernels for 30%

profile of v6, /device:TPU:0, one launch (start us, length us, event | category | flops | bytes accessed | tf_op | source)
XLA Modules:
  0.0 62.7 jit_solution(13251690771045174770)
XLA Ops:
  0.0 3.1 %collective-permute-start.3 = (bf16[8,64,128]{2,1,0:T(8,128)(2,1)}, bf16[8,64,128]{2,1,0:T(8,128)(2,1)S(1)}, u32[]{:S(2)}, u32[]{:S(2)}) collective-permute-start(bf16[8,64,128]{2,1,0:T(8,128)(2,1)} %bitcast.7), channel_id=1, source_target_pairs={{0,96},{1,97},{2,98},{3,99},{4,100},{5,101},{6,102},{7,103},{8,104... | collective-permute-start | bytes 393224 | tf_op jit(solution)/shard_map/ppermute | solution.py:38
  3.1 0.6 %collective-permute-start.2 = (bf16[8,64,128]{2,1,0:T(8,128)(2,1)}, bf16[8,64,128]{2,1,0:T(8,128)(2,1)S(1)}, u32[]{:S(2)}, u32[]{:S(2)}) collective-permute-start(bf16[8,64,128]{2,1,0:T(8,128)(2,1)} %bitcast.8), channel_id=1, source_target_pairs={{0,64},{1,65},{2,66},{3,67},{4,68},{5,69},{6,70},{7,71},{8,72},{9,... | collective-permute-start | bytes 393224 | tf_op jit(solution)/shard_map/ppermute | solution.py:38
  3.7 1.0 %collective-permute-start.1 = (bf16[8,64,128]{2,1,0:T(8,128)(2,1)}, bf16[8,64,128]{2,1,0:T(8,128)(2,1)S(1)}, u32[]{:S(2)}, u32[]{:S(2)}) collective-permute-start(bf16[8,64,128]{2,1,0:T(8,128)(2,1)} %bitcast.9), channel_id=1, source_target_pairs={{0,32},{1,33},{2,34},{3,35},{4,36},{5,37},{6,38},{7,39},{8,40},{9,... | collective-permute-start | bytes 393224 | tf_op jit(solution)/shard_map/ppermute | solution.py:38
  4.7 0.0 collective-permute-start.5
  4.7 0.5 collective-permute-start
  5.2 3.7 %shard_map.55 = (bf16[576,8192]{1,0:T(8,128)(2,1)S(1)}, bf16[8,64,128]{2,1,0:T(8,128)(2,1)S(1)}, bf16[4,8,192]{2,1,0:T(8,128)(2,1)S(1)}, bf16[8,64,128]{2,1,0:T(8,128)(2,1)S(1)}) custom-call(bf16[576,8192]{1,0:T(8,128)(2,1)} %bitcast.6, bf16[8,64,128]{2,1,0:T(8,128)(2,1)} %bitcast.10, bf16[4,8,192]{2,1,0:T(8,128)(2,1)} %bitcast.12, bf16[8,64,128]{2,1,0:T(8,128)(2,1)} %refs_3_.1), custom_call_target="tpu_custom_call" | custom-call | bytes 19423232 | tf_op jit(solution)/shard_map/pallas_call | solution.py:107
  8.9 0.0 collective-permute-done.other
  8.9 0.0 collective-permute-done.3.kw3
  9.0 2.2 %collective-permute-done.2.kw2 = bf16[8,64,128]{2,1,0:T(8,128)(2,1)S(1)} collective-permute-done((bf16[8,64,128]{2,1,0:T(8,128)(2,1)}, bf16[8,64,128]{2,1,0:T(8,128)(2,1)S(1)}, u32[]{:S(2)}, u32[]{:S(2)}) %collective-permute-start.2) | collective-permute-done | bytes 131104 | tf_op jit(solution)/shard_map/ppermute | solution.py:38
  11.2 1.4 %collective-permute-done.1.kw1 = bf16[8,64,128]{2,1,0:T(8,128)(2,1)S(1)} collective-permute-done((bf16[8,64,128]{2,1,0:T(8,128)(2,1)}, bf16[8,64,128]{2,1,0:T(8,128)(2,1)S(1)}, u32[]{:S(2)}, u32[]{:S(2)}) %collective-permute-start.1) | collective-permute-done | bytes 131104 | tf_op jit(solution)/shard_map/ppermute | solution.py:38
  12.6 0.5 shard_map.56
  13.1 0.0 collective-permute-start.4
  13.2 0.0 collective-permute-done.5.other
  13.2 1.2 %collective-permute-done.4 = bf16[32,576]{1,0:T(8,128)(2,1)S(1)} collective-permute-done((bf16[32,576]{1,0:T(8,128)(2,1)S(1)}, bf16[32,576]{1,0:T(8,128)(2,1)S(1)}, u32[]{:S(2)}, u32[]{:S(2)}) %collective-permute-start.4) | collective-permute-done | bytes 36896 | tf_op jit(solution)/shard_map/ppermute | solution.py:38
  14.4 4.1 %collective-permute-start.8 = (bf16[32,576]{1,0:T(8,128)(2,1)S(1)}, bf16[32,576]{1,0:T(8,128)(2,1)S(1)}, u32[]{:S(2)}, u32[]{:S(2)}) collective-permute-start(bf16[32,576]{1,0:T(8,128)(2,1)S(1)} %add.3.refs_0_), channel_id=1, source_target_pairs={{0,12},{1,13},{2,14},{3,15},{4,0},{5,1},{6,2},{7,3},{8,4},{9,5},{1... | collective-permute-start | bytes 110600 | tf_op jit(solution)/shard_map/ppermute | solution.py:38
  18.5 0.0 collective-permute-start.7
  18.5 1.3 %collective-permute-start.6 = (bf16[32,576]{1,0:T(8,128)(2,1)S(1)}, bf16[32,576]{1,0:T(8,128)(2,1)S(1)}, u32[]{:S(2)}, u32[]{:S(2)}) collective-permute-start(bf16[32,576]{1,0:T(8,128)(2,1)S(1)} %add.3.refs_0_), channel_id=1, source_target_pairs={{0,4},{1,5},{2,6},{3,7},{4,8},{5,9},{6,10},{7,11},{8,12},{9,13},{1... | collective-permute-start | bytes 110600 | tf_op jit(solution)/shard_map/ppermute | solution.py:38
  19.8 0.4 collective-permute-done.8.refs_3_
  20.2 3.9 %collective-permute-done.7.refs_2_ = bf16[32,576]{1,0:T(8,128)(2,1)S(1)} collective-permute-done((bf16[32,576]{1,0:T(8,128)(2,1)S(1)}, bf16[32,576]{1,0:T(8,128)(2,1)S(1)}, u32[]{:S(2)}, u32[]{:S(2)}) %collective-permute-start.7) | collective-permute-done | bytes 36896 | tf_op jit(solution)/shard_map/ppermute | solution.py:38
  24.1 0.0 collective-permute-done.6.refs_1_
  24.2 3.1 %collective-permute-start.10 = (bf16[128,576]{1,0:T(8,128)(2,1)S(1)}, bf16[128,576]{1,0:T(8,128)(2,1)S(1)}, u32[]{:S(2)}, u32[]{:S(2)}) collective-permute-start(bf16[128,576]{1,0:T(8,128)(2,1)S(1)} %shard_map.58.refs_1_), channel_id=1, source_target_pairs={{0,2},{1,3},{2,0},{3,1},{4,6},{5,7},{6,4},{7,5},{8,10},{9,11},{10,... | collective-permute-start | bytes 442376 | tf_op jit(solution)/shard_map/ppermute | solution.py:38
  27.3 0.6 collective-permute-start.9
  28.5 0.6 %collective-permute-start.14 = (bf16[2,8,64,128]{3,2,1,0:T(8,128)(2,1)S(1)}, bf16[2,8,64,128]{3,2,1,0:T(8,128)(2,1)S(1)}, u32[]{:S(2)}, u32[]{:S(2)}) collective-permute-start(bf16[2,8,64,128]{3,2,1,0:T(8,128)(2,1)S(1)} %shard_map.57.w0), channel_id=1, source_target_pairs={{0,96},{1,97},{2,98},{3,99},{4,100},{5,101},{6,102},{7,103},{8,104... | collective-permute-start | bytes 786440 | tf_op jit(solution)/shard_map/ppermute | solution.py:38
  29.2 0.6 %collective-permute-start.13 = (bf16[2,8,64,128]{3,2,1,0:T(8,128)(2,1)S(1)}, bf16[2,8,64,128]{3,2,1,0:T(8,128)(2,1)S(1)}, u32[]{:S(2)}, u32[]{:S(2)}) collective-permute-start(bf16[2,8,64,128]{3,2,1,0:T(8,128)(2,1)S(1)} %shard_map.57.w0), channel_id=1, source_target_pairs={{0,64},{1,65},{2,66},{3,67},{4,68},{5,69},{6,70},{7,71},{8,72},{9,... | collective-permute-start | bytes 786440 | tf_op jit(solution)/shard_map/ppermute | solution.py:38
  29.8 0.9 %collective-permute-start.12 = (bf16[2,8,64,128]{3,2,1,0:T(8,128)(2,1)S(1)}, bf16[2,8,64,128]{3,2,1,0:T(8,128)(2,1)S(1)}, u32[]{:S(2)}, u32[]{:S(2)}) collective-permute-start(bf16[2,8,64,128]{3,2,1,0:T(8,128)(2,1)S(1)} %shard_map.57.w0), channel_id=1, source_target_pairs={{0,32},{1,33},{2,34},{3,35},{4,36},{5,37},{6,38},{7,39},{8,40},{9,... | collective-permute-start | bytes 786440 | tf_op jit(solution)/shard_map/ppermute | solution.py:38
  30.6 0.4 collective-permute-done.10.refs_1_
  31.1 2.8 %collective-permute-start.11 = (bf16[128,576]{1,0:T(8,128)(2,1)S(1)}, bf16[128,576]{1,0:T(8,128)(2,1)S(1)}, u32[]{:S(2)}, u32[]{:S(2)}) collective-permute-start(bf16[128,576]{1,0:T(8,128)(2,1)S(1)} %shard_map.58.refs_1_), channel_id=1, source_target_pairs={{0,3},{1,0},{2,1},{3,2},{4,7},{5,4},{6,5},{7,6},{8,11},{9,8},{10,9... | collective-permute-start | bytes 442376 | tf_op jit(solution)/shard_map/ppermute | solution.py:38
  33.8 0.0 collective-permute-done.9.refs_0_
  33.8 7.3 %shard_map.59 = (bf16[128,640]{1,0:T(8,128)(2,1)S(1)}, bf16[128,640]{1,0:T(8,128)(2,1)S(1)}, bf16[8192,512]{1,0:T(8,128)(2,1)S(1)}) custom-call(s32[1]{0:T(128)S(6)} %copy.6.length, bf16[576,8192]{1,0:T(8,128)(2,1)S(1)} %get-tuple-element.26.cache, bf16[128,576]{1,0:T(8,128)(2,1)S(1)} %collective-permute-done.9.refs_0_, ...), custom_call_target="tpu_custom_call" | custom-call | flops 4563402752 | bytes 9437184 | tf_op jit(solution)/shard_map/pallas_call | solution.py:265
  41.2 1.0 %collective-permute-start.15 = (bf16[128,640]{1,0:T(8,128)(2,1)S(1)}, bf16[128,640]{1,0:T(8,128)(2,1)S(1)}, u32[]{:S(2)}, u32[]{:S(2)}) collective-permute-start(bf16[128,640]{1,0:T(8,128)(2,1)S(1)} %get-tuple-element.36), channel_id=1, source_target_pairs={{0,3},{1,0},{2,1},{3,2},{4,7},{5,4},{6,5},{7,6},{8,11},{9,8},{10,9... | collective-permute-start | bytes 491528 | tf_op jit(solution)/shard_map/ppermute | solution.py:38
  42.2 0.0 collective-permute-done.11.refs_1_
  42.2 1.7 %collective-permute-start.16 = (bf16[128,640]{1,0:T(8,128)(2,1)S(1)}, bf16[128,640]{1,0:T(8,128)(2,1)S(1)}, u32[]{:S(2)}, u32[]{:S(2)}) collective-permute-start(bf16[128,640]{1,0:T(8,128)(2,1)S(1)} %get-tuple-element.37), channel_id=1, source_target_pairs={{0,2},{1,3},{2,0},{3,1},{4,6},{5,7},{6,4},{7,5},{8,10},{9,11},{10,... | collective-permute-start | bytes 491528 | tf_op jit(solution)/shard_map/ppermute | solution.py:38
  43.9 0.0 collective-permute-done.14.w3
  43.9 0.0 collective-permute-done.13.w2
  43.9 0.0 collective-permute-done.12.w1
  43.9 3.6 %shard_map.61 = bf16[128,640]{1,0:T(8,128)(2,1)S(1)} custom-call(s32[1]{0:T(128)S(6)} %copy.6.length, bf16[576,8192]{1,0:T(8,128)(2,1)S(1)} %get-tuple-element.26.cache, bf16[8192,512]{1,0:T(8,128)(2,1)S(1)} %get-tuple-element.33.refs_0_, bf16[128,576]{1,0:T(8,128)(2,1)S(1)} %collective-permute-done.11.refs_1_), custom_call_target="tpu_custom_call" | custom-call | flops 2281701376 | bytes 9437184 | tf_op jit(solution)/shard_map/pallas_call | solution.py:265
  47.5 0.1 collective-permute-start.17
  47.6 3.3 %shard_map.60.refs_0_ = bf16[128,640]{1,0:T(8,128)(2,1)S(1)} custom-call(s32[1]{0:T(128)S(6)} %copy.6.length, bf16[576,8192]{1,0:T(8,128)(2,1)S(1)} %get-tuple-element.26.cache, bf16[8192,512]{1,0:T(8,128)(2,1)S(1)} %get-tuple-element.33.refs_0_, bf16[128,576]{1,0:T(8,128)(2,1)S(1)} %shard_map.58.refs_1_), custom_call_target="tpu_custom_call" | custom-call | flops 2281701376 | bytes 9437184 | tf_op jit(solution)/shard_map/pallas_call | solution.py:265
  50.9 0.0 collective-permute-done.15.refs_1_
  50.9 0.0 collective-permute-done.16.refs_2_
  50.9 3.2 %collective-permute-done.17.refs_3_ = bf16[128,640]{1,0:T(8,128)(2,1)S(1)} collective-permute-done((bf16[128,640]{1,0:T(8,128)(2,1)S(1)}, bf16[128,640]{1,0:T(8,128)(2,1)S(1)}, u32[]{:S(2)}, u32[]{:S(2)}) %collective-permute-start.17) | collective-permute-done | bytes 163872 | tf_op jit(solution)/shard_map/ppermute | solution.py:38
  54.1 0.3 shard_map.62
  54.5 1.0 %collective-permute-start.18 = (bf16[32,640]{1,0:T(8,128)(2,1)S(1)}, bf16[32,640]{1,0:T(8,128)(2,1)S(1)}, u32[]{:S(2)}, u32[]{:S(2)}) collective-permute-start(bf16[32,640]{1,0:T(8,128)(2,1)S(1)} %get-tuple-element.40), channel_id=1, source_target_pairs={{0,12},{1,13},{2,14},{3,15},{4,0},{5,1},{6,2},{7,3},{8,4},{9,5},{1... | collective-permute-start | bytes 122888 | tf_op jit(solution)/shard_map/ppermute | solution.py:38
  55.5 1.0 %collective-permute-start.19 = (bf16[32,640]{1,0:T(8,128)(2,1)S(1)}, bf16[32,640]{1,0:T(8,128)(2,1)S(1)}, u32[]{:S(2)}, u32[]{:S(2)}) collective-permute-start(bf16[32,640]{1,0:T(8,128)(2,1)S(1)} %get-tuple-element.41), channel_id=1, source_target_pairs={{0,8},{1,9},{2,10},{3,11},{4,12},{5,13},{6,14},{7,15},{8,0},{9,1},... | collective-permute-start | bytes 122888 | tf_op jit(solution)/shard_map/ppermute | solution.py:38
  56.5 1.3 %collective-permute-start.20 = (bf16[32,640]{1,0:T(8,128)(2,1)S(1)}, bf16[32,640]{1,0:T(8,128)(2,1)S(1)}, u32[]{:S(2)}, u32[]{:S(2)}) collective-permute-start(bf16[32,640]{1,0:T(8,128)(2,1)S(1)} %get-tuple-element.42), channel_id=1, source_target_pairs={{0,4},{1,5},{2,6},{3,7},{4,8},{5,9},{6,10},{7,11},{8,12},{9,13},{1... | collective-permute-start | bytes 122888 | tf_op jit(solution)/shard_map/ppermute | solution.py:38
  57.8 0.1 shard_map.63.weight
  57.9 0.6 collective-permute-done.18.b
  58.5 2.5 %collective-permute-done.19.c = bf16[32,640]{1,0:T(8,128)(2,1)S(1)} collective-permute-done((bf16[32,640]{1,0:T(8,128)(2,1)S(1)}, bf16[32,640]{1,0:T(8,128)(2,1)S(1)}, u32[]{:S(2)}, u32[]{:S(2)}) %collective-permute-start.19) | collective-permute-done | bytes 40992 | tf_op jit(solution)/shard_map/ppermute | solution.py:38
  61.0 0.7 %collective-permute-done.20.d = bf16[32,640]{1,0:T(8,128)(2,1)S(1)} collective-permute-done((bf16[32,640]{1,0:T(8,128)(2,1)S(1)}, bf16[32,640]{1,0:T(8,128)(2,1)S(1)}, u32[]{:S(2)}, u32[]{:S(2)}) %collective-permute-start.20) | collective-permute-done | bytes 40992 | tf_op jit(solution)/shard_map/ppermute | solution.py:38
  61.7 1.0 %shard_map.64 = bf16[4,8,128]{2,1,0:T(8,128)(2,1)} custom-call(bf16[32,640]{1,0:T(8,128)(2,1)S(1)} %get-tuple-element.39.a, bf16[32,640]{1,0:T(8,128)(2,1)S(1)} %collective-permute-done.18.b, bf16[32,640]{1,0:T(8,128)(2,1)S(1)} %collective-permute-done.19.c, bf16[32,640]{1,0:T(8,128)(2,1)S(1)} %collective-permute-done.20.d, ...), custom_call_target="tpu_custom_call" | custom-call | tf_op jit(solution)/shard_map/pallas_call | solution.py:353
  (3 shorter events, 0.1 us)
Async XLA Ops:
  0.0 9.0 %collective-permute-start.3 = (bf16[8,64,128]{2,1,0:T(8,128)(2,1)}, bf16[8,64,128]{2,1,0:T(8,128)(2,1)S(1)}, u32[]{:S(2)}, u32[]{:S(2)}) collective-permute-start(bf16[8,64,128]{2,1,0:T(8,128)(2,1)} %bitcast.7), channel_id=1, source_target_pairs={{0,96},{1,97},{2,98},{3,99},{4,100},{5,101},{6,102},{7,103},{8,104... | collective-permute-start | bytes 393224 | tf_op jit(solution)/shard_map/ppermute | solution.py:38
  3.1 8.1 %collective-permute-start.2 = (bf16[8,64,128]{2,1,0:T(8,128)(2,1)}, bf16[8,64,128]{2,1,0:T(8,128)(2,1)S(1)}, u32[]{:S(2)}, u32[]{:S(2)}) collective-permute-start(bf16[8,64,128]{2,1,0:T(8,128)(2,1)} %bitcast.8), channel_id=1, source_target_pairs={{0,64},{1,65},{2,66},{3,67},{4,68},{5,69},{6,70},{7,71},{8,72},{9,... | collective-permute-start | bytes 393224 | tf_op jit(solution)/shard_map/ppermute | solution.py:38
  3.7 8.9 %collective-permute-start.1 = (bf16[8,64,128]{2,1,0:T(8,128)(2,1)}, bf16[8,64,128]{2,1,0:T(8,128)(2,1)S(1)}, u32[]{:S(2)}, u32[]{:S(2)}) collective-permute-start(bf16[8,64,128]{2,1,0:T(8,128)(2,1)} %bitcast.9), channel_id=1, source_target_pairs={{0,32},{1,33},{2,34},{3,35},{4,36},{5,37},{6,38},{7,39},{8,40},{9,... | collective-permute-start | bytes 393224 | tf_op jit(solution)/shard_map/ppermute | solution.py:38
  4.7 8.5 %collective-permute-start.5 = (bf16[8,64,128]{2,1,0:T(8,128)(2,1)}, bf16[8,64,128]{2,1,0:T(8,128)(2,1)S(1)}, u32[]{:S(2)}, u32[]{:S(2)}) collective-permute-start(bf16[8,64,128]{2,1,0:T(8,128)(2,1)} %refs_3_.1), channel_id=1, source_target_pairs={{0,16},{1,17},{2,18},{3,19},{4,20},{5,21},{6,22},{7,23},{8,24},{9,... | collective-permute-start | bytes 393224 | tf_op jit(solution)/shard_map/ppermute | solution.py:38
  4.7 4.2 %collective-permute-start = (bf16[4,8,192]{2,1,0:T(8,128)(2,1)}, bf16[4,8,192]{2,1,0:T(8,128)(2,1)S(1)}, u32[]{:S(2)}, u32[]{:S(2)}) collective-permute-start(bf16[4,8,192]{2,1,0:T(8,128)(2,1)} %bitcast.11), channel_id=1, source_target_pairs={{0,16},{1,17},{2,18},{3,19},{4,20},{5,21},{6,22},{7,23},{8,24},{9,... | collective-permute-start | bytes 36872 | tf_op jit(solution)/shard_map/ppermute | solution.py:38
  13.1 1.3 %collective-permute-start.4 = (bf16[32,576]{1,0:T(8,128)(2,1)S(1)}, bf16[32,576]{1,0:T(8,128)(2,1)S(1)}, u32[]{:S(2)}, u32[]{:S(2)}) collective-permute-start(bf16[32,576]{1,0:T(8,128)(2,1)S(1)} %get-tuple-element.30), channel_id=1, source_target_pairs={{0,16},{1,17},{2,18},{3,19},{4,20},{5,21},{6,22},{7,23},{8,24},{9,... | collective-permute-start | bytes 110600 | tf_op jit(solution)/shard_map/ppermute | solution.py:38
  14.4 5.8 %collective-permute-start.8 = (bf16[32,576]{1,0:T(8,128)(2,1)S(1)}, bf16[32,576]{1,0:T(8,128)(2,1)S(1)}, u32[]{:S(2)}, u32[]{:S(2)}) collective-permute-start(bf16[32,576]{1,0:T(8,128)(2,1)S(1)} %add.3.refs_0_), channel_id=1, source_target_pairs={{0,12},{1,13},{2,14},{3,15},{4,0},{5,1},{6,2},{7,3},{8,4},{9,5},{1... | collective-permute-start | bytes 110600 | tf_op jit(solution)/shard_map/ppermute | solution.py:38
  18.5 5.6 %collective-permute-start.7 = (bf16[32,576]{1,0:T(8,128)(2,1)S(1)}, bf16[32,576]{1,0:T(8,128)(2,1)S(1)}, u32[]{:S(2)}, u32[]{:S(2)}) collective-permute-start(bf16[32,576]{1,0:T(8,128)(2,1)S(1)} %add.3.refs_0_), channel_id=1, source_target_pairs={{0,8},{1,9},{2,10},{3,11},{4,12},{5,13},{6,14},{7,15},{8,0},{9,1},... | collective-permute-start | bytes 110600 | tf_op jit(solution)/shard_map/ppermute | solution.py:38
  18.5 5.7 %collective-permute-start.6 = (bf16[32,576]{1,0:T(8,128)(2,1)S(1)}, bf16[32,576]{1,0:T(8,128)(2,1)S(1)}, u32[]{:S(2)}, u32[]{:S(2)}) collective-permute-start(bf16[32,576]{1,0:T(8,128)(2,1)S(1)} %add.3.refs_0_), channel_id=1, source_target_pairs={{0,4},{1,5},{2,6},{3,7},{4,8},{5,9},{6,10},{7,11},{8,12},{9,13},{1... | collective-permute-start | bytes 110600 | tf_op jit(solution)/shard_map/ppermute | solution.py:38
  24.2 6.9 %collective-permute-start.10 = (bf16[128,576]{1,0:T(8,128)(2,1)S(1)}, bf16[128,576]{1,0:T(8,128)(2,1)S(1)}, u32[]{:S(2)}, u32[]{:S(2)}) collective-permute-start(bf16[128,576]{1,0:T(8,128)(2,1)S(1)} %shard_map.58.refs_1_), channel_id=1, source_target_pairs={{0,2},{1,3},{2,0},{3,1},{4,6},{5,7},{6,4},{7,5},{8,10},{9,11},{10,... | collective-permute-start | bytes 442376 | tf_op jit(solution)/shard_map/ppermute | solution.py:38
  27.3 6.6 %collective-permute-start.9 = (bf16[128,576]{1,0:T(8,128)(2,1)S(1)}, bf16[128,576]{1,0:T(8,128)(2,1)S(1)}, u32[]{:S(2)}, u32[]{:S(2)}) collective-permute-start(bf16[128,576]{1,0:T(8,128)(2,1)S(1)} %shard_map.58.refs_1_), channel_id=1, source_target_pairs={{0,1},{1,2},{2,3},{3,0},{4,5},{5,6},{6,7},{7,4},{8,9},{9,10},{10,1... | collective-permute-start | bytes 442376 | tf_op jit(solution)/shard_map/ppermute | solution.py:38
  28.5 15.4 %collective-permute-start.14 = (bf16[2,8,64,128]{3,2,1,0:T(8,128)(2,1)S(1)}, bf16[2,8,64,128]{3,2,1,0:T(8,128)(2,1)S(1)}, u32[]{:S(2)}, u32[]{:S(2)}) collective-permute-start(bf16[2,8,64,128]{3,2,1,0:T(8,128)(2,1)S(1)} %shard_map.57.w0), channel_id=1, source_target_pairs={{0,96},{1,97},{2,98},{3,99},{4,100},{5,101},{6,102},{7,103},{8,104... | collective-permute-start | bytes 786440 | tf_op jit(solution)/shard_map/ppermute | solution.py:38
  29.2 14.8 %collective-permute-start.13 = (bf16[2,8,64,128]{3,2,1,0:T(8,128)(2,1)S(1)}, bf16[2,8,64,128]{3,2,1,0:T(8,128)(2,1)S(1)}, u32[]{:S(2)}, u32[]{:S(2)}) collective-permute-start(bf16[2,8,64,128]{3,2,1,0:T(8,128)(2,1)S(1)} %shard_map.57.w0), channel_id=1, source_target_pairs={{0,64},{1,65},{2,66},{3,67},{4,68},{5,69},{6,70},{7,71},{8,72},{9,... | collective-permute-start | bytes 786440 | tf_op jit(solution)/shard_map/ppermute | solution.py:38
  29.8 14.1 %collective-permute-start.12 = (bf16[2,8,64,128]{3,2,1,0:T(8,128)(2,1)S(1)}, bf16[2,8,64,128]{3,2,1,0:T(8,128)(2,1)S(1)}, u32[]{:S(2)}, u32[]{:S(2)}) collective-permute-start(bf16[2,8,64,128]{3,2,1,0:T(8,128)(2,1)S(1)} %shard_map.57.w0), channel_id=1, source_target_pairs={{0,32},{1,33},{2,34},{3,35},{4,36},{5,37},{6,38},{7,39},{8,40},{9,... | collective-permute-start | bytes 786440 | tf_op jit(solution)/shard_map/ppermute | solution.py:38
  31.1 11.1 %collective-permute-start.11 = (bf16[128,576]{1,0:T(8,128)(2,1)S(1)}, bf16[128,576]{1,0:T(8,128)(2,1)S(1)}, u32[]{:S(2)}, u32[]{:S(2)}) collective-permute-start(bf16[128,576]{1,0:T(8,128)(2,1)S(1)} %shard_map.58.refs_1_), channel_id=1, source_target_pairs={{0,3},{1,0},{2,1},{3,2},{4,7},{5,4},{6,5},{7,6},{8,11},{9,8},{10,9... | collective-permute-start | bytes 442376 | tf_op jit(solution)/shard_map/ppermute | solution.py:38
  41.2 9.7 %collective-permute-start.15 = (bf16[128,640]{1,0:T(8,128)(2,1)S(1)}, bf16[128,640]{1,0:T(8,128)(2,1)S(1)}, u32[]{:S(2)}, u32[]{:S(2)}) collective-permute-start(bf16[128,640]{1,0:T(8,128)(2,1)S(1)} %get-tuple-element.36), channel_id=1, source_target_pairs={{0,3},{1,0},{2,1},{3,2},{4,7},{5,4},{6,5},{7,6},{8,11},{9,8},{10,9... | collective-permute-start | bytes 491528 | tf_op jit(solution)/shard_map/ppermute | solution.py:38
  42.2 8.7 %collective-permute-start.16 = (bf16[128,640]{1,0:T(8,128)(2,1)S(1)}, bf16[128,640]{1,0:T(8,128)(2,1)S(1)}, u32[]{:S(2)}, u32[]{:S(2)}) collective-permute-start(bf16[128,640]{1,0:T(8,128)(2,1)S(1)} %get-tuple-element.37), channel_id=1, source_target_pairs={{0,2},{1,3},{2,0},{3,1},{4,6},{5,7},{6,4},{7,5},{8,10},{9,11},{10,... | collective-permute-start | bytes 491528 | tf_op jit(solution)/shard_map/ppermute | solution.py:38
  47.5 6.6 %collective-permute-start.17 = (bf16[128,640]{1,0:T(8,128)(2,1)S(1)}, bf16[128,640]{1,0:T(8,128)(2,1)S(1)}, u32[]{:S(2)}, u32[]{:S(2)}) collective-permute-start(bf16[128,640]{1,0:T(8,128)(2,1)S(1)} %shard_map.61), channel_id=1, source_target_pairs={{0,1},{1,2},{2,3},{3,0},{4,5},{5,6},{6,7},{7,4},{8,9},{9,10},{10,1... | collective-permute-start | bytes 491528 | tf_op jit(solution)/shard_map/ppermute | solution.py:38
  54.5 4.1 %collective-permute-start.18 = (bf16[32,640]{1,0:T(8,128)(2,1)S(1)}, bf16[32,640]{1,0:T(8,128)(2,1)S(1)}, u32[]{:S(2)}, u32[]{:S(2)}) collective-permute-start(bf16[32,640]{1,0:T(8,128)(2,1)S(1)} %get-tuple-element.40), channel_id=1, source_target_pairs={{0,12},{1,13},{2,14},{3,15},{4,0},{5,1},{6,2},{7,3},{8,4},{9,5},{1... | collective-permute-start | bytes 122888 | tf_op jit(solution)/shard_map/ppermute | solution.py:38
  55.5 5.5 %collective-permute-start.19 = (bf16[32,640]{1,0:T(8,128)(2,1)S(1)}, bf16[32,640]{1,0:T(8,128)(2,1)S(1)}, u32[]{:S(2)}, u32[]{:S(2)}) collective-permute-start(bf16[32,640]{1,0:T(8,128)(2,1)S(1)} %get-tuple-element.41), channel_id=1, source_target_pairs={{0,8},{1,9},{2,10},{3,11},{4,12},{5,13},{6,14},{7,15},{8,0},{9,1},... | collective-permute-start | bytes 122888 | tf_op jit(solution)/shard_map/ppermute | solution.py:38
  56.5 5.2 %collective-permute-start.20 = (bf16[32,640]{1,0:T(8,128)(2,1)S(1)}, bf16[32,640]{1,0:T(8,128)(2,1)S(1)}, u32[]{:S(2)}, u32[]{:S(2)}) collective-permute-start(bf16[32,640]{1,0:T(8,128)(2,1)S(1)} %get-tuple-element.42), channel_id=1, source_target_pairs={{0,4},{1,5},{2,6},{3,7},{4,8},{5,9},{6,10},{7,11},{8,12},{9,13},{1... | collective-permute-start | bytes 122888 | tf_op jit(solution)/shard_map/ppermute | solution.py:38
